TPU v7x, 512 devices: a whole 4x8x8 slice. The times are simulated.
512 devices in a mesh: tm: 128 (over y, z, core), row: 2 (over x_hi), col: 2 (over x_lo).
Axes of the slice: x: 4 (x_hi: 2, x_lo: 2; x = x_hi * 2 + x_lo), y: 8, z: 8, core: 2. Of those that a mesh axis runs over, the one named last changes fastest.
Arguments:
- observed: float32 [8192, 16, 256], P('tm', 'row', 'col'), may hold values from -6 to 6
- kernel: float32 [33, 16, 256], P(None, 'row', 'col'), may hold values from 0.05 to 1
Outputs:
- restored: float32 [8192, 16, 256], P('tm', 'row', 'col')
All inputs are finite; a program needn't handle non-finite values.
Results may differ from a plain program's by a relative error of at most 0.00002.
Values sent between devices are 32-bit elements; how exact they have to be, the bound alone decides.
No kernel may reach another device: no remote copies, remote signals or barrier semaphores. Data moves between devices by JAX's collectives and lax.ppermute only.
A program may use at most 128 MiB of HBM per device.

v0:
```python
import jax
import jax.numpy as jnp
from jax import lax
from jax.sharding import PartitionSpec as P

PASSES = 2


primal_step = 1.0
dual_step = 0.5
tv_weight = 0.1
inner_step = 1.0 / 12.0


def extended_2(cells, sides, width):
    for axis, dim in sides:
        count = lax.axis_size(axis)
        ends = count - 1
        head = lax.slice_in_dim(cells, 0, width, axis=dim)
        tail = lax.slice_in_dim(cells, cells.shape[dim] - width, cells.shape[dim], axis=dim)
        cells = jnp.concatenate(
            [
                lax.ppermute(tail, axis, [(i, (i + 1) % count) for i in range(ends)]),
                cells,
                lax.ppermute(head, axis, [((i + 1) % count, i) for i in range(ends)]),
            ],
            axis=dim,
        )
    return cells


def apply_taps(padded, kern, count, forward):
    taps = kern.shape[0]
    reach = taps - 1
    result = jnp.zeros((count,) + padded.shape[1:], jnp.float32)
    for tap in range(taps):
        begin = tap if forward else reach - tap
        result = result + kern[tap] * padded[begin : begin + count]
    return result


def margin(tv_dual, moved):
    stacked = jnp.concatenate([tv_dual, moved[None]], axis=0)
    return extended_2(stacked, (("tm", 1), ("row", 2), ("col", 3)), 1)


def wide_divergence(padded):
    part_t = padded[0, 1:, 1:, 1:] - padded[0, :-1, 1:, 1:]
    part_r = padded[1, 1:, 1:, 1:] - padded[1, 1:, :-1, 1:]
    part_c = padded[2, 1:, 1:, 1:] - padded[2, 1:, 1:, :-1]
    return part_t + part_r + part_c


def body(observed, kernel):
    kern = kernel / jnp.sum(kernel, axis=0)
    frames, rows, cols = observed.shape
    half = (kernel.shape[0] - 1) // 2
    theta = primal_step * tv_weight
    shape = (frames, rows, cols)
    tv_dual = jnp.zeros((3,) + shape, jnp.float32)
    last_t = (lax.axis_index("tm") == lax.axis_size("tm") - 1) & (
        lax.broadcasted_iota(jnp.int32, shape, 0) == frames - 1
    )
    last_r = (lax.axis_index("row") == lax.axis_size("row") - 1) & (
        lax.broadcasted_iota(jnp.int32, shape, 1) == rows - 1
    )
    last_c = (lax.axis_index("col") == lax.axis_size("col") - 1) & (
        lax.broadcasted_iota(jnp.int32, shape, 2) == cols - 1
    )
    extended = extended_2(observed, (("tm", 0),), half)
    blurred = apply_taps(extended, kern, frames, True)
    data_dual = dual_step * (blurred - observed) / (1.0 + dual_step)
    dual_edges = extended_2(data_dual, (("tm", 0),), half)
    back = apply_taps(dual_edges, kern, frames, False)
    moved = observed - primal_step * back
    for inner in range(PASSES):
        padded = margin(tv_dual, moved)
        target = wide_divergence(padded) - padded[3, 1:, 1:, 1:] / theta
        base = target[:frames, :rows, :cols]
        grad_t = jnp.where(last_t, 0.0, target[1:, :rows, :cols] - base)
        grad_r = jnp.where(last_r, 0.0, target[:frames, 1:, :cols] - base)
        grad_c = jnp.where(last_c, 0.0, target[:frames, :rows, 1:] - base)
        trial = tv_dual + inner_step * jnp.stack([grad_t, grad_r, grad_c], axis=0)
        length = jnp.sqrt(trial[0] * trial[0] + trial[1] * trial[1] + trial[2] * trial[2])
        tv_dual = trial / jnp.maximum(1.0, length)
    padded = margin(tv_dual, moved)
    updated = moved - theta * wide_divergence(padded)[:frames, :rows, :cols]
    return updated


def solution(mesh):
    in_specs = (P("tm", "row", "col"), P(None, "row", "col"))
    out_specs = P("tm", "row", "col")
    return jax.shard_map(body, mesh=mesh, in_specs=in_specs, out_specs=out_specs, check_vma=False)
```

profile of v0, /device:TPU:32, one launch (start us, length us, event | category | flops | bytes accessed | tf_op | source)
XLA Modules:
  0.0 170.7 jit_solution(4349414000937241608)
XLA Ops:
  0.9 1.9 %collective-permute-start = (f32[16,8,128]{2,1,0:T(8,128)S(1)}, f32[16,8,128]{2,1,0:T(8,128)S(1)}, u32[]{:S(2)}, u32[]{:S(2)}) collective-permute-start(f32[16,8,128]{2,1,0:T(8,128)S(1)} %get-tuple-element.41), channel_id=1, source_target_pairs={{0,4},{4,8},{8,12},{12,16},{16,20},{20,24},{24,28},{28,32},{32,36}... | collective-permute-start | bytes 196616 | tf_op jit(solution)/shard_map/ppermute | solution.py:23
  2.9 10.3 %collective-permute-start.1 = (f32[16,8,128]{2,1,0:T(8,128)S(1)}, f32[16,8,128]{2,1,0:T(8,128)S(1)}, u32[]{:S(2)}, u32[]{:S(2)}) collective-permute-start(f32[16,8,128]{2,1,0:T(8,128)S(1)} %get-tuple-element.42), channel_id=1, source_target_pairs={{4,0},{8,4},{12,8},{16,12},{20,16},{24,20},{28,24},{32,28},{36,32}... | collective-permute-start | bytes 196616 | tf_op jit(solution)/shard_map/ppermute | solution.py:25
  16.8 6.0 %collective-permute-start.2 = (f32[16,8,128]{2,1,0:T(8,128)S(1)}, f32[16,8,128]{2,1,0:T(8,128)S(1)}, u32[]{:S(2)}, u32[]{:S(2)}) collective-permute-start(f32[16,8,128]{2,1,0:T(8,128)S(1)} %get-tuple-element.37), channel_id=1, source_target_pairs={{4,0},{8,4},{12,8},{16,12},{20,16},{24,20},{28,24},{32,28},{36,32}... | collective-permute-start | bytes 196616 | tf_op jit(solution)/shard_map/ppermute | solution.py:25
  22.7 1.9 %collective-permute-start.3 = (f32[16,8,128]{2,1,0:T(8,128)S(1)}, f32[16,8,128]{2,1,0:T(8,128)S(1)}, u32[]{:S(2)}, u32[]{:S(2)}) collective-permute-start(f32[16,8,128]{2,1,0:T(8,128)S(1)} %get-tuple-element.38), channel_id=1, source_target_pairs={{0,4},{4,8},{8,12},{12,16},{16,20},{20,24},{24,28},{28,32},{32,36}... | collective-permute-start | bytes 196616 | tf_op jit(solution)/shard_map/ppermute | solution.py:23
  24.7 6.9 %collective-permute-done.3 = f32[16,8,128]{2,1,0:T(8,128)S(1)} collective-permute-done((f32[16,8,128]{2,1,0:T(8,128)S(1)}, f32[16,8,128]{2,1,0:T(8,128)S(1)}, u32[]{:S(2)}, u32[]{:S(2)}) %collective-permute-start.3) | collective-permute-done | bytes 65568 | tf_op jit(solution)/shard_map/ppermute | solution.py:23
  32.3 1.9 %collective-permute-start.4 = (f32[4,1,8,128]{3,2,1,0:T(8,128)S(1)}, f32[4,1,8,128]{3,2,1,0:T(8,128)S(1)}, u32[]{:S(2)}, u32[]{:S(2)}) collective-permute-start(f32[4,1,8,128]{3,2,1,0:T(8,128)S(1)} %get-tuple-element.35), channel_id=1, source_target_pairs={{0,4},{4,8},{8,12},{12,16},{16,20},{20,24},{24,28},{28,32},{32,36}... | collective-permute-start | bytes 49160 | tf_op jit(solution)/shard_map/ppermute | solution.py:23
  34.2 7.0 %collective-permute-start.5 = (f32[4,1,8,128]{3,2,1,0:T(8,128)S(1)}, f32[4,1,8,128]{3,2,1,0:T(8,128)S(1)}, u32[]{:S(2)}, u32[]{:S(2)}) collective-permute-start(f32[4,1,8,128]{3,2,1,0:T(8,128)S(1)} %get-tuple-element.36), channel_id=1, source_target_pairs={{4,0},{8,4},{12,8},{16,12},{20,16},{24,20},{28,24},{32,28},{36,32}... | collective-permute-start | bytes 49160 | tf_op jit(solution)/shard_map/ppermute | solution.py:25
  42.8 4.9 %collective-permute-start.6 = (f32[4,66,1,128]{3,2,1,0:T(1,128)S(1)}, f32[4,66,1,128]{3,2,1,0:T(1,128)S(1)}, u32[]{:S(2)}, u32[]{:S(2)}) collective-permute-start(f32[4,66,1,128]{3,2,1,0:T(1,128)S(1)} %get-tuple-element.21), channel_id=1, source_target_pairs={{0,2},{1,3},{4,6},{5,7},{8,10},{9,11},{12,14},{13,15},{16,18},{17,... | collective-permute-start | bytes 405512 | tf_op jit(solution)/shard_map/ppermute | solution.py:23
  47.7 1.3 collective-permute-start.7
  50.3 5.9 %collective-permute-done.7 = f32[4,66,1,128]{3,2,1,0:T(1,128)S(1)} collective-permute-done((f32[4,66,1,128]{3,2,1,0:T(1,128)S(1)}, f32[4,66,1,128]{3,2,1,0:T(1,128)S(1)}, u32[]{:S(2)}, u32[]{:S(2)}) %collective-permute-start.7) | collective-permute-done | bytes 135200 | tf_op jit(solution)/shard_map/ppermute | solution.py:25
  57.2 2.1 %fusion.203 = (f32[4,66,10,1]{3,2,1,0:T(8,128)S(1)}, f32[4,66,10,1]{3,2,1,0:T(8,128)}) fusion(f32[4,66,10,128]{3,2,1,0:T(8,128)S(1)} %pad_maximum_fusion.5), kind=kLoop, calls=%fused_computation.389 | loop fusion | bytes 42240 | tf_op jit(solution)/shard_map/slice | solution.py:20
  59.3 2.3 %copy.27 = f32[4,66,10,1]{1,0,3,2:T(4,128)S(1)} copy(f32[4,66,10,1]{3,2,1,0:T(8,128)} %get-tuple-element.16) | data formatting | bytes 21120 | tf_op jit(solution)/shard_map/slice | solution.py:19
  61.6 1.3 collective-permute-start.8
  63.4 1.4 copy.29
  64.9 5.1 %collective-permute-start.9 = (f32[4,66,10,1]{1,0,3,2:T(4,128)}, f32[4,66,10,1]{1,0,3,2:T(4,128)}, u32[]{:S(2)}, u32[]{:S(2)}) collective-permute-start(f32[4,66,10,1]{1,0,3,2:T(4,128)} %copy.29), channel_id=1, source_target_pairs={{0,1},{2,3},{4,5},{6,7},{8,9},{10,11},{12,13},{14,15},{16,17},{18,... | collective-permute-start | bytes 31688 | tf_op jit(solution)/shard_map/ppermute | solution.py:23
  71.1 3.3 %pad_maximum_fusion.2 = f32[4,66,10,129]{3,2,1,0:T(8,128)} fusion(f32[4,66,10,1]{3,2,1,0:T(8,128)S(1)} %copy.28, f32[4,66,1,128]{3,2,1,0:T(1,128)} %copy-done.8, f32[4,1,8,128]{3,2,1,0:T(8,128)S(1)} %collective-permute-done.5, f32[4,64,8,128]{3,2,1,0:T(8,128)S(1)} %get-tuple-element.34, f32[4,1,8,128]{3,2,1,0:T(8,128)S(1)} %collective-permute-done.4, ...), kind=kLoop, calls=%fused_computation.12 | loop fusion | flops 1702800 | bytes 2724480 | tf_op jit(solution)/shard_map/concatenate | solution.py:21
  74.4 1.7 %copy.30 = f32[4,66,10,1]{3,2,1,0:T(8,128)S(1)} copy(f32[4,66,10,1]{1,0,3,2:T(4,128)} %collective-permute-done.9) | data formatting | bytes 21120 | tf_op jit(solution)/shard_map/ppermute | solution.py:23
  76.2 3.8 %fusion.42 = f32[65,9,129]{2,1,0:T(8,128)S(1)} fusion(f32[4,66,10,129]{3,2,1,0:T(8,128)} %pad_maximum_fusion.2, f32[4,66,10,1]{3,2,1,0:T(8,128)S(1)} %copy.30, f32[4,66,1,128]{3,2,1,0:T(1,128)} %copy-done.8, f32[4,66,1,128]{3,2,1,0:T(1,128)} %copy-done.7, f32[4,1,8,128]{3,2,1,0:T(8,128)S(1)} %collective-permute-done.5, ...), kind=kLoop, calls=%fused_computation.88 | loop fusion | flops 905580 | bytes 3475260 | tf_op jit(solution)/shard_map/sub | solution.py:78
  81.7 1.9 %collective-permute-start.10 = (f32[4,1,8,128]{3,2,1,0:T(8,128)S(1)}, f32[4,1,8,128]{3,2,1,0:T(8,128)S(1)}, u32[]{:S(2)}, u32[]{:S(2)}) collective-permute-start(f32[4,1,8,128]{3,2,1,0:T(8,128)S(1)} %get-tuple-element.5), channel_id=1, source_target_pairs={{0,4},{4,8},{8,12},{12,16},{16,20},{20,24},{24,28},{28,32},{32,36}... | collective-permute-start | bytes 49160 | tf_op jit(solution)/shard_map/ppermute | solution.py:23
  83.6 7.0 %collective-permute-start.11 = (f32[4,1,8,128]{3,2,1,0:T(8,128)S(1)}, f32[4,1,8,128]{3,2,1,0:T(8,128)S(1)}, u32[]{:S(2)}, u32[]{:S(2)}) collective-permute-start(f32[4,1,8,128]{3,2,1,0:T(8,128)S(1)} %get-tuple-element.31), channel_id=1, source_target_pairs={{4,0},{8,4},{12,8},{16,12},{20,16},{24,20},{28,24},{32,28},{36,32}... | collective-permute-start | bytes 49160 | tf_op jit(solution)/shard_map/ppermute | solution.py:25
  90.6 1.4 collective-permute-done.11
  92.3 1.5 collective-permute-start.12
  93.8 1.3 collective-permute-start.13
  95.0 1.2 collective-permute-done.12
  96.3 5.9 %collective-permute-done.13 = f32[4,66,1,128]{3,2,1,0:T(1,128)S(1)} collective-permute-done((f32[4,66,1,128]{3,2,1,0:T(1,128)S(1)}, f32[4,66,1,128]{3,2,1,0:T(1,128)S(1)}, u32[]{:S(2)}, u32[]{:S(2)}) %collective-permute-start.13) | collective-permute-done | bytes 135200 | tf_op jit(solution)/shard_map/ppermute | solution.py:25
  103.2 2.1 %fusion.202 = (f32[4,66,10,1]{3,2,1,0:T(8,128)S(1)}, f32[4,66,10,1]{3,2,1,0:T(8,128)}) fusion(f32[4,66,10,128]{3,2,1,0:T(8,128)S(1)} %fusion.13), kind=kLoop, calls=%fused_computation.388 | loop fusion | bytes 42240 | tf_op jit(solution)/shard_map/slice | solution.py:20
  105.3 2.9 %copy.31 = f32[4,66,10,1]{1,0,3,2:T(4,128)} copy(f32[4,66,10,1]{3,2,1,0:T(8,128)} %get-tuple-element.14) | data formatting | bytes 21120 | tf_op jit(solution)/shard_map/slice | solution.py:19
  108.2 1.3 collective-permute-start.14
  109.5 1.4 copy.33
  110.9 5.7 %collective-permute-start.15 = (f32[4,66,10,1]{1,0,3,2:T(4,128)}, f32[4,66,10,1]{1,0,3,2:T(4,128)}, u32[]{:S(2)}, u32[]{:S(2)}) collective-permute-start(f32[4,66,10,1]{1,0,3,2:T(4,128)} %copy.33), channel_id=1, source_target_pairs={{0,1},{2,3},{4,5},{6,7},{8,9},{10,11},{12,13},{14,15},{16,17},{18,... | collective-permute-start | bytes 31688 | tf_op jit(solution)/shard_map/ppermute | solution.py:23
  116.6 1.7 %copy.32 = f32[4,66,10,1]{3,2,1,0:T(8,128)S(1)} copy(f32[4,66,10,1]{1,0,3,2:T(4,128)} %collective-permute-done.14) | data formatting | bytes 21120 | tf_op jit(solution)/shard_map/ppermute | solution.py:25
  118.4 3.5 %fusion.4 = f32[4,66,10,129]{3,2,1,0:T(8,128)} fusion(f32[1,64,8,128]{3,2,1,0:T(8,128)S(1)} %bitcast.96, f32[4,66,10,1]{3,2,1,0:T(8,128)S(1)} %copy.32, f32[4,66,1,128]{3,2,1,0:T(1,128)} %copy-done.10, f32[4,1,8,128]{3,2,1,0:T(8,128)S(1)} %collective-permute-done.11, f32[3,64,8,128]{3,2,1,0:T(8,128)S(1)} %broadcast_divide_fusion.1, ...), kind=kLoop, calls=%fused_computation.6 | loop fusion | flops 2043360 | bytes 2724480 | tf_op jit(solution)/shard_map/concatenate | solution.py:21
  121.9 1.7 %copy.34 = f32[4,66,10,1]{3,2,1,0:T(8,128)S(1)} copy(f32[4,66,10,1]{1,0,3,2:T(4,128)} %collective-permute-done.15) | data formatting | bytes 21120 | tf_op jit(solution)/shard_map/ppermute | solution.py:23
  123.6 3.8 %fusion.30 = f32[65,9,129]{2,1,0:T(8,128)S(1)} fusion(f32[1,64,8,128]{3,2,1,0:T(8,128)S(1)} %bitcast.97, f32[4,66,10,129]{3,2,1,0:T(8,128)} %fusion.4, f32[4,66,10,1]{3,2,1,0:T(8,128)S(1)} %copy.34, f32[4,66,1,128]{3,2,1,0:T(1,128)} %copy-done.10, f32[4,66,1,128]{3,2,1,0:T(1,128)} %copy-done.9, f32[4,1,8,128]{3,2,1,0:T(8,128)S(1)} %collective-permute-done.11, ...), kind=kLoop, calls=%fused_computation.70 | loop fusion | flops 981045 | bytes 3475260 | tf_op jit(solution)/shard_map/sub | solution.py:78
  128.2 1.9 %collective-permute-start.16 = (f32[4,1,8,128]{3,2,1,0:T(8,128)S(1)}, f32[4,1,8,128]{3,2,1,0:T(8,128)S(1)}, u32[]{:S(2)}, u32[]{:S(2)}) collective-permute-start(f32[4,1,8,128]{3,2,1,0:T(8,128)S(1)} %get-tuple-element.29), channel_id=1, source_target_pairs={{0,4},{4,8},{8,12},{12,16},{16,20},{20,24},{24,28},{28,32},{32,36}... | collective-permute-start | bytes 49160 | tf_op jit(solution)/shard_map/ppermute | solution.py:23
  130.1 7.0 %collective-permute-start.17 = (f32[4,1,8,128]{3,2,1,0:T(8,128)S(1)}, f32[4,1,8,128]{3,2,1,0:T(8,128)S(1)}, u32[]{:S(2)}, u32[]{:S(2)}) collective-permute-start(f32[4,1,8,128]{3,2,1,0:T(8,128)S(1)} %get-tuple-element.30), channel_id=1, source_target_pairs={{4,0},{8,4},{12,8},{16,12},{20,16},{24,20},{28,24},{32,28},{36,32}... | collective-permute-start | bytes 49160 | tf_op jit(solution)/shard_map/ppermute | solution.py:25
  137.1 1.4 collective-permute-done.17
  138.7 1.5 collective-permute-start.18
  140.2 1.3 collective-permute-start.19
  141.5 1.2 collective-permute-done.18
  142.8 5.9 %collective-permute-done.19 = f32[4,66,1,128]{3,2,1,0:T(1,128)S(1)} collective-permute-done((f32[4,66,1,128]{3,2,1,0:T(1,128)S(1)}, f32[4,66,1,128]{3,2,1,0:T(1,128)S(1)}, u32[]{:S(2)}, u32[]{:S(2)}) %collective-permute-start.19) | collective-permute-done | bytes 135200 | tf_op jit(solution)/shard_map/ppermute | solution.py:25
  149.0 2.1 %fusion.201 = (f32[4,66,10,1]{3,2,1,0:T(8,128)}, f32[4,66,10,1]{3,2,1,0:T(8,128)S(1)}) fusion(f32[4,66,10,128]{3,2,1,0:T(8,128)S(1)} %fusion.17), kind=kLoop, calls=%fused_computation.387 | loop fusion | bytes 42240 | tf_op jit(solution)/shard_map/slice | solution.py:19
  151.1 2.9 %copy.35 = f32[4,66,10,1]{1,0,3,2:T(4,128)} copy(f32[4,66,10,1]{3,2,1,0:T(8,128)} %get-tuple-element.11) | data formatting | bytes 21120 | tf_op jit(solution)/shard_map/slice | solution.py:19
  154.0 1.3 collective-permute-start.20
  156.2 5.1 %collective-permute-start.21 = (f32[4,66,10,1]{1,0,3,2:T(4,128)S(1)}, f32[4,66,10,1]{1,0,3,2:T(4,128)S(1)}, u32[]{:S(2)}, u32[]{:S(2)}) collective-permute-start(f32[4,66,10,1]{1,0,3,2:T(4,128)S(1)} %copy.37), channel_id=1, source_target_pairs={{0,1},{2,3},{4,5},{6,7},{8,9},{10,11},{12,13},{14,15},{16,17},{18,... | collective-permute-start | bytes 31688 | tf_op jit(solution)/shard_map/ppermute | solution.py:23
  161.3 1.7 %copy.36 = f32[4,66,10,1]{3,2,1,0:T(8,128)S(1)} copy(f32[4,66,10,1]{1,0,3,2:T(4,128)} %collective-permute-done.20) | data formatting | bytes 21120 | tf_op jit(solution)/shard_map/ppermute | solution.py:25
  163.0 2.6 %fusion.9 = f32[4,66,10,129]{3,2,1,0:T(8,128)} fusion(f32[1,64,8,128]{3,2,1,0:T(8,128)S(1)} %bitcast.100, f32[4,66,10,1]{3,2,1,0:T(8,128)S(1)} %copy.36, f32[4,66,1,128]{3,2,1,0:T(1,128)S(1)} %collective-permute-done.19, f32[4,1,8,128]{3,2,1,0:T(8,128)S(1)} %collective-permute-done.17, f32[3,64,8,128]{3,2,1,0:T(8,128)S(1)} %broadcast_divide_fusion, ...), kind=kLoop, calls=%fused_computation.11 | loop fusion | flops 2043360 | bytes 2724480 | tf_op jit(solution)/shard_map/concatenate | solution.py:21
  166.7 3.3 %fusion.38 = f32[65,9,129]{2,1,0:T(8,128)S(1)} fusion(f32[1,64,8,128]{3,2,1,0:T(8,128)S(1)} %bitcast.101, f32[4,66,10,1]{3,2,1,0:T(8,128)S(1)} %copy.38, f32[4,66,1,128]{3,2,1,0:T(1,128)S(1)} %collective-permute-done.19, f32[4,66,1,128]{3,2,1,0:T(1,128)S(1)} %collective-permute-done.18, f32[4,1,8,128]{3,2,1,0:T(8,128)S(1)} %collective-permute-done.17, ...), kind=kLoop, calls=%fused_computation.78 | loop fusion | flops 830115 | bytes 3173400 | tf_op jit(solution)/shard_map/add | solution.py:51
  (77 shorter events, 17.5 us)
Async XLA Ops:
  0.0 16.1 %copy-start.6 = (f32[64,8,128]{2,1,0:T(8,128)S(1)}, f32[64,8,128]{2,1,0:T(8,128)}, u32[]{:S(2)}) copy-start(f32[64,8,128]{2,1,0:T(8,128)} %param.2) | copy-start | bytes 786436
  0.9 14.1 %collective-permute-start = (f32[16,8,128]{2,1,0:T(8,128)S(1)}, f32[16,8,128]{2,1,0:T(8,128)S(1)}, u32[]{:S(2)}, u32[]{:S(2)}) collective-permute-start(f32[16,8,128]{2,1,0:T(8,128)S(1)} %get-tuple-element.41), channel_id=1, source_target_pairs={{0,4},{4,8},{8,12},{12,16},{16,20},{20,24},{24,28},{28,32},{32,36}... | collective-permute-start | bytes 196616 | tf_op jit(solution)/shard_map/ppermute | solution.py:23
  2.9 13.2 %collective-permute-start.1 = (f32[16,8,128]{2,1,0:T(8,128)S(1)}, f32[16,8,128]{2,1,0:T(8,128)S(1)}, u32[]{:S(2)}, u32[]{:S(2)}) collective-permute-start(f32[16,8,128]{2,1,0:T(8,128)S(1)} %get-tuple-element.42), channel_id=1, source_target_pairs={{4,0},{8,4},{12,8},{16,12},{20,16},{24,20},{28,24},{32,28},{36,32}... | collective-permute-start | bytes 196616 | tf_op jit(solution)/shard_map/ppermute | solution.py:25
  16.8 7.9 %collective-permute-start.2 = (f32[16,8,128]{2,1,0:T(8,128)S(1)}, f32[16,8,128]{2,1,0:T(8,128)S(1)}, u32[]{:S(2)}, u32[]{:S(2)}) collective-permute-start(f32[16,8,128]{2,1,0:T(8,128)S(1)} %get-tuple-element.37), channel_id=1, source_target_pairs={{4,0},{8,4},{12,8},{16,12},{20,16},{24,20},{28,24},{32,28},{36,32}... | collective-permute-start | bytes 196616 | tf_op jit(solution)/shard_map/ppermute | solution.py:25
  22.7 8.9 %collective-permute-start.3 = (f32[16,8,128]{2,1,0:T(8,128)S(1)}, f32[16,8,128]{2,1,0:T(8,128)S(1)}, u32[]{:S(2)}, u32[]{:S(2)}) collective-permute-start(f32[16,8,128]{2,1,0:T(8,128)S(1)} %get-tuple-element.38), channel_id=1, source_target_pairs={{0,4},{4,8},{8,12},{12,16},{16,20},{20,24},{24,28},{28,32},{32,36}... | collective-permute-start | bytes 196616 | tf_op jit(solution)/shard_map/ppermute | solution.py:23
  32.3 10.0 %collective-permute-start.4 = (f32[4,1,8,128]{3,2,1,0:T(8,128)S(1)}, f32[4,1,8,128]{3,2,1,0:T(8,128)S(1)}, u32[]{:S(2)}, u32[]{:S(2)}) collective-permute-start(f32[4,1,8,128]{3,2,1,0:T(8,128)S(1)} %get-tuple-element.35), channel_id=1, source_target_pairs={{0,4},{4,8},{8,12},{12,16},{16,20},{20,24},{24,28},{28,32},{32,36}... | collective-permute-start | bytes 49160 | tf_op jit(solution)/shard_map/ppermute | solution.py:23
  34.2 8.4 %collective-permute-start.5 = (f32[4,1,8,128]{3,2,1,0:T(8,128)S(1)}, f32[4,1,8,128]{3,2,1,0:T(8,128)S(1)}, u32[]{:S(2)}, u32[]{:S(2)}) collective-permute-start(f32[4,1,8,128]{3,2,1,0:T(8,128)S(1)} %get-tuple-element.36), channel_id=1, source_target_pairs={{4,0},{8,4},{12,8},{16,12},{20,16},{24,20},{28,24},{32,28},{36,32}... | collective-permute-start | bytes 49160 | tf_op jit(solution)/shard_map/ppermute | solution.py:25
  42.8 7.5 %collective-permute-start.6 = (f32[4,66,1,128]{3,2,1,0:T(1,128)S(1)}, f32[4,66,1,128]{3,2,1,0:T(1,128)S(1)}, u32[]{:S(2)}, u32[]{:S(2)}) collective-permute-start(f32[4,66,1,128]{3,2,1,0:T(1,128)S(1)} %get-tuple-element.21), channel_id=1, source_target_pairs={{0,2},{1,3},{4,6},{5,7},{8,10},{9,11},{12,14},{13,15},{16,18},{17,... | collective-permute-start | bytes 405512 | tf_op jit(solution)/shard_map/ppermute | solution.py:23
  47.7 8.4 %collective-permute-start.7 = (f32[4,66,1,128]{3,2,1,0:T(1,128)S(1)}, f32[4,66,1,128]{3,2,1,0:T(1,128)S(1)}, u32[]{:S(2)}, u32[]{:S(2)}) collective-permute-start(f32[4,66,1,128]{3,2,1,0:T(1,128)S(1)} %get-tuple-element.22), channel_id=1, source_target_pairs={{2,0},{3,1},{6,4},{7,5},{10,8},{11,9},{14,12},{15,13},{18,16},{19,... | collective-permute-start | bytes 405512 | tf_op jit(solution)/shard_map/ppermute | solution.py:25
  50.3 5.9 %copy-start.7 = (f32[4,66,1,128]{3,2,1,0:T(1,128)}, f32[4,66,1,128]{3,2,1,0:T(1,128)S(1)}, u32[]{:S(2)}) copy-start(f32[4,66,1,128]{3,2,1,0:T(1,128)S(1)} %collective-permute-done.6) | copy-start | bytes 405508
  56.2 0.7 copy-start.8
  61.6 8.4 %collective-permute-start.8 = (f32[4,66,10,1]{1,0,3,2:T(4,128)S(1)}, f32[4,66,10,1]{1,0,3,2:T(4,128)S(1)}, u32[]{:S(2)}, u32[]{:S(2)}) collective-permute-start(f32[4,66,10,1]{1,0,3,2:T(4,128)S(1)} %copy.27), channel_id=1, source_target_pairs={{1,0},{3,2},{5,4},{7,6},{9,8},{11,10},{13,12},{15,14},{17,16},{19,... | collective-permute-start | bytes 31688 | tf_op jit(solution)/shard_map/ppermute | solution.py:25
  64.9 9.5 %collective-permute-start.9 = (f32[4,66,10,1]{1,0,3,2:T(4,128)}, f32[4,66,10,1]{1,0,3,2:T(4,128)}, u32[]{:S(2)}, u32[]{:S(2)}) collective-permute-start(f32[4,66,10,1]{1,0,3,2:T(4,128)} %copy.29), channel_id=1, source_target_pairs={{0,1},{2,3},{4,5},{6,7},{8,9},{10,11},{12,13},{14,15},{16,17},{18,... | collective-permute-start | bytes 31688 | tf_op jit(solution)/shard_map/ppermute | solution.py:23
  76.1 3.8 %copy-start.11 = (pred[128]{0:T(512)(128)(4,1)S(1)}, pred[128]{0:T(512)(128)(4,1)}, u32[]{:S(2)}) copy-start(pred[128]{0:T(512)(128)(4,1)} %compare_and_fusion) | copy-start | bytes 388
  80.2 0.7 copy-start
  80.2 0.8 copy-start.2
  80.4 11.7 %copy-start.4 = (f32[64,8,128]{2,1,0:T(8,128)}, f32[64,8,128]{2,1,0:T(8,128)S(1)}, u32[]{:S(2)}) copy-start(f32[64,8,128]{2,1,0:T(8,128)S(1)} %fusion.155) | copy-start | bytes 786436
  81.7 8.9 %collective-permute-start.10 = (f32[4,1,8,128]{3,2,1,0:T(8,128)S(1)}, f32[4,1,8,128]{3,2,1,0:T(8,128)S(1)}, u32[]{:S(2)}, u32[]{:S(2)}) collective-permute-start(f32[4,1,8,128]{3,2,1,0:T(8,128)S(1)} %get-tuple-element.5), channel_id=1, source_target_pairs={{0,4},{4,8},{8,12},{12,16},{16,20},{20,24},{24,28},{28,32},{32,36}... | collective-permute-start | bytes 49160 | tf_op jit(solution)/shard_map/ppermute | solution.py:23
  83.6 8.4 %collective-permute-start.11 = (f32[4,1,8,128]{3,2,1,0:T(8,128)S(1)}, f32[4,1,8,128]{3,2,1,0:T(8,128)S(1)}, u32[]{:S(2)}, u32[]{:S(2)}) collective-permute-start(f32[4,1,8,128]{3,2,1,0:T(8,128)S(1)} %get-tuple-element.31), channel_id=1, source_target_pairs={{4,0},{8,4},{12,8},{16,12},{20,16},{24,20},{28,24},{32,28},{36,32}... | collective-permute-start | bytes 49160 | tf_op jit(solution)/shard_map/ppermute | solution.py:25
  92.3 4.0 %collective-permute-start.12 = (f32[4,66,1,128]{3,2,1,0:T(1,128)S(1)}, f32[4,66,1,128]{3,2,1,0:T(1,128)S(1)}, u32[]{:S(2)}, u32[]{:S(2)}) collective-permute-start(f32[4,66,1,128]{3,2,1,0:T(1,128)S(1)} %get-tuple-element.19), channel_id=1, source_target_pairs={{0,2},{1,3},{4,6},{5,7},{8,10},{9,11},{12,14},{13,15},{16,18},{17,... | collective-permute-start | bytes 405512 | tf_op jit(solution)/shard_map/ppermute | solution.py:23
  93.8 8.4 %collective-permute-start.13 = (f32[4,66,1,128]{3,2,1,0:T(1,128)S(1)}, f32[4,66,1,128]{3,2,1,0:T(1,128)S(1)}, u32[]{:S(2)}, u32[]{:S(2)}) collective-permute-start(f32[4,66,1,128]{3,2,1,0:T(1,128)S(1)} %get-tuple-element.20), channel_id=1, source_target_pairs={{2,0},{3,1},{6,4},{7,5},{10,8},{11,9},{14,12},{15,13},{18,16},{19,... | collective-permute-start | bytes 405512 | tf_op jit(solution)/shard_map/ppermute | solution.py:25
  96.3 5.9 %copy-start.9 = (f32[4,66,1,128]{3,2,1,0:T(1,128)}, f32[4,66,1,128]{3,2,1,0:T(1,128)S(1)}, u32[]{:S(2)}) copy-start(f32[4,66,1,128]{3,2,1,0:T(1,128)S(1)} %collective-permute-done.12) | copy-start | bytes 405508
  102.2 0.6 copy-start.10
  108.2 8.4 %collective-permute-start.14 = (f32[4,66,10,1]{1,0,3,2:T(4,128)}, f32[4,66,10,1]{1,0,3,2:T(4,128)}, u32[]{:S(2)}, u32[]{:S(2)}) collective-permute-start(f32[4,66,10,1]{1,0,3,2:T(4,128)} %copy.31), channel_id=1, source_target_pairs={{1,0},{3,2},{5,4},{7,6},{9,8},{11,10},{13,12},{15,14},{17,16},{19,... | collective-permute-start | bytes 31688 | tf_op jit(solution)/shard_map/ppermute | solution.py:25
  110.9 10.9 %collective-permute-start.15 = (f32[4,66,10,1]{1,0,3,2:T(4,128)}, f32[4,66,10,1]{1,0,3,2:T(4,128)}, u32[]{:S(2)}, u32[]{:S(2)}) collective-permute-start(f32[4,66,10,1]{1,0,3,2:T(4,128)} %copy.33), channel_id=1, source_target_pairs={{0,1},{2,3},{4,5},{6,7},{8,9},{10,11},{12,13},{14,15},{16,17},{18,... | collective-permute-start | bytes 31688 | tf_op jit(solution)/shard_map/ppermute | solution.py:23
  123.6 4.1 %copy-start.1 = (f32[1,64,8,128]{3,2,1,0:T(8,128)S(1)}, f32[1,64,8,128]{3,2,1,0:T(8,128)}, u32[]{:S(2)}) copy-start(f32[1,64,8,128]{3,2,1,0:T(8,128)} %copy-done) | copy-start | bytes 786436
  123.6 4.1 %copy-start.3 = (f32[1,64,8,128]{3,2,1,0:T(8,128)S(1)}, f32[1,64,8,128]{3,2,1,0:T(8,128)}, u32[]{:S(2)}) copy-start(f32[1,64,8,128]{3,2,1,0:T(8,128)} %copy-done.2) | copy-start | bytes 786436
  123.6 4.1 %copy-start.5 = (f32[64,8,128]{2,1,0:T(8,128)S(1)}, f32[64,8,128]{2,1,0:T(8,128)}, u32[]{:S(2)}) copy-start(f32[64,8,128]{2,1,0:T(8,128)} %copy-done.4) | copy-start | bytes 786436
  128.2 8.9 %collective-permute-start.16 = (f32[4,1,8,128]{3,2,1,0:T(8,128)S(1)}, f32[4,1,8,128]{3,2,1,0:T(8,128)S(1)}, u32[]{:S(2)}, u32[]{:S(2)}) collective-permute-start(f32[4,1,8,128]{3,2,1,0:T(8,128)S(1)} %get-tuple-element.29), channel_id=1, source_target_pairs={{0,4},{4,8},{8,12},{12,16},{16,20},{20,24},{24,28},{28,32},{32,36}... | collective-permute-start | bytes 49160 | tf_op jit(solution)/shard_map/ppermute | solution.py:23
  130.1 8.4 %collective-permute-start.17 = (f32[4,1,8,128]{3,2,1,0:T(8,128)S(1)}, f32[4,1,8,128]{3,2,1,0:T(8,128)S(1)}, u32[]{:S(2)}, u32[]{:S(2)}) collective-permute-start(f32[4,1,8,128]{3,2,1,0:T(8,128)S(1)} %get-tuple-element.30), channel_id=1, source_target_pairs={{4,0},{8,4},{12,8},{16,12},{20,16},{24,20},{28,24},{32,28},{36,32}... | collective-permute-start | bytes 49160 | tf_op jit(solution)/shard_map/ppermute | solution.py:25
  138.7 4.0 %collective-permute-start.18 = (f32[4,66,1,128]{3,2,1,0:T(1,128)S(1)}, f32[4,66,1,128]{3,2,1,0:T(1,128)S(1)}, u32[]{:S(2)}, u32[]{:S(2)}) collective-permute-start(f32[4,66,1,128]{3,2,1,0:T(1,128)S(1)} %get-tuple-element.17), channel_id=1, source_target_pairs={{0,2},{1,3},{4,6},{5,7},{8,10},{9,11},{12,14},{13,15},{16,18},{17,... | collective-permute-start | bytes 405512 | tf_op jit(solution)/shard_map/ppermute | solution.py:23
  140.2 8.4 %collective-permute-start.19 = (f32[4,66,1,128]{3,2,1,0:T(1,128)S(1)}, f32[4,66,1,128]{3,2,1,0:T(1,128)S(1)}, u32[]{:S(2)}, u32[]{:S(2)}) collective-permute-start(f32[4,66,1,128]{3,2,1,0:T(1,128)S(1)} %get-tuple-element.18), channel_id=1, source_target_pairs={{2,0},{3,1},{6,4},{7,5},{10,8},{11,9},{14,12},{15,13},{18,16},{19,... | collective-permute-start | bytes 405512 | tf_op jit(solution)/shard_map/ppermute | solution.py:25
  154.0 7.3 %collective-permute-start.20 = (f32[4,66,10,1]{1,0,3,2:T(4,128)}, f32[4,66,10,1]{1,0,3,2:T(4,128)}, u32[]{:S(2)}, u32[]{:S(2)}) collective-permute-start(f32[4,66,10,1]{1,0,3,2:T(4,128)} %copy.35), channel_id=1, source_target_pairs={{1,0},{3,2},{5,4},{7,6},{9,8},{11,10},{13,12},{15,14},{17,16},{19,... | collective-permute-start | bytes 31688 | tf_op jit(solution)/shard_map/ppermute | solution.py:25
  156.2 9.5 %collective-permute-start.21 = (f32[4,66,10,1]{1,0,3,2:T(4,128)S(1)}, f32[4,66,10,1]{1,0,3,2:T(4,128)S(1)}, u32[]{:S(2)}, u32[]{:S(2)}) collective-permute-start(f32[4,66,10,1]{1,0,3,2:T(4,128)S(1)} %copy.37), channel_id=1, source_target_pairs={{0,1},{2,3},{4,5},{6,7},{8,9},{10,11},{12,13},{14,15},{16,17},{18,... | collective-permute-start | bytes 31688 | tf_op jit(solution)/shard_map/ppermute | solution.py:23
where the time goes:
time: 172 us; the launch traced here: 171 us
  starting transfers between devices  78.3 us (46%)
  local copies, waits for them, and re-layouts  32.3 us (19%)
  waiting for transfers between devices  31.4 us (18%)
  other arithmetic  28.2 us (16%)
    ppermute x11, starting transfers between devices, extended_2(): lax.ppermute(head, axis, [((i + 1) % count, i) for i in range(ends)])  44.8 us
    ppermute x11, starting transfers between devices, extended_2(): lax.ppermute(tail, axis, [(i, (i + 1) % count) for i in range(ends)])  33.5 us
    ppermute x11, waiting for transfers between devices, extended_2(): lax.ppermute(head, axis, [((i + 1) % count, i) for i in range(ends)])  20.7 us
    concatenate x8, other arithmetic, extended_2(): jnp.concatenate([lax.ppermute(tail, axis, [(i, (i + 1) % count) for i in...  10.7 us
    ppermute x11, waiting for transfers between devices, extended_2(): lax.ppermute(tail, axis, [(i, (i + 1) % count) for i in range(ends)])  10.6 us
    slice x5, local copies, waits for them, and re-layouts, extended_2(): head = lax.slice_in_dim(cells, 0, width, axis=dim)  10.2 us
    slice x9, local copies, waits for them, and re-layouts, extended_2(): lax.slice_in_dim(cells, cells.shape[dim] - width, cells.shape[dim], axis=...  9.13 us
    sub x2, other arithmetic, body(): target = wide_divergence(padded) - padded[3, 1:, 1:, 1:] / theta  7.63 us
  transfers between devices with their start and end apart: 22, of which 10 were waited for; matrix products, arithmetic and copies ran while one was open for 13% of the time, Pallas kernels for 0%

commit v1 on v0

v1 whole, which is shorter than its diff:
```python
import jax
import jax.numpy as jnp
from jax import lax
from jax.experimental import pallas as pl
from jax.experimental.pallas import tpu as pltpu
from jax.sharding import PartitionSpec as P

theta = 0.1
inner_step = 1.0 / 12.0
scale = -inner_step / theta

REACH = 2
BLOCK = 10
PAIR = ((0, 1), (1, 0))


def blur_kernel(u_ref, near_ref, far_ref, kernel_ref, v_ref, strip_ref, edge_ref, upad, fwd, adj, q, vflat):
    tm, row, col = lax.axis_index("tm"), lax.axis_index("row"), lax.axis_index("col")
    frames, rows, cols = u_ref.shape
    taps = kernel_ref.shape[0]
    half = taps // 2
    halo = 2 * half + REACH
    span = frames + 2 * REACH
    deep = v_ref.shape[1]

    odd = lax.rem(tm, 2)
    upad[halo : halo + frames] = u_ref[...]
    upad[pl.ds((1 - odd) * (halo + frames), halo)] = near_ref[...]
    upad[pl.ds(odd * (halo + frames), halo)] = far_ref[...]

    total = kernel_ref[0]
    for tap in range(1, taps):
        total = total + kernel_ref[tap]
    inverse = 1.0 / total
    for tap in range(taps):
        share = kernel_ref[tap] * inverse
        adj[tap] = share
        fwd[tap] = (share - 1.0 if tap == half else share) * (1.0 / 3.0)

    q_count = frames + 2 * (half + REACH)

    def forward(step, carry):
        base = step * BLOCK
        window = [upad[base + i] for i in range(BLOCK + taps - 1)]
        acc = [None] * BLOCK
        for tap in range(taps):
            weight = fwd[tap]
            for i in range(BLOCK):
                term = weight * window[i + tap]
                acc[i] = term if tap == 0 else acc[i] + term
        for i in range(BLOCK):
            q[base + i] = acc[i]
        return carry

    lax.fori_loop(0, q_count // BLOCK, forward, 0)
    nothing = jnp.zeros((half + REACH, rows, cols), jnp.float32)

    @pl.when(tm == 0)
    def _():
        q[: half + REACH] = nothing

    @pl.when(tm == lax.axis_size("tm") - 1)
    def _():
        q[q_count - half - REACH : q_count] = nothing

    q[q_count:] = jnp.zeros((q.shape[0] - q_count, rows, cols), jnp.float32)

    def adjoint(step, carry):
        base = step * BLOCK
        window = [q[base + i] for i in range(BLOCK + taps - 1)]
        acc = [None] * BLOCK
        for tap in range(taps):
            weight = adj[tap]
            for i in range(BLOCK):
                term = weight * window[i + taps - 1 - tap]
                acc[i] = term if tap == 0 else acc[i] + term
        for i in range(BLOCK):
            at = pl.multiple_of((base + i) * rows, rows)
            vflat[pl.ds(at, rows)] = upad[base + i + 2 * half] - acc[i]
        return carry

    steps = -(-span // BLOCK)
    lax.fori_loop(0, steps, adjoint, 0)
    vflat[steps * BLOCK * rows :] = jnp.zeros((vflat.shape[0] - steps * BLOCK * rows, cols), jnp.float32)

    lane = lax.broadcasted_iota(jnp.int32, (deep, cols), 1)
    edge = jnp.zeros((deep, cols), jnp.float32)
    for r in range(rows):
        plane = vflat[pl.ds(r, deep, stride=rows)]
        v_ref[r] = plane
        first = 4 * (r + 2 * row)
        moved = pltpu.roll(plane, first + 2, axis=1)
        low = first + 2 * col
        edge = jnp.where((lane >= low) & (lane < low + 2), moved, edge)
    edge_ref[...] = edge
    begin = (rows - 2) * (1 - row)
    strip_ref[0] = v_ref[begin]
    strip_ref[1] = v_ref[begin + 1]


def unit(z_t, z_r, z_c):
    factor = lax.rsqrt(jnp.maximum(1.0, z_t * z_t + z_r * z_r + z_c * z_c))
    return z_t * factor, z_r * factor, z_c * factor


def tv_kernel(v_ref, strip_ref, side_ref, corner_ref, out_ref, w, p_t, p_r, p_c, e_w, e_t, e_c):
    tm, row, col = lax.axis_index("tm"), lax.axis_index("row"), lax.axis_index("col")
    rows, deep, cols = v_ref.shape
    frames = out_ref.shape[0] // rows
    wide = rows + REACH

    lane = lax.broadcasted_iota(jnp.int32, (deep, cols), 1)
    time = lax.broadcasted_iota(jnp.int32, (deep, cols), 0)
    ends = ((tm == 0) & (time == REACH - 1)) | (
        (tm == lax.axis_size("tm") - 1) & (time == frames + REACH - 1)
    )
    keep_t = jnp.where(ends, 0.0, 1.0)
    keep_c = jnp.where((col == 1) & (lane == cols - 1), 0.0, 1.0)
    last, first = lane == cols - 1, lane == 0
    keep_r = jnp.where(lane < 4 * (wide - 1), 1.0, 0.0)
    is_right = jnp.where(col == 1, 1.0, 0.0)

    own = REACH * row
    foreign = rows * (1 - row)
    for r in range(rows):
        w[r + own, :deep] = v_ref[r] * scale
    for i in range(REACH):
        w[foreign + i, :deep] = strip_ref[i] * scale
    w[wide, :deep] = w[wide - 1, :deep]

    low = 4 * foreign
    corner = pltpu.roll(corner_ref[...], jnp.where(row == 0, 24, cols - 24), axis=1)
    edge = side_ref[...] + jnp.where((lane >= low) & (lane < low + 8), corner, 0.0)
    edge = edge * scale
    for r in range(wide):
        moved = pltpu.roll(w[r, :deep], 4 * r + 2, axis=1)
        begin = 4 * r + 2 * col
        edge = jnp.where((lane >= begin) & (lane < begin + 2), moved, edge)

    def edge_slopes(field):
        e_w[:deep] = field
        g_t = (e_w[1 : deep + 1] - field) * keep_t
        g_r = (pltpu.roll(field, cols - 4, axis=1) - field) * keep_r
        g_c = pltpu.roll(field, cols - 1, axis=1) - field
        return g_t, g_r, g_c

    e1 = unit(*edge_slopes(edge))
    e_t[8 : deep + 8] = e1[0]
    edge_div = e1[0] - e_t[7 : deep + 7] + e1[1] - pltpu.roll(e1[1], 4, axis=1) + e1[2] - pltpu.roll(e1[2], 1, axis=1)
    edge2 = edge_div * inner_step + edge
    slopes2 = edge_slopes(edge2)
    e2 = unit(e1[0] + slopes2[0], e1[1] + slopes2[1], e1[2] + slopes2[2])
    e_c[0] = edge
    e_c[1] = e1[2] * is_right
    e_c[2] = edge2
    e_c[3] = e2[2] * is_right

    def slopes(r, which):
        here = w[r, :deep]
        g_t = (w[r, 1 : deep + 1] - here) * keep_t
        g_r = w[r + 1, :deep] - here
        right = jnp.where(last, pltpu.roll(e_c[which], cols - 3 - 4 * r, axis=1), pltpu.roll(here, cols - 1, axis=1))
        return g_t, g_r, (right - here) * keep_c

    def store(r, p):
        p_t[r, 8 : deep + 8] = p[0]
        p_r[r + 1] = p[1]
        p_c[r] = p[2]

    def divergence(r, which):
        here = p_c[r]
        left = jnp.where(first, pltpu.roll(e_c[which], cols - 1 - 4 * r, axis=1), pltpu.roll(here, 1, axis=1))
        return p_t[r, 8 : deep + 8] - p_t[r, 7 : deep + 7] + p_r[r + 1] - p_r[r] + here - left

    p_r[0] = jnp.zeros((deep, cols), jnp.float32)

    def first_pass(r, carry):
        store(r, unit(*slopes(r, 0)))
        return carry

    def second_w(r, carry):
        w[r, :deep] = divergence(r, 1) * inner_step + w[r, :deep]
        return carry

    def second_pass(r, carry):
        g_t, g_r, g_c = slopes(r, 2)
        store(r, unit(p_t[r, 8 : deep + 8] + g_t, p_r[r + 1] + g_r, p_c[r] + g_c))
        return carry

    lax.fori_loop(0, wide, first_pass, 0)
    lax.fori_loop(0, wide, second_w, 0)
    w[wide, :deep] = w[wide - 1, :deep]
    lax.fori_loop(0, wide, second_pass, 0)
    for r in range(rows):
        updated = v_ref[r] - theta * divergence(r + own, 3)
        p_c[r + own] = updated
        out_ref[pl.ds(r, frames, stride=rows)] = p_c[r + own, REACH : REACH + frames]


def body(observed, kernel):
    frames, rows, cols = observed.shape
    taps = kernel.shape[0]
    half = taps // 2
    halo = 2 * half + REACH
    deep = -(-(frames + 2 * REACH) // 8) * 8
    count = lax.axis_size("tm")
    odd = lax.axis_index("tm") % 2
    vmem = pl.BlockSpec(memory_space=pltpu.VMEM)
    f32 = jnp.float32

    near = lax.dynamic_slice_in_dim(observed, (1 - odd) * (frames - halo), halo, axis=0)
    far = lax.dynamic_slice_in_dim(observed, odd * (frames - halo), halo, axis=0)
    far = lax.ppermute(far, "tm", [(i, i + 1 if i % 2 else i - 1) for i in range(1, count - 1)])
    near = lax.ppermute(near, "tm", [(i, i ^ 1) for i in range(count)])

    v, strip, edge = pl.pallas_call(
        blur_kernel,
        out_shape=(
            jax.ShapeDtypeStruct((rows, deep, cols), f32),
            jax.ShapeDtypeStruct((REACH, deep, cols), f32),
            jax.ShapeDtypeStruct((deep, cols), f32),
        ),
        in_specs=[vmem] * 4,
        out_specs=(vmem,) * 3,
        scratch_shapes=[
            pltpu.VMEM((frames + 2 * halo, rows, cols), f32),
            pltpu.VMEM((taps, rows, cols), f32),
            pltpu.VMEM((taps, rows, cols), f32),
            pltpu.VMEM((deep + 2 * half, rows, cols), f32),
            pltpu.VMEM((deep * rows, cols), f32),
        ],
        name="blur",
    )(observed, near, far, kernel)

    strip = lax.ppermute(strip, "row", PAIR)
    side = lax.ppermute(edge, "col", PAIR)
    corner = lax.ppermute(edge, ("row", "col"), [(0, 3), (3, 0), (1, 2), (2, 1)])

    wide = rows + REACH
    out = pl.pallas_call(
        tv_kernel,
        out_shape=jax.ShapeDtypeStruct((frames * rows, cols), f32),
        in_specs=[vmem] * 4,
        out_specs=vmem,
        scratch_shapes=[
            pltpu.VMEM((wide + 1, deep + 8, cols), f32),
            pltpu.VMEM((wide, deep + 8, cols), f32),
            pltpu.VMEM((wide + 1, deep, cols), f32),
            pltpu.VMEM((wide, deep, cols), f32),
            pltpu.VMEM((deep + 8, cols), f32),
            pltpu.VMEM((deep + 8, cols), f32),
            pltpu.VMEM((4, deep, cols), f32),
        ],
        name="tv",
    )(v, strip, side, corner)
    return out.reshape(frames, rows, cols)


def solution(mesh):
    in_specs = (P("tm", "row", "col"), P(None, "row", "col"))
    out_specs = P("tm", "row", "col")
    return jax.shard_map(body, mesh=mesh, in_specs=in_specs, out_specs=out_specs, check_vma=False)
```

time: 172 us -> 40.7 us (0.24)
  the two profiles are of different devices: /device:TPU:32 before, /device:TPU:56 now
where the time goes in v1:
time: 40.7 us; the launch traced here: 40.5 us
  starting transfers between devices  23 us (57%)
  Pallas kernels  9.57 us (24%)
  waiting for transfers between devices  5.46 us (13%)
  local copies, waits for them, and re-layouts  2.42 us (6%)
    ppermute x1, starting transfers between devices, body(): lax.ppermute(far, 'tm', [(i, i + 1 if i % 2 else i - 1) for i in range(1,...  11.2 us
    pallas_call x1, Pallas kernels, body(): pl.pallas_call(tv_kernel, out_shape=jax.ShapeDtypeStruct((frames * rows,...  5.59 us
    ppermute x1, starting transfers between devices, body(): strip = lax.ppermute(strip, 'row', PAIR)  4.92 us
    pallas_call x1, Pallas kernels, body(): pl.pallas_call(blur_kernel, out_shape=(jax.ShapeDtypeStruct((rows, deep,...  3.99 us
    ppermute x1, starting transfers between devices, body(): lax.ppermute(edge, ('row', 'col'), [(0, 3), (3, 0), (1, 2), (2, 1)])  3.05 us
    ppermute x1, waiting for transfers between devices, body(): lax.ppermute(edge, ('row', 'col'), [(0, 3), (3, 0), (1, 2), (2, 1)])  2.29 us
    ppermute x1, starting transfers between devices, body(): near = lax.ppermute(near, 'tm', [(i, i ^ 1) for i in range(count)])  1.92 us
    ppermute x1, starting transfers between devices, body(): side = lax.ppermute(edge, 'col', PAIR)  1.92 us
  transfers between devices with their start and end apart: 5, of which 4 were waited for; matrix products, arithmetic and copies ran while one was open for 0% of the time, Pallas kernels for 0%

profile of v1, /device:TPU:56, one launch (start us, length us, event | category | flops | bytes accessed | tf_op | source)
XLA Modules:
  0.0 40.5 jit_solution(368202810380671435)
XLA Ops:
  0.0 1.0 %constant_dynamic-slice_fusion = (f32[34,8,128]{2,1,0:T(8,128)S(1)}, f32[34,8,128]{2,1,0:T(8,128)S(1)}) fusion(f32[64,8,128]{2,1,0:T(8,128)} %u_ref.1, s32[]{:T(128)S(6)} %select_n.15, s32[]{:T(128)S(6)} %select_n.14), kind=kLoop, calls=%fused_computation | loop fusion | bytes 557064 | tf_op jit(solution)/shard_map/dynamic_slice | solution.py:212
  1.0 11.2 %collective-permute-start.1 = (f32[34,8,128]{2,1,0:T(8,128)S(1)}, f32[34,8,128]{2,1,0:T(8,128)S(1)}, u32[]{:S(2)}, u32[]{:S(2)}) collective-permute-start(f32[34,8,128]{2,1,0:T(8,128)S(1)} %get-tuple-element.11), channel_id=1, source_target_pairs={{4,8},{8,4},{12,16},{16,12},{20,24},{24,20},{28,32},{32,28},{36,40... | collective-permute-start | bytes 417800 | tf_op jit(solution)/shard_map/ppermute | solution.py:213
  12.2 1.9 %collective-permute-start = (f32[34,8,128]{2,1,0:T(8,128)S(1)}, f32[34,8,128]{2,1,0:T(8,128)S(1)}, u32[]{:S(2)}, u32[]{:S(2)}) collective-permute-start(f32[34,8,128]{2,1,0:T(8,128)S(1)} %get-tuple-element.12), channel_id=1, source_target_pairs={{0,4},{4,0},{8,12},{12,8},{16,20},{20,16},{24,28},{28,24},{32,36},... | collective-permute-start | bytes 417800 | tf_op jit(solution)/shard_map/ppermute | solution.py:214
  14.1 0.8 %collective-permute-done.1.far_ref = f32[34,8,128]{2,1,0:T(8,128)S(1)} collective-permute-done((f32[34,8,128]{2,1,0:T(8,128)S(1)}, f32[34,8,128]{2,1,0:T(8,128)S(1)}, u32[]{:S(2)}, u32[]{:S(2)}) %collective-permute-start.1) | collective-permute-done | bytes 139296 | tf_op jit(solution)/shard_map/ppermute | solution.py:213
  14.9 0.0 copy-start
  14.9 0.5 %collective-permute-done.near_ref = f32[34,8,128]{2,1,0:T(8,128)S(1)} collective-permute-done((f32[34,8,128]{2,1,0:T(8,128)S(1)}, f32[34,8,128]{2,1,0:T(8,128)S(1)}, u32[]{:S(2)}, u32[]{:S(2)}) %collective-permute-start) | collective-permute-done | bytes 139296 | tf_op jit(solution)/shard_map/ppermute | solution.py:214
  15.4 0.1 copy-done
  15.6 0.0 copy-start.1
  15.6 0.7 %copy-done.1 = f32[34,8,128]{2,1,0:T(8,128)} copy-done((f32[34,8,128]{2,1,0:T(8,128)}, f32[34,8,128]{2,1,0:T(8,128)S(1)}, u32[]{:S(2)}) %copy-start.1) | copy-done | bytes 139288
  16.2 4.0 %blur.1 = (f32[8,72,128]{2,1,0:T(8,128)}, f32[2,72,128]{2,1,0:T(8,128)}, f32[72,128]{1,0:T(8,128)}) custom-call(f32[64,8,128]{2,1,0:T(8,128)} %u_ref.1, f32[34,8,128]{2,1,0:T(8,128)} %copy-done.1, f32[34,8,128]{2,1,0:T(8,128)} %copy-done, f32[33,8,128]{2,1,0:T(8,128)} %kernel_ref.1), custom_call_target="tpu_custom_call" | custom-call | tf_op jit(solution)/shard_map/blur/pallas_call | solution.py:216
  20.2 4.9 %collective-permute-start.2 = (f32[2,72,128]{2,1,0:T(8,128)}, f32[2,72,128]{2,1,0:T(8,128)S(1)}, u32[]{:S(2)}, u32[]{:S(2)}) collective-permute-start(f32[2,72,128]{2,1,0:T(8,128)} %get-tuple-element.9), channel_id=1, source_target_pairs={{0,2},{2,0},{1,3},{3,1},{4,6},{6,4},{5,7},{7,5},{8,10},{10,8},{9,1... | collective-permute-start | bytes 221192 | tf_op jit(solution)/shard_map/ppermute | solution.py:235
  25.1 3.0 %collective-permute-start.4 = (f32[72,128]{1,0:T(8,128)}, f32[72,128]{1,0:T(8,128)S(1)}, u32[]{:S(2)}, u32[]{:S(2)}) collective-permute-start(f32[72,128]{1,0:T(8,128)} %get-tuple-element.10), channel_id=1, source_target_pairs={{0,3},{3,0},{1,2},{2,1},{4,7},{7,4},{5,6},{6,5},{8,11},{11,8},{9,1... | collective-permute-start | bytes 110600 | tf_op jit(solution)/shard_map/ppermute | solution.py:237
  28.2 1.9 %collective-permute-start.3 = (f32[72,128]{1,0:T(8,128)}, f32[72,128]{1,0:T(8,128)S(1)}, u32[]{:S(2)}, u32[]{:S(2)}) collective-permute-start(f32[72,128]{1,0:T(8,128)} %get-tuple-element.10), channel_id=1, source_target_pairs={{0,1},{1,0},{2,3},{3,2},{4,5},{5,4},{6,7},{7,6},{8,9},{9,8},{10,11... | collective-permute-start | bytes 110600 | tf_op jit(solution)/shard_map/ppermute | solution.py:236
  30.1 2.3 %collective-permute-done.4.corner_ref = f32[72,128]{1,0:T(8,128)S(1)} collective-permute-done((f32[72,128]{1,0:T(8,128)}, f32[72,128]{1,0:T(8,128)S(1)}, u32[]{:S(2)}, u32[]{:S(2)}) %collective-permute-start.4) | collective-permute-done | bytes 36896 | tf_op jit(solution)/shard_map/ppermute | solution.py:237
  32.4 0.0 copy-start.3
  32.4 1.8 %collective-permute-done.3.side_ref = f32[72,128]{1,0:T(8,128)S(1)} collective-permute-done((f32[72,128]{1,0:T(8,128)}, f32[72,128]{1,0:T(8,128)S(1)}, u32[]{:S(2)}, u32[]{:S(2)}) %collective-permute-start.3) | collective-permute-done | bytes 36896 | tf_op jit(solution)/shard_map/ppermute | solution.py:236
  34.3 0.0 copy-start.4
  34.3 0.0 collective-permute-done.2.strip_ref
  34.3 0.0 copy-start.2
  34.3 0.0 copy-done.3
  34.3 0.6 %copy-done.4 = f32[72,128]{1,0:T(8,128)} copy-done((f32[72,128]{1,0:T(8,128)}, f32[72,128]{1,0:T(8,128)S(1)}, u32[]{:S(2)}) %copy-start.4) | copy-done | bytes 36888
  34.9 0.0 copy-done.2
  34.9 5.6 %tv.1 = f32[512,128]{1,0:T(8,128)} custom-call(f32[8,72,128]{2,1,0:T(8,128)} %get-tuple-element.8.v_ref, f32[2,72,128]{2,1,0:T(8,128)} %copy-done.2, f32[72,128]{1,0:T(8,128)} %copy-done.4, f32[72,128]{1,0:T(8,128)} %copy-done.3), custom_call_target="tpu_custom_call" | custom-call | tf_op jit(solution)/shard_map/tv/pallas_call | solution.py:240
Async XLA Ops:
  1.0 13.9 %collective-permute-start.1 = (f32[34,8,128]{2,1,0:T(8,128)S(1)}, f32[34,8,128]{2,1,0:T(8,128)S(1)}, u32[]{:S(2)}, u32[]{:S(2)}) collective-permute-start(f32[34,8,128]{2,1,0:T(8,128)S(1)} %get-tuple-element.11), channel_id=1, source_target_pairs={{4,8},{8,4},{12,16},{16,12},{20,24},{24,20},{28,32},{32,28},{36,40... | collective-permute-start | bytes 417800 | tf_op jit(solution)/shard_map/ppermute | solution.py:213
  12.2 3.3 %collective-permute-start = (f32[34,8,128]{2,1,0:T(8,128)S(1)}, f32[34,8,128]{2,1,0:T(8,128)S(1)}, u32[]{:S(2)}, u32[]{:S(2)}) collective-permute-start(f32[34,8,128]{2,1,0:T(8,128)S(1)} %get-tuple-element.12), channel_id=1, source_target_pairs={{0,4},{4,0},{8,12},{12,8},{16,20},{20,16},{24,28},{28,24},{32,36},... | collective-permute-start | bytes 417800 | tf_op jit(solution)/shard_map/ppermute | solution.py:214
  14.9 0.7 %copy-start = (f32[34,8,128]{2,1,0:T(8,128)}, f32[34,8,128]{2,1,0:T(8,128)S(1)}, u32[]{:S(2)}) copy-start(f32[34,8,128]{2,1,0:T(8,128)S(1)} %collective-permute-done.1.far_ref) | copy-start | bytes 417796
  15.6 0.7 %copy-start.1 = (f32[34,8,128]{2,1,0:T(8,128)}, f32[34,8,128]{2,1,0:T(8,128)S(1)}, u32[]{:S(2)}) copy-start(f32[34,8,128]{2,1,0:T(8,128)S(1)} %collective-permute-done.near_ref) | copy-start | bytes 417796
  20.2 14.1 %collective-permute-start.2 = (f32[2,72,128]{2,1,0:T(8,128)}, f32[2,72,128]{2,1,0:T(8,128)S(1)}, u32[]{:S(2)}, u32[]{:S(2)}) collective-permute-start(f32[2,72,128]{2,1,0:T(8,128)} %get-tuple-element.9), channel_id=1, source_target_pairs={{0,2},{2,0},{1,3},{3,1},{4,6},{6,4},{5,7},{7,5},{8,10},{10,8},{9,1... | collective-permute-start | bytes 221192 | tf_op jit(solution)/shard_map/ppermute | solution.py:235
  25.1 7.3 %collective-permute-start.4 = (f32[72,128]{1,0:T(8,128)}, f32[72,128]{1,0:T(8,128)S(1)}, u32[]{:S(2)}, u32[]{:S(2)}) collective-permute-start(f32[72,128]{1,0:T(8,128)} %get-tuple-element.10), channel_id=1, source_target_pairs={{0,3},{3,0},{1,2},{2,1},{4,7},{7,4},{5,6},{6,5},{8,11},{11,8},{9,1... | collective-permute-start | bytes 110600 | tf_op jit(solution)/shard_map/ppermute | solution.py:237
  28.2 6.1 %collective-permute-start.3 = (f32[72,128]{1,0:T(8,128)}, f32[72,128]{1,0:T(8,128)S(1)}, u32[]{:S(2)}, u32[]{:S(2)}) collective-permute-start(f32[72,128]{1,0:T(8,128)} %get-tuple-element.10), channel_id=1, source_target_pairs={{0,1},{1,0},{2,3},{3,2},{4,5},{5,4},{6,7},{7,6},{8,9},{9,8},{10,11... | collective-permute-start | bytes 110600 | tf_op jit(solution)/shard_map/ppermute | solution.py:236
  32.4 1.9 %copy-start.3 = (f32[72,128]{1,0:T(8,128)}, f32[72,128]{1,0:T(8,128)S(1)}, u32[]{:S(2)}) copy-start(f32[72,128]{1,0:T(8,128)S(1)} %collective-permute-done.4.corner_ref) | copy-start | bytes 110596
  34.3 0.6 %copy-start.4 = (f32[72,128]{1,0:T(8,128)}, f32[72,128]{1,0:T(8,128)S(1)}, u32[]{:S(2)}) copy-start(f32[72,128]{1,0:T(8,128)S(1)} %collective-permute-done.3.side_ref) | copy-start | bytes 110596
  34.3 0.6 %copy-start.2 = (f32[2,72,128]{2,1,0:T(8,128)}, f32[2,72,128]{2,1,0:T(8,128)S(1)}, u32[]{:S(2)}) copy-start(f32[2,72,128]{2,1,0:T(8,128)S(1)} %collective-permute-done.2.strip_ref) | copy-start | bytes 221188

commit v2 on v1

--- a/solution.py
+++ b/solution.py
@@ -197,6 +197,10 @@
         out_ref[pl.ds(r, frames, stride=rows)] = p_c[r + own, REACH : REACH + frames]
 
 
+def on_chip(x):
+    return pltpu.with_memory_space_constraint(x, pltpu.VMEM)
+
+
 def body(observed, kernel):
     frames, rows, cols = observed.shape
     taps = kernel.shape[0]
@@ -216,9 +220,9 @@
     v, strip, edge = pl.pallas_call(
         blur_kernel,
         out_shape=(
-            jax.ShapeDtypeStruct((rows, deep, cols), f32),
-            jax.ShapeDtypeStruct((REACH, deep, cols), f32),
-            jax.ShapeDtypeStruct((deep, cols), f32),
+            pltpu.VMEM((rows, deep, cols), f32),
+            pltpu.VMEM((REACH, deep, cols), f32),
+            pltpu.VMEM((deep, cols), f32),
         ),
         in_specs=[vmem] * 4,
         out_specs=(vmem,) * 3,
@@ -230,7 +234,7 @@
             pltpu.VMEM((deep * rows, cols), f32),
         ],
         name="blur",
-    )(observed, near, far, kernel)
+    )(*map(on_chip, (observed, near, far, kernel)))
 
     strip = lax.ppermute(strip, "row", PAIR)
     side = lax.ppermute(edge, "col", PAIR)
@@ -252,7 +256,7 @@
             pltpu.VMEM((4, deep, cols), f32),
         ],
         name="tv",
-    )(v, strip, side, corner)
+    )(*map(on_chip, (v, strip, side, corner)))
     return out.reshape(frames, rows, cols)
 
 

time: 40.7 us -> 36.4 us (0.89)
  Pallas kernels: 9.57 us -> 6.75 us
  local copies, waits for them, and re-layouts: 2.42 us -> 1.08 us
    pallas_call x1, Pallas kernels: 3.99 us -> 2.18 us  [body(): pl.pallas_call(blur_kernel, out_shape=(pltpu.VMEM((rows, deep, cols), f32...]
    unnamed x10 -> x4, local copies, waits for them, and re-layouts: 1.42 us -> 0.01 us
    pallas_call x1, Pallas kernels: 5.59 us -> 4.56 us  [body(): pl.pallas_call(tv_kernel, out_shape=jax.ShapeDtypeStruct((frames * rows,...]
where the time goes in v2:
time: 36.4 us; the launch traced here: 36.1 us
  starting transfers between devices  23 us (63%)
  Pallas kernels  6.75 us (19%)
  waiting for transfers between devices  5.25 us (14%)
  local copies, waits for them, and re-layouts  1.08 us (3%)
    ppermute x1, starting transfers between devices, body(): lax.ppermute(far, 'tm', [(i, i + 1 if i % 2 else i - 1) for i in range(1,...  11.2 us
    ppermute x1, starting transfers between devices, body(): strip = lax.ppermute(strip, 'row', PAIR)  4.93 us
    pallas_call x1, Pallas kernels, body(): pl.pallas_call(tv_kernel, out_shape=jax.ShapeDtypeStruct((frames * rows,...  4.56 us
    ppermute x1, starting transfers between devices, body(): lax.ppermute(edge, ('row', 'col'), [(0, 3), (3, 0), (1, 2), (2, 1)])  3.05 us
    pallas_call x1, Pallas kernels, body(): pl.pallas_call(blur_kernel, out_shape=(pltpu.VMEM((rows, deep, cols), f32...  2.18 us
    ppermute x1, waiting for transfers between devices, body(): lax.ppermute(edge, ('row', 'col'), [(0, 3), (3, 0), (1, 2), (2, 1)])  2.07 us
    ppermute x1, starting transfers between devices, body(): near = lax.ppermute(near, 'tm', [(i, i ^ 1) for i in range(count)])  1.92 us
    ppermute x1, starting transfers between devices, body(): side = lax.ppermute(edge, 'col', PAIR)  1.92 us
  transfers between devices with their start and end apart: 5, of which 4 were waited for; matrix products, arithmetic and copies ran while one was open for 0% of the time, Pallas kernels for 0%

profile of v2, /device:TPU:56, one launch (start us, length us, event | category | flops | bytes accessed | tf_op | source)
XLA Modules:
  0.0 36.1 jit_solution(5054283825793809162)
XLA Ops:
  0.0 0.0 copy-start
  0.0 0.0 copy-start.1
  0.0 1.1 %constant_dynamic-slice_fusion = (f32[34,8,128]{2,1,0:T(8,128)S(1)}, f32[34,8,128]{2,1,0:T(8,128)S(1)}) fusion(f32[64,8,128]{2,1,0:T(8,128)} %u_ref.1, s32[]{:T(128)S(6)} %select_n.15, s32[]{:T(128)S(6)} %select_n.14), kind=kLoop, calls=%fused_computation | loop fusion | bytes 557064 | tf_op jit(solution)/shard_map/dynamic_slice | solution.py:216
  1.1 11.2 %collective-permute-start.1 = (f32[34,8,128]{2,1,0:T(8,128)S(1)}, f32[34,8,128]{2,1,0:T(8,128)S(1)}, u32[]{:S(2)}, u32[]{:S(2)}) collective-permute-start(f32[34,8,128]{2,1,0:T(8,128)S(1)} %get-tuple-element.11), channel_id=1, source_target_pairs={{4,8},{8,4},{12,16},{16,12},{20,24},{24,20},{28,32},{32,28},{36,40... | collective-permute-start | bytes 417800 | tf_op jit(solution)/shard_map/ppermute | solution.py:217
  12.3 1.9 %collective-permute-start = (f32[34,8,128]{2,1,0:T(8,128)S(1)}, f32[34,8,128]{2,1,0:T(8,128)S(1)}, u32[]{:S(2)}, u32[]{:S(2)}) collective-permute-start(f32[34,8,128]{2,1,0:T(8,128)S(1)} %get-tuple-element.12), channel_id=1, source_target_pairs={{0,4},{4,0},{8,12},{12,8},{16,20},{20,16},{24,28},{28,24},{32,36},... | collective-permute-start | bytes 417800 | tf_op jit(solution)/shard_map/ppermute | solution.py:218
  14.2 0.8 %collective-permute-done.1.far_ref = f32[34,8,128]{2,1,0:T(8,128)S(1)} collective-permute-done((f32[34,8,128]{2,1,0:T(8,128)S(1)}, f32[34,8,128]{2,1,0:T(8,128)S(1)}, u32[]{:S(2)}, u32[]{:S(2)}) %collective-permute-start.1) | collective-permute-done | bytes 139296 | tf_op jit(solution)/shard_map/ppermute | solution.py:217
  15.0 0.5 %collective-permute-done.near_ref = f32[34,8,128]{2,1,0:T(8,128)S(1)} collective-permute-done((f32[34,8,128]{2,1,0:T(8,128)S(1)}, f32[34,8,128]{2,1,0:T(8,128)S(1)}, u32[]{:S(2)}, u32[]{:S(2)}) %collective-permute-start) | collective-permute-done | bytes 139296 | tf_op jit(solution)/shard_map/ppermute | solution.py:218
  15.5 0.0 copy-done
  15.5 0.0 copy-done.1
  15.5 2.2 %blur.1 = (f32[8,72,128]{2,1,0:T(8,128)S(1)}, f32[2,72,128]{2,1,0:T(8,128)S(1)}, f32[72,128]{1,0:T(8,128)S(1)}) custom-call(f32[64,8,128]{2,1,0:T(8,128)S(1)} %copy-done, f32[34,8,128]{2,1,0:T(8,128)S(1)} %collective-permute-done.near_ref, f32[34,8,128]{2,1,0:T(8,128)S(1)} %collective-permute-done.1.far_ref, f32[33,8,128]{2,1,0:T(8,128)S(1)} %copy-done.1), custom_call_target="tpu_custom_call" | custom-call | tf_op jit(solution)/shard_map/blur/pallas_call | solution.py:220
  17.7 4.9 %collective-permute-start.2 = (f32[2,72,128]{2,1,0:T(8,128)S(1)}, f32[2,72,128]{2,1,0:T(8,128)S(1)}, u32[]{:S(2)}, u32[]{:S(2)}) collective-permute-start(f32[2,72,128]{2,1,0:T(8,128)S(1)} %get-tuple-element.9), channel_id=1, source_target_pairs={{0,2},{2,0},{1,3},{3,1},{4,6},{6,4},{5,7},{7,5},{8,10},{10,8},{9,1... | collective-permute-start | bytes 221192 | tf_op jit(solution)/shard_map/ppermute | solution.py:239
  22.6 3.1 %collective-permute-start.4 = (f32[72,128]{1,0:T(8,128)S(1)}, f32[72,128]{1,0:T(8,128)S(1)}, u32[]{:S(2)}, u32[]{:S(2)}) collective-permute-start(f32[72,128]{1,0:T(8,128)S(1)} %get-tuple-element.10), channel_id=1, source_target_pairs={{0,3},{3,0},{1,2},{2,1},{4,7},{7,4},{5,6},{6,5},{8,11},{11,8},{9,1... | collective-permute-start | bytes 110600 | tf_op jit(solution)/shard_map/ppermute | solution.py:241
  25.7 1.9 %collective-permute-start.3 = (f32[72,128]{1,0:T(8,128)S(1)}, f32[72,128]{1,0:T(8,128)S(1)}, u32[]{:S(2)}, u32[]{:S(2)}) collective-permute-start(f32[72,128]{1,0:T(8,128)S(1)} %get-tuple-element.10), channel_id=1, source_target_pairs={{0,1},{1,0},{2,3},{3,2},{4,5},{5,4},{6,7},{7,6},{8,9},{9,8},{10,11... | collective-permute-start | bytes 110600 | tf_op jit(solution)/shard_map/ppermute | solution.py:240
  27.6 2.1 %collective-permute-done.4.corner_ref = f32[72,128]{1,0:T(8,128)S(1)} collective-permute-done((f32[72,128]{1,0:T(8,128)S(1)}, f32[72,128]{1,0:T(8,128)S(1)}, u32[]{:S(2)}, u32[]{:S(2)}) %collective-permute-start.4) | collective-permute-done | bytes 36896 | tf_op jit(solution)/shard_map/ppermute | solution.py:241
  29.7 1.9 %collective-permute-done.3.side_ref = f32[72,128]{1,0:T(8,128)S(1)} collective-permute-done((f32[72,128]{1,0:T(8,128)S(1)}, f32[72,128]{1,0:T(8,128)S(1)}, u32[]{:S(2)}, u32[]{:S(2)}) %collective-permute-start.3) | collective-permute-done | bytes 36896 | tf_op jit(solution)/shard_map/ppermute | solution.py:240
  31.6 0.0 collective-permute-done.2.strip_ref
  31.6 4.6 %tv.1 = f32[512,128]{1,0:T(8,128)} custom-call(f32[8,72,128]{2,1,0:T(8,128)S(1)} %get-tuple-element.8.v_ref, f32[2,72,128]{2,1,0:T(8,128)S(1)} %collective-permute-done.2.strip_ref, f32[72,128]{1,0:T(8,128)S(1)} %collective-permute-done.3.side_ref, f32[72,128]{1,0:T(8,128)S(1)} %collective-permute-done.4.corner_ref), custom_call_target="tpu_custom_call" | custom-call | tf_op jit(solution)/shard_map/tv/pallas_call | solution.py:244
Async XLA Ops:
  0.0 15.5 %copy-start = (f32[64,8,128]{2,1,0:T(8,128)S(1)}, f32[64,8,128]{2,1,0:T(8,128)}, u32[]{:S(2)}) copy-start(f32[64,8,128]{2,1,0:T(8,128)} %u_ref.1) | copy-start | bytes 786436
  0.0 15.5 %copy-start.1 = (f32[33,8,128]{2,1,0:T(8,128)S(1)}, f32[33,8,128]{2,1,0:T(8,128)}, u32[]{:S(2)}) copy-start(f32[33,8,128]{2,1,0:T(8,128)} %kernel_ref.1) | copy-start | bytes 405508
  1.1 13.9 %collective-permute-start.1 = (f32[34,8,128]{2,1,0:T(8,128)S(1)}, f32[34,8,128]{2,1,0:T(8,128)S(1)}, u32[]{:S(2)}, u32[]{:S(2)}) collective-permute-start(f32[34,8,128]{2,1,0:T(8,128)S(1)} %get-tuple-element.11), channel_id=1, source_target_pairs={{4,8},{8,4},{12,16},{16,12},{20,24},{24,20},{28,32},{32,28},{36,40... | collective-permute-start | bytes 417800 | tf_op jit(solution)/shard_map/ppermute | solution.py:217
  12.3 3.3 %collective-permute-start = (f32[34,8,128]{2,1,0:T(8,128)S(1)}, f32[34,8,128]{2,1,0:T(8,128)S(1)}, u32[]{:S(2)}, u32[]{:S(2)}) collective-permute-start(f32[34,8,128]{2,1,0:T(8,128)S(1)} %get-tuple-element.12), channel_id=1, source_target_pairs={{0,4},{4,0},{8,12},{12,8},{16,20},{20,16},{24,28},{28,24},{32,36},... | collective-permute-start | bytes 417800 | tf_op jit(solution)/shard_map/ppermute | solution.py:218
  17.7 13.9 %collective-permute-start.2 = (f32[2,72,128]{2,1,0:T(8,128)S(1)}, f32[2,72,128]{2,1,0:T(8,128)S(1)}, u32[]{:S(2)}, u32[]{:S(2)}) collective-permute-start(f32[2,72,128]{2,1,0:T(8,128)S(1)} %get-tuple-element.9), channel_id=1, source_target_pairs={{0,2},{2,0},{1,3},{3,1},{4,6},{6,4},{5,7},{7,5},{8,10},{10,8},{9,1... | collective-permute-start | bytes 221192 | tf_op jit(solution)/shard_map/ppermute | solution.py:239
  22.6 7.1 %collective-permute-start.4 = (f32[72,128]{1,0:T(8,128)S(1)}, f32[72,128]{1,0:T(8,128)S(1)}, u32[]{:S(2)}, u32[]{:S(2)}) collective-permute-start(f32[72,128]{1,0:T(8,128)S(1)} %get-tuple-element.10), channel_id=1, source_target_pairs={{0,3},{3,0},{1,2},{2,1},{4,7},{7,4},{5,6},{6,5},{8,11},{11,8},{9,1... | collective-permute-start | bytes 110600 | tf_op jit(solution)/shard_map/ppermute | solution.py:241
  25.7 5.9 %collective-permute-start.3 = (f32[72,128]{1,0:T(8,128)S(1)}, f32[72,128]{1,0:T(8,128)S(1)}, u32[]{:S(2)}, u32[]{:S(2)}) collective-permute-start(f32[72,128]{1,0:T(8,128)S(1)} %get-tuple-element.10), channel_id=1, source_target_pairs={{0,1},{1,0},{2,3},{3,2},{4,5},{5,4},{6,7},{7,6},{8,9},{9,8},{10,11... | collective-permute-start | bytes 110600 | tf_op jit(solution)/shard_map/ppermute | solution.py:240

commit v3 on v2

--- a/solution.py
+++ b/solution.py
@@ -11,10 +11,9 @@
 
 REACH = 2
 BLOCK = 10
-PAIR = ((0, 1), (1, 0))
-
-
-def blur_kernel(u_ref, near_ref, far_ref, kernel_ref, v_ref, strip_ref, edge_ref, upad, fwd, adj, q, vflat):
+
+
+def blur_kernel(u_ref, near_ref, far_ref, kernel_ref, v_ref, message_ref, upad, fwd, adj, q, vflat):
     tm, row, col = lax.axis_index("tm"), lax.axis_index("row"), lax.axis_index("col")
     frames, rows, cols = u_ref.shape
     taps = kernel_ref.shape[0]
@@ -92,10 +91,13 @@
         moved = pltpu.roll(plane, first + 2, axis=1)
         low = first + 2 * col
         edge = jnp.where((lane >= low) & (lane < low + 2), moved, edge)
-    edge_ref[...] = edge
-    begin = (rows - 2) * (1 - row)
-    strip_ref[0] = v_ref[begin]
-    strip_ref[1] = v_ref[begin + 1]
+    third = deep // 3
+    packed = edge[:third] + pltpu.roll(edge[third : 2 * third], 40, axis=1) + pltpu.roll(edge[2 * third :], 80, axis=1)
+    message_ref[2 * row + (1 - col), :third] = packed
+    message_ref[2 * (1 - row) + (1 - col), :third] = packed
+    begin = (rows - REACH) * (1 - row)
+    for i in range(REACH):
+        message_ref[2 * (1 - row) + col, i * deep : (i + 1) * deep] = v_ref[begin + i]
 
 
 def unit(z_t, z_r, z_c):
@@ -103,7 +105,13 @@
     return z_t * factor, z_r * factor, z_c * factor
 
 
-def tv_kernel(v_ref, strip_ref, side_ref, corner_ref, out_ref, w, p_t, p_r, p_c, e_w, e_t, e_c):
+def unpacked(packed):
+    lane = lax.broadcasted_iota(jnp.int32, packed.shape, 1)
+    parts = [packed, pltpu.roll(packed, 88, axis=1), pltpu.roll(packed, 48, axis=1)]
+    return jnp.concatenate([jnp.where(lane < 40, part, 0.0) for part in parts], axis=0)
+
+
+def tv_kernel(v_ref, got_ref, out_ref, w, p_t, p_r, p_c, e_w, e_t, e_c):
     tm, row, col = lax.axis_index("tm"), lax.axis_index("row"), lax.axis_index("col")
     rows, deep, cols = v_ref.shape
     frames = out_ref.shape[0] // rows
@@ -125,12 +133,12 @@
     for r in range(rows):
         w[r + own, :deep] = v_ref[r] * scale
     for i in range(REACH):
-        w[foreign + i, :deep] = strip_ref[i] * scale
+        w[foreign + i, :deep] = got_ref[2 * (1 - row) + col, i * deep : (i + 1) * deep] * scale
     w[wide, :deep] = w[wide - 1, :deep]
 
     low = 4 * foreign
-    corner = pltpu.roll(corner_ref[...], jnp.where(row == 0, 24, cols - 24), axis=1)
-    edge = side_ref[...] + jnp.where((lane >= low) & (lane < low + 8), corner, 0.0)
+    corner = pltpu.roll(unpacked(got_ref[2 * (1 - row) + (1 - col), : deep // 3]), jnp.where(row == 0, 24, cols - 24), axis=1)
+    edge = unpacked(got_ref[2 * row + (1 - col), : deep // 3]) + jnp.where((lane >= low) & (lane < low + 8), corner, 0.0)
     edge = edge * scale
     for r in range(wide):
         moved = pltpu.roll(w[r, :deep], 4 * r + 2, axis=1)
@@ -174,23 +182,23 @@
 
     p_r[0] = jnp.zeros((deep, cols), jnp.float32)
 
-    def first_pass(r, carry):
+    def first_pass(r):
         store(r, unit(*slopes(r, 0)))
-        return carry
-
-    def second_w(r, carry):
+
+    def second_w(r):
         w[r, :deep] = divergence(r, 1) * inner_step + w[r, :deep]
-        return carry
-
-    def second_pass(r, carry):
+
+    def second_pass(r):
         g_t, g_r, g_c = slopes(r, 2)
         store(r, unit(p_t[r, 8 : deep + 8] + g_t, p_r[r + 1] + g_r, p_c[r] + g_c))
-        return carry
-
-    lax.fori_loop(0, wide, first_pass, 0)
-    lax.fori_loop(0, wide, second_w, 0)
+
+    for r in range(wide):
+        first_pass(r)
+    for r in range(wide):
+        second_w(r)
     w[wide, :deep] = w[wide - 1, :deep]
-    lax.fori_loop(0, wide, second_pass, 0)
+    for r in range(wide):
+        second_pass(r)
     for r in range(rows):
         updated = v_ref[r] - theta * divergence(r + own, 3)
         p_c[r + own] = updated
@@ -199,6 +207,10 @@
 
 def on_chip(x):
     return pltpu.with_memory_space_constraint(x, pltpu.VMEM)
+
+
+def on_chip_result(shape):
+    return pltpu.VMEM(shape, jnp.float32)
 
 
 def body(observed, kernel):
@@ -217,15 +229,14 @@
     far = lax.ppermute(far, "tm", [(i, i + 1 if i % 2 else i - 1) for i in range(1, count - 1)])
     near = lax.ppermute(near, "tm", [(i, i ^ 1) for i in range(count)])
 
-    v, strip, edge = pl.pallas_call(
+    v, message = pl.pallas_call(
         blur_kernel,
         out_shape=(
-            pltpu.VMEM((rows, deep, cols), f32),
-            pltpu.VMEM((REACH, deep, cols), f32),
-            pltpu.VMEM((deep, cols), f32),
+            on_chip_result((rows, deep, cols)),
+            on_chip_result((4, REACH * deep, cols)),
         ),
         in_specs=[vmem] * 4,
-        out_specs=(vmem,) * 3,
+        out_specs=(vmem,) * 2,
         scratch_shapes=[
             pltpu.VMEM((frames + 2 * halo, rows, cols), f32),
             pltpu.VMEM((taps, rows, cols), f32),
@@ -236,15 +247,13 @@
         name="blur",
     )(*map(on_chip, (observed, near, far, kernel)))
 
-    strip = lax.ppermute(strip, "row", PAIR)
-    side = lax.ppermute(edge, "col", PAIR)
-    corner = lax.ppermute(edge, ("row", "col"), [(0, 3), (3, 0), (1, 2), (2, 1)])
+    got = lax.all_to_all(message, ("row", "col"), 0, 0, tiled=True)
 
     wide = rows + REACH
     out = pl.pallas_call(
         tv_kernel,
         out_shape=jax.ShapeDtypeStruct((frames * rows, cols), f32),
-        in_specs=[vmem] * 4,
+        in_specs=[vmem] * 2,
         out_specs=vmem,
         scratch_shapes=[
             pltpu.VMEM((wide + 1, deep + 8, cols), f32),
@@ -256,7 +265,7 @@
             pltpu.VMEM((4, deep, cols), f32),
         ],
         name="tv",
-    )(*map(on_chip, (v, strip, side, corner)))
+    )(*map(on_chip, (v, got)))
     return out.reshape(frames, rows, cols)
 
 

time: 36.4 us -> 31.3 us (0.86)
  blocking collectives: 0 us -> 11.4 us
  starting transfers between devices: 23 us -> 13.1 us
  waiting for transfers between devices: 5.25 us -> 1.32 us
  Pallas kernels: 6.75 us -> 4.22 us
    all_to_all x0 -> x1, blocking collectives: none -> 11.4 us  [body(): got = lax.all_to_all(message, ('row', 'col'), 0, 0, tiled=True)]
    ppermute x3 -> x0, starting transfers between devices: 9.9 us -> none  [the longest x1 4.93 us: body(): strip = lax.ppermute(strip, 'row', PAIR)]
    ppermute x3 -> x0, waiting for transfers between devices: 3.93 us -> none  [the longest x1 2.07 us: body(): lax.ppermute(edge, ('row', 'col'), [(0, 3), (3, 0), (1, 2), (2, 1)])]
    pallas_call x1, Pallas kernels: 4.56 us -> 2.01 us  [body(): pl.pallas_call(tv_kernel, out_shape=jax.ShapeDtypeStruct((frames * rows,...]
  transfers between devices with their start and end apart: 5 -> 2, of which waited for: 4 -> 2; matrix products, arithmetic and copies ran while one was open for 0% -> 0% of each run, Pallas kernels for 0% -> 0%
where the time goes in v3:
time: 31.3 us; the launch traced here: 31.2 us
  starting transfers between devices  13.1 us (42%)
  blocking collectives  11.4 us (36%)
  Pallas kernels  4.22 us (13%)
  waiting for transfers between devices  1.32 us (4%)
  local copies, waits for them, and re-layouts  1.08 us (3%)
    all_to_all x1, blocking collectives, body(): got = lax.all_to_all(message, ('row', 'col'), 0, 0, tiled=True)  11.4 us
    ppermute x1, starting transfers between devices, body(): lax.ppermute(far, 'tm', [(i, i + 1 if i % 2 else i - 1) for i in range(1,...  11.2 us
    pallas_call x1, Pallas kernels, body(): pl.pallas_call(blur_kernel, out_shape=(on_chip_result((rows, deep, cols))...  2.21 us
    pallas_call x1, Pallas kernels, body(): pl.pallas_call(tv_kernel, out_shape=jax.ShapeDtypeStruct((frames * rows,...  2.01 us
    ppermute x1, starting transfers between devices, body(): near = lax.ppermute(near, 'tm', [(i, i ^ 1) for i in range(count)])  1.92 us
    dynamic_slice x1, local copies, waits for them, and re-layouts, body(): lax.dynamic_slice_in_dim(observed, odd * (frames - halo), halo, axis=0)  1.07 us
    ppermute x1, waiting for transfers between devices, body(): lax.ppermute(far, 'tm', [(i, i + 1 if i % 2 else i - 1) for i in range(1,...  0.8 us
  transfers between devices with their start and end apart: 2, of which 2 were waited for; matrix products, arithmetic and copies ran while one was open for 0% of the time, Pallas kernels for 0%

profile of v3, /device:TPU:56, one launch (start us, length us, event | category | flops | bytes accessed | tf_op | source)
XLA Modules:
  0.0 31.2 jit_solution(8969829482306369988)
XLA Ops:
  0.0 0.0 copy-start
  0.0 0.0 copy-start.1
  0.0 1.1 %constant_dynamic-slice_fusion = (f32[34,8,128]{2,1,0:T(8,128)S(1)}, f32[34,8,128]{2,1,0:T(8,128)S(1)}) fusion(f32[64,8,128]{2,1,0:T(8,128)} %u_ref.1, s32[]{:T(128)S(6)} %select_n.15, s32[]{:T(128)S(6)} %select_n.14), kind=kLoop, calls=%fused_computation | loop fusion | bytes 557064 | tf_op jit(solution)/shard_map/dynamic_slice | solution.py:228
  1.1 11.2 %collective-permute-start.1 = (f32[34,8,128]{2,1,0:T(8,128)S(1)}, f32[34,8,128]{2,1,0:T(8,128)S(1)}, u32[]{:S(2)}, u32[]{:S(2)}) collective-permute-start(f32[34,8,128]{2,1,0:T(8,128)S(1)} %get-tuple-element.9), channel_id=1, source_target_pairs={{4,8},{8,4},{12,16},{16,12},{20,24},{24,20},{28,32},{32,28},{36,40... | collective-permute-start | bytes 417800 | tf_op jit(solution)/shard_map/ppermute | solution.py:229
  12.3 1.9 %collective-permute-start = (f32[34,8,128]{2,1,0:T(8,128)S(1)}, f32[34,8,128]{2,1,0:T(8,128)S(1)}, u32[]{:S(2)}, u32[]{:S(2)}) collective-permute-start(f32[34,8,128]{2,1,0:T(8,128)S(1)} %get-tuple-element.10), channel_id=1, source_target_pairs={{0,4},{4,0},{8,12},{12,8},{16,20},{20,16},{24,28},{28,24},{32,36},... | collective-permute-start | bytes 417800 | tf_op jit(solution)/shard_map/ppermute | solution.py:230
  14.2 0.8 %collective-permute-done.1.far_ref = f32[34,8,128]{2,1,0:T(8,128)S(1)} collective-permute-done((f32[34,8,128]{2,1,0:T(8,128)S(1)}, f32[34,8,128]{2,1,0:T(8,128)S(1)}, u32[]{:S(2)}, u32[]{:S(2)}) %collective-permute-start.1) | collective-permute-done | bytes 139296 | tf_op jit(solution)/shard_map/ppermute | solution.py:229
  15.0 0.5 %collective-permute-done.near_ref = f32[34,8,128]{2,1,0:T(8,128)S(1)} collective-permute-done((f32[34,8,128]{2,1,0:T(8,128)S(1)}, f32[34,8,128]{2,1,0:T(8,128)S(1)}, u32[]{:S(2)}, u32[]{:S(2)}) %collective-permute-start) | collective-permute-done | bytes 139296 | tf_op jit(solution)/shard_map/ppermute | solution.py:230
  15.5 0.0 copy-done
  15.5 0.0 copy-done.1
  15.5 2.2 %blur.1 = (f32[8,72,128]{2,1,0:T(8,128)S(1)}, f32[4,144,128]{2,1,0:T(8,128)S(1)}) custom-call(f32[64,8,128]{2,1,0:T(8,128)S(1)} %copy-done, f32[34,8,128]{2,1,0:T(8,128)S(1)} %collective-permute-done.near_ref, f32[34,8,128]{2,1,0:T(8,128)S(1)} %collective-permute-done.1.far_ref, f32[33,8,128]{2,1,0:T(8,128)S(1)} %copy-done.1), custom_call_target="tpu_custom_call" | custom-call | tf_op jit(solution)/shard_map/blur/pallas_call | solution.py:232
  17.7 11.4 %all_to_all.5.got_ref = f32[4,144,128]{2,1,0:T(8,128)S(1)} all-to-all(f32[4,144,128]{2,1,0:T(8,128)S(1)} %get-tuple-element.8), channel_id=1, replica_groups=mesh['tm'=128,'row'=2,'col'=2] {'row','col'}, dimensions={0} | all-to-all | bytes 589824 | tf_op jit(solution)/shard_map/all_to_all | solution.py:250
  29.1 2.0 %tv.1 = f32[512,128]{1,0:T(8,128)} custom-call(f32[8,72,128]{2,1,0:T(8,128)S(1)} %get-tuple-element.7.v_ref, f32[4,144,128]{2,1,0:T(8,128)S(1)} %all_to_all.5.got_ref), custom_call_target="tpu_custom_call" | custom-call | tf_op jit(solution)/shard_map/tv/pallas_call | solution.py:253
Async XLA Ops:
  0.0 15.5 %copy-start = (f32[64,8,128]{2,1,0:T(8,128)S(1)}, f32[64,8,128]{2,1,0:T(8,128)}, u32[]{:S(2)}) copy-start(f32[64,8,128]{2,1,0:T(8,128)} %u_ref.1) | copy-start | bytes 786436
  0.0 15.5 %copy-start.1 = (f32[33,8,128]{2,1,0:T(8,128)S(1)}, f32[33,8,128]{2,1,0:T(8,128)}, u32[]{:S(2)}) copy-start(f32[33,8,128]{2,1,0:T(8,128)} %kernel_ref.1) | copy-start | bytes 405508
  1.1 13.9 %collective-permute-start.1 = (f32[34,8,128]{2,1,0:T(8,128)S(1)}, f32[34,8,128]{2,1,0:T(8,128)S(1)}, u32[]{:S(2)}, u32[]{:S(2)}) collective-permute-start(f32[34,8,128]{2,1,0:T(8,128)S(1)} %get-tuple-element.9), channel_id=1, source_target_pairs={{4,8},{8,4},{12,16},{16,12},{20,24},{24,20},{28,32},{32,28},{36,40... | collective-permute-start | bytes 417800 | tf_op jit(solution)/shard_map/ppermute | solution.py:229
  12.3 3.3 %collective-permute-start = (f32[34,8,128]{2,1,0:T(8,128)S(1)}, f32[34,8,128]{2,1,0:T(8,128)S(1)}, u32[]{:S(2)}, u32[]{:S(2)}) collective-permute-start(f32[34,8,128]{2,1,0:T(8,128)S(1)} %get-tuple-element.10), channel_id=1, source_target_pairs={{0,4},{4,0},{8,12},{12,8},{16,20},{20,16},{24,28},{28,24},{32,36},... | collective-permute-start | bytes 417800 | tf_op jit(solution)/shard_map/ppermute | solution.py:230

commit v4 on v3

--- a/solution.py
+++ b/solution.py
@@ -13,91 +13,187 @@
 BLOCK = 10
 
 
-def blur_kernel(u_ref, near_ref, far_ref, kernel_ref, v_ref, message_ref, upad, fwd, adj, q, vflat):
+def edge_lanes(planes, row, col):
+    edge = jnp.zeros_like(planes[0])
+    lane = lax.broadcasted_iota(jnp.int32, edge.shape, 1)
+    for r, plane in enumerate(planes):
+        first = 4 * (r + REACH * row)
+        low = first + 2 * col
+        edge = jnp.where((lane >= low) & (lane < low + 2), pltpu.roll(plane, first + 2, axis=1), edge)
+    return edge
+
+
+def border(ref, count, rows, row, col):
+    begin = (rows - REACH) * (1 - row)
+    planes = [ref[pl.ds(r, count, stride=rows)] for r in range(rows)]
+    strips = [ref[pl.ds(begin + i, count, stride=rows)] for i in range(REACH)]
+    return strips + [edge_lanes(planes, row, col)]
+
+
+def weights_kernel(u_ref, kernel_ref, fwd_ref, adj_ref, border_u, border_fwd, border_adj):
+    row, col = lax.axis_index("row"), lax.axis_index("col")
+    frames, cols = border_u.shape[1:]
+    rows = u_ref.shape[0] // frames
+    taps = kernel_ref.shape[0] // rows
+    half = taps // 2
+    third = 1.0 / 3.0
+    total = kernel_ref[pl.ds(0, rows)]
+    for tap in range(1, taps):
+        total = total + kernel_ref[pl.ds(tap * rows, rows)]
+    inverse = 1.0 / total
+    for tap in range(taps):
+        share = kernel_ref[pl.ds(tap * rows, rows)] * inverse
+        adj_ref[pl.ds(tap * rows, rows)] = share
+        fwd_ref[pl.ds(tap * rows, rows)] = (share - 1.0 if tap == half else share) * third
+    center = jnp.where(lax.broadcasted_iota(jnp.int32, (taps, cols), 0) == half, third, 0.0)
+    for i, plane in enumerate(border(adj_ref, taps, rows, row, col)):
+        border_adj[i, :taps] = plane
+        border_fwd[i, :taps] = plane * third - center
+    for i, plane in enumerate(border(u_ref, frames, rows, row, col)):
+        border_u[i] = plane
+
+
+def border_kernel(near_ref, far_ref, border_u, border_fwd, border_adj, message_ref, u, q, v, packed, sems):
     tm, row, col = lax.axis_index("tm"), lax.axis_index("row"), lax.axis_index("col")
-    frames, rows, cols = u_ref.shape
-    taps = kernel_ref.shape[0]
+    planes, frames, cols = border_u.shape
+    taps = 2 * (q.shape[1] - v.shape[1]) // 2 + 1
+    half = taps // 2
+    halo = 2 * half + REACH
+    rows = near_ref.shape[0] // halo
+    deep = v.shape[1]
+    length = q.shape[1]
+
+    odd = lax.rem(tm, 2) == 1
+    near = border(near_ref, halo, rows, row, col)
+    far = border(far_ref, halo, rows, row, col)
+    for i in range(planes):
+        u[i, :halo] = jnp.where(odd, near[i], far[i])
+        u[i, halo : halo + frames] = border_u[i]
+        u[i, halo + frames : frames + 2 * halo] = jnp.where(odd, far[i], near[i])
+        u[i, frames + 2 * halo :] = jnp.zeros((u.shape[1] - frames - 2 * halo, cols), jnp.float32)
+
+    def forward(i):
+        acc = [None] * (length // 8)
+        for tap in range(taps):
+            weight = jnp.broadcast_to(border_fwd[i, tap : tap + 1], (8, cols))
+            for c in range(length // 8):
+                term = weight * u[i, 8 * c + tap : 8 * c + tap + 8]
+                acc[c] = term if tap == 0 else acc[c] + term
+        for c in range(length // 8):
+            q[i, 8 * c : 8 * c + 8] = acc[c]
+
+    def close(begin, end):
+        nothing = jnp.zeros((end - begin, half + REACH, cols), jnp.float32)
+
+        @pl.when(tm == 0)
+        def _():
+            q[begin:end, : half + REACH] = nothing
+
+        @pl.when(tm == lax.axis_size("tm") - 1)
+        def _():
+            q[begin:end, q_count - half - REACH : q_count] = nothing
+
+    def adjoint(i):
+        acc = [None] * (deep // 8)
+        for tap in range(taps):
+            weight = jnp.broadcast_to(border_adj[i, tap : tap + 1], (8, cols))
+            for c in range(deep // 8):
+                at = 8 * c + 2 * half - tap
+                term = weight * q[i, at : at + 8]
+                acc[c] = term if tap == 0 else acc[c] + term
+        for c in range(deep // 8):
+            v[i, 8 * c : 8 * c + 8] = u[i, 8 * c + 2 * half : 8 * c + 2 * half + 8] - acc[c]
+
+    q_count = frames + 2 * (half + REACH)
+    across, beside, corner = 2 * (1 - row) + col, 2 * row + (1 - col), 2 * (1 - row) + (1 - col)
+    third = deep // 3
+    copies = [
+        pltpu.make_async_copy(v.at[0], message_ref.at[across, pl.ds(0, deep)], sems.at[0]),
+        pltpu.make_async_copy(v.at[1], message_ref.at[across, pl.ds(deep, deep)], sems.at[1]),
+        pltpu.make_async_copy(packed, message_ref.at[beside, pl.ds(0, third)], sems.at[2]),
+        pltpu.make_async_copy(packed, message_ref.at[corner, pl.ds(0, third)], sems.at[3]),
+    ]
+    for i in range(REACH):
+        forward(i)
+    close(0, REACH)
+    for i in range(REACH):
+        adjoint(i)
+        copies[i].start()
+    forward(REACH)
+    close(REACH, planes)
+    adjoint(REACH)
+    edge = v[REACH]
+    packed[...] = edge[:third] + pltpu.roll(edge[third : 2 * third], 40, axis=1) + pltpu.roll(edge[2 * third :], 80, axis=1)
+    copies[2].start()
+    copies[3].start()
+    for copy in copies:
+        copy.wait()
+
+
+def blur_kernel(u_ref, near_ref, far_ref, fwd, adj, v_ref, upad, q, vflat):
+    tm = lax.axis_index("tm")
+    rows, deep, cols = v_ref.shape
+    taps = fwd.shape[0] // rows
+    frames = u_ref.shape[0] // rows
     half = taps // 2
     halo = 2 * half + REACH
     span = frames + 2 * REACH
-    deep = v_ref.shape[1]
+
+    def at(frame, count=1):
+        return pl.ds(pl.multiple_of(frame * rows, rows), count * rows)
 
     odd = lax.rem(tm, 2)
-    upad[halo : halo + frames] = u_ref[...]
-    upad[pl.ds((1 - odd) * (halo + frames), halo)] = near_ref[...]
-    upad[pl.ds(odd * (halo + frames), halo)] = far_ref[...]
-
-    total = kernel_ref[0]
-    for tap in range(1, taps):
-        total = total + kernel_ref[tap]
-    inverse = 1.0 / total
-    for tap in range(taps):
-        share = kernel_ref[tap] * inverse
-        adj[tap] = share
-        fwd[tap] = (share - 1.0 if tap == half else share) * (1.0 / 3.0)
+    upad[at(halo, frames)] = u_ref[...]
+    upad[at((1 - odd) * (halo + frames), halo)] = near_ref[...]
+    upad[at(odd * (halo + frames), halo)] = far_ref[...]
 
     q_count = frames + 2 * (half + REACH)
 
     def forward(step, carry):
         base = step * BLOCK
-        window = [upad[base + i] for i in range(BLOCK + taps - 1)]
+        window = [upad[at(base + i)] for i in range(BLOCK + taps - 1)]
         acc = [None] * BLOCK
         for tap in range(taps):
-            weight = fwd[tap]
+            weight = fwd[at(tap)]
             for i in range(BLOCK):
                 term = weight * window[i + tap]
                 acc[i] = term if tap == 0 else acc[i] + term
         for i in range(BLOCK):
-            q[base + i] = acc[i]
+            q[at(base + i)] = acc[i]
         return carry
 
     lax.fori_loop(0, q_count // BLOCK, forward, 0)
-    nothing = jnp.zeros((half + REACH, rows, cols), jnp.float32)
+    nothing = jnp.zeros(((half + REACH) * rows, cols), jnp.float32)
 
     @pl.when(tm == 0)
     def _():
-        q[: half + REACH] = nothing
+        q[at(0, half + REACH)] = nothing
 
     @pl.when(tm == lax.axis_size("tm") - 1)
     def _():
-        q[q_count - half - REACH : q_count] = nothing
-
-    q[q_count:] = jnp.zeros((q.shape[0] - q_count, rows, cols), jnp.float32)
+        q[at(q_count - half - REACH, half + REACH)] = nothing
+
+    q[q_count * rows :] = jnp.zeros((q.shape[0] - q_count * rows, cols), jnp.float32)
 
     def adjoint(step, carry):
         base = step * BLOCK
-        window = [q[base + i] for i in range(BLOCK + taps - 1)]
+        window = [q[at(base + i)] for i in range(BLOCK + taps - 1)]
         acc = [None] * BLOCK
         for tap in range(taps):
-            weight = adj[tap]
+            weight = adj[at(tap)]
             for i in range(BLOCK):
                 term = weight * window[i + taps - 1 - tap]
                 acc[i] = term if tap == 0 else acc[i] + term
         for i in range(BLOCK):
-            at = pl.multiple_of((base + i) * rows, rows)
-            vflat[pl.ds(at, rows)] = upad[base + i + 2 * half] - acc[i]
+            vflat[at(base + i)] = upad[at(base + i + 2 * half)] - acc[i]
         return carry
 
     steps = -(-span // BLOCK)
     lax.fori_loop(0, steps, adjoint, 0)
     vflat[steps * BLOCK * rows :] = jnp.zeros((vflat.shape[0] - steps * BLOCK * rows, cols), jnp.float32)
 
-    lane = lax.broadcasted_iota(jnp.int32, (deep, cols), 1)
-    edge = jnp.zeros((deep, cols), jnp.float32)
     for r in range(rows):
-        plane = vflat[pl.ds(r, deep, stride=rows)]
-        v_ref[r] = plane
-        first = 4 * (r + 2 * row)
-        moved = pltpu.roll(plane, first + 2, axis=1)
-        low = first + 2 * col
-        edge = jnp.where((lane >= low) & (lane < low + 2), moved, edge)
-    third = deep // 3
-    packed = edge[:third] + pltpu.roll(edge[third : 2 * third], 40, axis=1) + pltpu.roll(edge[2 * third :], 80, axis=1)
-    message_ref[2 * row + (1 - col), :third] = packed
-    message_ref[2 * (1 - row) + (1 - col), :third] = packed
-    begin = (rows - REACH) * (1 - row)
-    for i in range(REACH):
-        message_ref[2 * (1 - row) + col, i * deep : (i + 1) * deep] = v_ref[begin + i]
+        v_ref[r] = vflat[pl.ds(r, deep, stride=rows)]
 
 
 def unit(z_t, z_r, z_c):
@@ -224,29 +320,58 @@
     vmem = pl.BlockSpec(memory_space=pltpu.VMEM)
     f32 = jnp.float32
 
-    near = lax.dynamic_slice_in_dim(observed, (1 - odd) * (frames - halo), halo, axis=0)
-    far = lax.dynamic_slice_in_dim(observed, odd * (frames - halo), halo, axis=0)
+    near = lax.dynamic_slice_in_dim(observed, (1 - odd) * (frames - halo), halo, axis=0).reshape(halo * rows, cols)
+    far = lax.dynamic_slice_in_dim(observed, odd * (frames - halo), halo, axis=0).reshape(halo * rows, cols)
     far = lax.ppermute(far, "tm", [(i, i + 1 if i % 2 else i - 1) for i in range(1, count - 1)])
     near = lax.ppermute(near, "tm", [(i, i ^ 1) for i in range(count)])
-
-    v, message = pl.pallas_call(
+    near, far = on_chip(near), on_chip(far)
+    mine = on_chip(observed.reshape(frames * rows, cols))
+
+    planes = REACH + 1
+    padded_taps = -(-taps // 8) * 8
+    fwd, adj, border_u, border_fwd, border_adj = pl.pallas_call(
+        weights_kernel,
+        out_shape=(
+            on_chip_result((taps * rows, cols)),
+            on_chip_result((taps * rows, cols)),
+            on_chip_result((planes, frames, cols)),
+            on_chip_result((planes, padded_taps, cols)),
+            on_chip_result((planes, padded_taps, cols)),
+        ),
+        in_specs=[vmem] * 2,
+        out_specs=(vmem,) * 5,
+        name="weights",
+    )(mine, on_chip(kernel.reshape(taps * rows, cols)))
+    fwd, adj, border_u, border_fwd, border_adj = map(on_chip, (fwd, adj, border_u, border_fwd, border_adj))
+
+    length = deep + 2 * half
+    message = pl.pallas_call(
+        border_kernel,
+        out_shape=jax.ShapeDtypeStruct((4, REACH * deep, cols), f32),
+        in_specs=[vmem] * 5,
+        out_specs=pl.BlockSpec(memory_space=pl.ANY),
+        scratch_shapes=[
+            pltpu.VMEM((planes, length + 2 * half, cols), f32),
+            pltpu.VMEM((planes, length, cols), f32),
+            pltpu.VMEM((planes, deep, cols), f32),
+            pltpu.VMEM((deep // 3, cols), f32),
+            pltpu.SemaphoreType.DMA((4,)),
+        ],
+        name="border",
+    )(near, far, border_u, border_fwd, border_adj)
+    v = pl.pallas_call(
         blur_kernel,
-        out_shape=(
-            on_chip_result((rows, deep, cols)),
-            on_chip_result((4, REACH * deep, cols)),
-        ),
-        in_specs=[vmem] * 4,
-        out_specs=(vmem,) * 2,
+        out_shape=on_chip_result((rows, deep, cols)),
+        in_specs=[vmem] * 5,
+        out_specs=vmem,
         scratch_shapes=[
-            pltpu.VMEM((frames + 2 * halo, rows, cols), f32),
-            pltpu.VMEM((taps, rows, cols), f32),
-            pltpu.VMEM((taps, rows, cols), f32),
-            pltpu.VMEM((deep + 2 * half, rows, cols), f32),
+            pltpu.VMEM(((frames + 2 * halo) * rows, cols), f32),
+            pltpu.VMEM(((deep + 2 * half) * rows, cols), f32),
             pltpu.VMEM((deep * rows, cols), f32),
         ],
+        cost_estimate=pl.CostEstimate(flops=2 * taps * (2 * deep + 2 * half) * rows * cols, bytes_accessed=0, transcendentals=0),
         name="blur",
-    )(*map(on_chip, (observed, near, far, kernel)))
-
+    )(mine, near, far, fwd, adj)
     got = lax.all_to_all(message, ("row", "col"), 0, 0, tiled=True)
 
     wide = rows + REACH

time: 31.3 us -> 31 us (level)
  blocking collectives: 11.4 us -> 0 us
  waiting for transfers between devices: 1.32 us -> 6.31 us
  starting transfers between devices: 13.1 us -> 17.4 us
  Pallas kernels: 4.22 us -> 5.95 us
    all_to_all x1 -> x0, blocking collectives: 11.4 us -> none  [body(): got = lax.all_to_all(message, ('row', 'col'), 0, 0, tiled=True)]
    all_to_all x0 -> x1, waiting for transfers between devices: none -> 5.24 us  [body(): got = lax.all_to_all(message, ('row', 'col'), 0, 0, tiled=True)]
    all_to_all x0 -> x1, starting transfers between devices: none -> 4.3 us  [body(): got = lax.all_to_all(message, ('row', 'col'), 0, 0, tiled=True)]
    pallas_call x1 -> x3, Pallas kernels: 2.21 us -> 3.95 us  [the longest x1 2.08 us: body(): pl.pallas_call(blur_kernel, out_shape=on_chip_result((rows, deep, cols)),...]
    dynamic_slice x1 -> x0, local copies, waits for them, and re-layouts: 1.07 us -> none  [body(): lax.dynamic_slice_in_dim(observed, odd * (frames - halo), halo, axis=0)]
    reshape x0 -> x1, local copies, waits for them, and re-layouts: none -> 1.07 us  [body(): lax.dynamic_slice_in_dim(observed, odd * (frames - halo), halo, axis=0)]
  transfers between devices with their start and end apart: 2 -> 3, of which waited for: 2 -> 3; matrix products, arithmetic and copies ran while one was open for 0% -> 0% of each run, Pallas kernels for 0% -> 8%
where the time goes in v4:
time: 31 us; the launch traced here: 30.8 us
  starting transfers between devices  17.4 us (56%)
  waiting for transfers between devices  6.31 us (20%)
  Pallas kernels  5.95 us (19%)
  local copies, waits for them, and re-layouts  1.08 us (3%)
    ppermute x1, starting transfers between devices, body(): lax.ppermute(far, 'tm', [(i, i + 1 if i % 2 else i - 1) for i in range(1,...  11.2 us
    all_to_all x1, waiting for transfers between devices, body(): got = lax.all_to_all(message, ('row', 'col'), 0, 0, tiled=True)  5.24 us
    all_to_all x1, starting transfers between devices, body(): got = lax.all_to_all(message, ('row', 'col'), 0, 0, tiled=True)  4.3 us
    pallas_call x1, Pallas kernels, body(): pl.pallas_call(blur_kernel, out_shape=on_chip_result((rows, deep, cols)),...  2.08 us
    pallas_call x1, Pallas kernels, body(): pl.pallas_call(tv_kernel, out_shape=jax.ShapeDtypeStruct((frames * rows,...  2 us
    ppermute x1, starting transfers between devices, body(): near = lax.ppermute(near, 'tm', [(i, i ^ 1) for i in range(count)])  1.92 us
    pallas_call x1, Pallas kernels, body(): pl.pallas_call(border_kernel, out_shape=jax.ShapeDtypeStruct((4, REACH *...  1.64 us
    reshape x1, local copies, waits for them, and re-layouts, body(): lax.dynamic_slice_in_dim(observed, odd * (frames - halo), halo, axis=0)  1.07 us
  transfers between devices with their start and end apart: 3, of which 3 were waited for; matrix products, arithmetic and copies ran while one was open for 0% of the time, Pallas kernels for 8%

profile of v4, /device:TPU:56, one launch (start us, length us, event | category | flops | bytes accessed | tf_op | source)
XLA Modules:
  0.0 30.8 jit_solution(11927604838451166443)
XLA Ops:
  0.0 0.0 copy-start
  0.0 0.0 copy-start.1
  0.0 1.1 %dynamic-slice_bitcast_fusion = (f32[272,128]{1,0:T(8,128)S(1)}, f32[272,128]{1,0:T(8,128)S(1)}) fusion(f32[64,8,128]{2,1,0:T(8,128)} %param.2, s32[]{:T(128)S(6)} %select_n.15, s32[]{:T(128)S(6)} %select_n.14), kind=kLoop, calls=%fused_computation | loop fusion | bytes 557064 | tf_op jit(solution)/shard_map/reshape | solution.py:324
  1.1 11.2 %collective-permute-start.1 = (f32[272,128]{1,0:T(8,128)S(1)}, f32[272,128]{1,0:T(8,128)S(1)}, u32[]{:S(2)}, u32[]{:S(2)}) collective-permute-start(f32[272,128]{1,0:T(8,128)S(1)} %get-tuple-element.15), channel_id=1, source_target_pairs={{4,8},{8,4},{12,16},{16,12},{20,24},{24,20},{28,32},{32,28},{36,40... | collective-permute-start | bytes 417800 | tf_op jit(solution)/shard_map/ppermute | solution.py:325
  12.3 1.9 %collective-permute-start = (f32[272,128]{1,0:T(8,128)S(1)}, f32[272,128]{1,0:T(8,128)S(1)}, u32[]{:S(2)}, u32[]{:S(2)}) collective-permute-start(f32[272,128]{1,0:T(8,128)S(1)} %get-tuple-element.16), channel_id=1, source_target_pairs={{0,4},{4,0},{8,12},{12,8},{16,20},{20,16},{24,28},{28,24},{32,36},... | collective-permute-start | bytes 417800 | tf_op jit(solution)/shard_map/ppermute | solution.py:326
  14.2 0.0 copy-done
  14.2 0.0 copy-done.1
  14.2 0.2 weights.1
  14.4 0.5 %collective-permute-done.1.far_ref = f32[272,128]{1,0:T(8,128)S(1)} collective-permute-done((f32[272,128]{1,0:T(8,128)S(1)}, f32[272,128]{1,0:T(8,128)S(1)}, u32[]{:S(2)}, u32[]{:S(2)}) %collective-permute-start.1) | collective-permute-done | bytes 139296 | tf_op jit(solution)/shard_map/ppermute | solution.py:325
  15.0 0.5 %collective-permute-done.near_ref = f32[272,128]{1,0:T(8,128)S(1)} collective-permute-done((f32[272,128]{1,0:T(8,128)S(1)}, f32[272,128]{1,0:T(8,128)S(1)}, u32[]{:S(2)}, u32[]{:S(2)}) %collective-permute-start) | collective-permute-done | bytes 139296 | tf_op jit(solution)/shard_map/ppermute | solution.py:326
  15.5 1.6 %border.1 = f32[4,144,128]{2,1,0:T(8,128)} custom-call(f32[272,128]{1,0:T(8,128)S(1)} %collective-permute-done.near_ref, f32[272,128]{1,0:T(8,128)S(1)} %collective-permute-done.1.far_ref, f32[3,64,128]{2,1,0:T(8,128)S(1)} %get-tuple-element.12.border_u, f32[3,40,128]{2,1,0:T(8,128)S(1)} %get-tuple-element.13.border_fwd, ...), custom_call_target="tpu_custom_call" | custom-call | tf_op jit(solution)/shard_map/border/pallas_call | solution.py:348
  17.2 4.3 %all-to-all-start = ((f32[4,144,128]{2,1,0:T(8,128)}), f32[4,144,128]{2,1,0:T(8,128)S(1)}, u32[]{:S(2)}, u32[]{:S(2)}) async-start(f32[4,144,128]{2,1,0:T(8,128)} %border.1), calls=%async_computation | async-start | bytes 589824 | tf_op jit(solution)/shard_map/all_to_all | solution.py:375
  21.5 2.1 %blur.1.v_ref = f32[8,72,128]{2,1,0:T(8,128)S(1)} custom-call(f32[512,128]{1,0:T(8,128)S(1)} %bitcast.8, f32[272,128]{1,0:T(8,128)S(1)} %collective-permute-done.near_ref, f32[272,128]{1,0:T(8,128)S(1)} %collective-permute-done.1.far_ref, f32[264,128]{1,0:T(8,128)S(1)} %get-tuple-element.10.fwd, f32[264,128]{1,0:T(8,128)S(1)} %get-tuple-element.11.adj), custom_call_target="tpu_custom_call" | custom-call | flops 11894784 | tf_op jit(solution)/shard_map/blur/pallas_call | solution.py:362
  23.5 5.2 %all-to-all-done.got_ref = f32[4,144,128]{2,1,0:T(8,128)S(1)} async-done(((f32[4,144,128]{2,1,0:T(8,128)}), f32[4,144,128]{2,1,0:T(8,128)S(1)}, u32[]{:S(2)}, u32[]{:S(2)}) %all-to-all-start) | async-done | bytes 294944 | tf_op jit(solution)/shard_map/all_to_all | solution.py:375
  28.8 2.0 %tv.1 = f32[512,128]{1,0:T(8,128)} custom-call(f32[8,72,128]{2,1,0:T(8,128)S(1)} %blur.1.v_ref, f32[4,144,128]{2,1,0:T(8,128)S(1)} %all-to-all-done.got_ref), custom_call_target="tpu_custom_call" | custom-call | tf_op jit(solution)/shard_map/tv/pallas_call | solution.py:378
Async XLA Ops:
  0.0 14.2 %copy-start = (f32[64,8,128]{2,1,0:T(8,128)S(1)}, f32[64,8,128]{2,1,0:T(8,128)}, u32[]{:S(2)}) copy-start(f32[64,8,128]{2,1,0:T(8,128)} %param.2) | copy-start | bytes 786436
  0.0 14.2 %copy-start.1 = (f32[33,8,128]{2,1,0:T(8,128)S(1)}, f32[33,8,128]{2,1,0:T(8,128)}, u32[]{:S(2)}) copy-start(f32[33,8,128]{2,1,0:T(8,128)} %param.3) | copy-start | bytes 405508
  1.1 13.9 %collective-permute-start.1 = (f32[272,128]{1,0:T(8,128)S(1)}, f32[272,128]{1,0:T(8,128)S(1)}, u32[]{:S(2)}, u32[]{:S(2)}) collective-permute-start(f32[272,128]{1,0:T(8,128)S(1)} %get-tuple-element.15), channel_id=1, source_target_pairs={{4,8},{8,4},{12,16},{16,12},{20,24},{24,20},{28,32},{32,28},{36,40... | collective-permute-start | bytes 417800 | tf_op jit(solution)/shard_map/ppermute | solution.py:325
  12.3 3.3 %collective-permute-start = (f32[272,128]{1,0:T(8,128)S(1)}, f32[272,128]{1,0:T(8,128)S(1)}, u32[]{:S(2)}, u32[]{:S(2)}) collective-permute-start(f32[272,128]{1,0:T(8,128)S(1)} %get-tuple-element.16), channel_id=1, source_target_pairs={{0,4},{4,0},{8,12},{12,8},{16,20},{20,16},{24,28},{28,24},{32,36},... | collective-permute-start | bytes 417800 | tf_op jit(solution)/shard_map/ppermute | solution.py:326
  17.2 11.6 %all-to-all-start = ((f32[4,144,128]{2,1,0:T(8,128)}), f32[4,144,128]{2,1,0:T(8,128)S(1)}, u32[]{:S(2)}, u32[]{:S(2)}) async-start(f32[4,144,128]{2,1,0:T(8,128)} %border.1), calls=%async_computation | async-start | bytes 589824 | tf_op jit(solution)/shard_map/all_to_all | solution.py:375

commit v5 on v3

--- a/solution.py
+++ b/solution.py
@@ -10,77 +10,99 @@
 scale = -inner_step / theta
 
 REACH = 2
-BLOCK = 10
-
-
-def blur_kernel(u_ref, near_ref, far_ref, kernel_ref, v_ref, message_ref, upad, fwd, adj, q, vflat):
-    tm, row, col = lax.axis_index("tm"), lax.axis_index("row"), lax.axis_index("col")
-    frames, rows, cols = u_ref.shape
-    taps = kernel_ref.shape[0]
+ROWS = 8
+HALF = 36
+BLOCK, WIDE_BLOCK = 10, 12
+
+
+def at(frame, count=1):
+    return pl.ds(pl.multiple_of(frame * ROWS, ROWS), count * ROWS)
+
+
+def blur(weights, field, begin, block, flip=False):
+    taps = weights.shape[0] // ROWS
+    window = [field[at(begin + i)] for i in range(block + taps - 1)]
+    acc = [None] * block
+    for tap in range(taps):
+        weight = weights[at(tap)]
+        for i in range(block):
+            term = weight * window[i + (taps - 1 - tap if flip else tap)]
+            acc[i] = term if tap == 0 else acc[i] + term
+    return acc
+
+
+def own_kernel(u_ref, kernel_ref, fwd, adj, q_ref):
+    taps = kernel_ref.shape[0] // ROWS
     half = taps // 2
-    halo = 2 * half + REACH
-    span = frames + 2 * REACH
-    deep = v_ref.shape[1]
-
-    odd = lax.rem(tm, 2)
-    upad[halo : halo + frames] = u_ref[...]
-    upad[pl.ds((1 - odd) * (halo + frames), halo)] = near_ref[...]
-    upad[pl.ds(odd * (halo + frames), halo)] = far_ref[...]
-
-    total = kernel_ref[0]
+    total = kernel_ref[at(0)]
     for tap in range(1, taps):
-        total = total + kernel_ref[tap]
+        total = total + kernel_ref[at(tap)]
     inverse = 1.0 / total
     for tap in range(taps):
-        share = kernel_ref[tap] * inverse
-        adj[tap] = share
-        fwd[tap] = (share - 1.0 if tap == half else share) * (1.0 / 3.0)
-
-    q_count = frames + 2 * (half + REACH)
+        share = kernel_ref[at(tap)] * inverse
+        adj[at(tap)] = share
+        fwd[at(tap)] = (share - 1.0 if tap == half else share) * (1.0 / 3.0)
 
     def forward(step, carry):
-        base = step * BLOCK
-        window = [upad[base + i] for i in range(BLOCK + taps - 1)]
-        acc = [None] * BLOCK
-        for tap in range(taps):
-            weight = fwd[tap]
-            for i in range(BLOCK):
-                term = weight * window[i + tap]
-                acc[i] = term if tap == 0 else acc[i] + term
-        for i in range(BLOCK):
-            q[base + i] = acc[i]
+        for i, value in enumerate(blur(fwd, u_ref, 1 + step * BLOCK, BLOCK)):
+            q_ref[at(step * BLOCK + i)] = value
         return carry
 
-    lax.fori_loop(0, q_count // BLOCK, forward, 0)
-    nothing = jnp.zeros((half + REACH, rows, cols), jnp.float32)
-
-    @pl.when(tm == 0)
+    lax.fori_loop(0, q_ref.shape[0] // ROWS // BLOCK, forward, 0)
+
+
+def half_blur(side, part_ref, u_ref, q_own, fwd, adj, u, q, v, v_begin):
+    frames = u_ref.shape[0] // ROWS
+    halo = part_ref.shape[0] // ROWS
+    half = (halo - REACH) // 2
+    u[at(side * halo, halo)] = part_ref[...]
+    u[at((1 - side) * halo, halo)] = u_ref[at(side * (frames - halo), halo)]
+    q[at(halo + 1, q_own.shape[0] // ROWS)] = q_own[...]
+
+    def forward(step, carry):
+        for i, value in enumerate(blur(fwd, u, step * WIDE_BLOCK, WIDE_BLOCK)):
+            q[at(side * frames + step * WIDE_BLOCK + i)] = value
+        return carry
+
+    lax.fori_loop(0, HALF // WIDE_BLOCK, forward, 0)
+    tm = lax.axis_index("tm")
+    nothing = jnp.zeros(((half + REACH) * ROWS, q.shape[1]), jnp.float32)
+
+    @pl.when((tm == 0) & (side == 0))
     def _():
-        q[: half + REACH] = nothing
-
-    @pl.when(tm == lax.axis_size("tm") - 1)
+        q[at(0, half + REACH)] = nothing
+
+    @pl.when((tm == lax.axis_size("tm") - 1) & (side == 1))
     def _():
-        q[q_count - half - REACH : q_count] = nothing
-
-    q[q_count:] = jnp.zeros((q.shape[0] - q_count, rows, cols), jnp.float32)
+        q[at(frames + half + REACH, half + REACH)] = nothing
 
     def adjoint(step, carry):
-        base = step * BLOCK
-        window = [q[base + i] for i in range(BLOCK + taps - 1)]
-        acc = [None] * BLOCK
-        for tap in range(taps):
-            weight = adj[tap]
-            for i in range(BLOCK):
-                term = weight * window[i + taps - 1 - tap]
-                acc[i] = term if tap == 0 else acc[i] + term
-        for i in range(BLOCK):
-            at = pl.multiple_of((base + i) * rows, rows)
-            vflat[pl.ds(at, rows)] = upad[base + i + 2 * half] - acc[i]
+        base = step * WIDE_BLOCK
+        for i, value in enumerate(blur(adj, q, side * 2 * half + base, WIDE_BLOCK, True)):
+            v[at(v_begin + base + i)] = u[at((1 - side) * 2 * half + base + i)] - value
         return carry
 
-    steps = -(-span // BLOCK)
-    lax.fori_loop(0, steps, adjoint, 0)
-    vflat[steps * BLOCK * rows :] = jnp.zeros((vflat.shape[0] - steps * BLOCK * rows, cols), jnp.float32)
+    lax.fori_loop(0, HALF // WIDE_BLOCK, adjoint, 0)
+
+
+def far_kernel(part_ref, u_ref, q_own, fwd, adj, q_ref, v_ref, u, q):
+    side = lax.rem(lax.axis_index("tm"), 2)
+    frames = u_ref.shape[0] // ROWS
+    half_blur(side, part_ref, u_ref, q_own, fwd, adj, u, q, v_ref, 0)
+    q_ref[...] = q[at(side * frames, HALF)]
+
+
+def near_kernel(part_ref, u_ref, q_own, fwd, adj, q_far, v_far, v_ref, message_ref, u, q, vflat):
+    row, col = lax.axis_index("row"), lax.axis_index("col")
+    side = 1 - lax.rem(lax.axis_index("tm"), 2)
+    frames = u_ref.shape[0] // ROWS
+    halo = part_ref.shape[0] // ROWS
+    rows, deep, cols = v_ref.shape
+    span = frames + 2 * REACH
+    q[at((1 - side) * frames, HALF)] = q_far[...]
+    vflat[at((1 - side) * (span - HALF), HALF)] = v_far[...]
+    half_blur(side, part_ref, u_ref, q_own, fwd, adj, u, q, vflat, side * (span - HALF))
+    vflat[at(span, deep - span)] = jnp.zeros(((deep - span) * rows, cols), jnp.float32)
 
     lane = lax.broadcasted_iota(jnp.int32, (deep, cols), 1)
     edge = jnp.zeros((deep, cols), jnp.float32)
@@ -224,29 +246,44 @@
     vmem = pl.BlockSpec(memory_space=pltpu.VMEM)
     f32 = jnp.float32
 
-    near = lax.dynamic_slice_in_dim(observed, (1 - odd) * (frames - halo), halo, axis=0)
-    far = lax.dynamic_slice_in_dim(observed, odd * (frames - halo), halo, axis=0)
+    near = lax.dynamic_slice_in_dim(observed, (1 - odd) * (frames - halo), halo, axis=0).reshape(halo * rows, cols)
+    far = lax.dynamic_slice_in_dim(observed, odd * (frames - halo), halo, axis=0).reshape(halo * rows, cols)
     far = lax.ppermute(far, "tm", [(i, i + 1 if i % 2 else i - 1) for i in range(1, count - 1)])
     near = lax.ppermute(near, "tm", [(i, i ^ 1) for i in range(count)])
-
+    near, far = on_chip(near), on_chip(far)
+    mine = on_chip(observed.reshape(frames * rows, cols))
+
+    def flat(count):
+        return (count * rows, cols)
+
+    fwd, adj, q_own = pl.pallas_call(
+        own_kernel,
+        out_shape=(on_chip_result(flat(taps)), on_chip_result(flat(taps)), on_chip_result(flat(frames - 2 * half - 2))),
+        in_specs=[vmem] * 2,
+        out_specs=(vmem,) * 3,
+        name="own",
+    )(mine, on_chip(kernel.reshape(taps * rows, cols)))
+    fwd, adj, q_own = map(on_chip, (fwd, adj, q_own))
+    q_far, v_far = pl.pallas_call(
+        far_kernel,
+        out_shape=(on_chip_result(flat(HALF)),) * 2,
+        in_specs=[vmem] * 5,
+        out_specs=(vmem,) * 2,
+        scratch_shapes=[pltpu.VMEM(flat(2 * halo), f32), pltpu.VMEM(flat(deep + 2 * half), f32)],
+        name="far",
+    )(far, mine, q_own, fwd, adj)
     v, message = pl.pallas_call(
-        blur_kernel,
-        out_shape=(
-            on_chip_result((rows, deep, cols)),
-            on_chip_result((4, REACH * deep, cols)),
-        ),
-        in_specs=[vmem] * 4,
+        near_kernel,
+        out_shape=(on_chip_result((rows, deep, cols)), on_chip_result((4, REACH * deep, cols))),
+        in_specs=[vmem] * 7,
         out_specs=(vmem,) * 2,
         scratch_shapes=[
-            pltpu.VMEM((frames + 2 * halo, rows, cols), f32),
-            pltpu.VMEM((taps, rows, cols), f32),
-            pltpu.VMEM((taps, rows, cols), f32),
-            pltpu.VMEM((deep + 2 * half, rows, cols), f32),
-            pltpu.VMEM((deep * rows, cols), f32),
+            pltpu.VMEM(flat(2 * halo), f32),
+            pltpu.VMEM(flat(deep + 2 * half), f32),
+            pltpu.VMEM(flat(deep), f32),
         ],
-        name="blur",
-    )(*map(on_chip, (observed, near, far, kernel)))
-
+        name="near",
+    )(near, mine, q_own, fwd, adj, on_chip(q_far), on_chip(v_far))
     got = lax.all_to_all(message, ("row", "col"), 0, 0, tiled=True)
 
     wide = rows + REACH

time: 31.3 us -> 30.5 us (0.974)
  waiting for transfers between devices: 1.32 us -> 0.37 us
    dynamic_slice x1 -> x0, local copies, waits for them, and re-layouts: 1.07 us -> none  [body(): lax.dynamic_slice_in_dim(observed, odd * (frames - halo), halo, axis=0)]
    reshape x0 -> x1, local copies, waits for them, and re-layouts: none -> 1.07 us  [body(): lax.dynamic_slice_in_dim(observed, odd * (frames - halo), halo, axis=0)]
    ppermute x1, waiting for transfers between devices: 0.53 us -> 0.01 us  [body(): near = lax.ppermute(near, 'tm', [(i, i ^ 1) for i in range(count)])]
    ppermute x1, waiting for transfers between devices: 0.8 us -> 0.37 us  [body(): lax.ppermute(far, 'tm', [(i, i + 1 if i % 2 else i - 1) for i in range(1,...]
    pallas_call x1 -> x3, Pallas kernels: 2.21 us -> 2.31 us  [the longest x1 1.06 us: body(): pl.pallas_call(near_kernel, out_shape=(on_chip_result((rows, deep, cols))...]
  transfers between devices with their start and end apart: 2 -> 2, of which waited for: 2 -> 1; matrix products, arithmetic and copies ran while one was open for 0% -> 0% of each run, Pallas kernels for 0% -> 4%
where the time goes in v5:
time: 30.5 us; the launch traced here: 30.3 us
  starting transfers between devices  13.1 us (43%)
  blocking collectives  11.4 us (37%)
  Pallas kernels  4.31 us (14%)
  local copies, waits for them, and re-layouts  1.08 us (4%)
  waiting for transfers between devices  0.37 us (1%)
    all_to_all x1, blocking collectives, body(): got = lax.all_to_all(message, ('row', 'col'), 0, 0, tiled=True)  11.4 us
    ppermute x1, starting transfers between devices, body(): lax.ppermute(far, 'tm', [(i, i + 1 if i % 2 else i - 1) for i in range(1,...  11.2 us
    pallas_call x1, Pallas kernels, body(): pl.pallas_call(tv_kernel, out_shape=jax.ShapeDtypeStruct((frames * rows,...  2 us
    ppermute x1, starting transfers between devices, body(): near = lax.ppermute(near, 'tm', [(i, i ^ 1) for i in range(count)])  1.92 us
    reshape x1, local copies, waits for them, and re-layouts, body(): lax.dynamic_slice_in_dim(observed, odd * (frames - halo), halo, axis=0)  1.07 us
    pallas_call x1, Pallas kernels, body(): pl.pallas_call(near_kernel, out_shape=(on_chip_result((rows, deep, cols))...  1.06 us
    pallas_call x1, Pallas kernels, body(): pl.pallas_call(far_kernel, out_shape=(on_chip_result(flat(HALF)),) * 2, i...  0.85 us
  transfers between devices with their start and end apart: 2, of which 1 were waited for; matrix products, arithmetic and copies ran while one was open for 0% of the time, Pallas kernels for 4%

profile of v5, /device:TPU:56, one launch (start us, length us, event | category | flops | bytes accessed | tf_op | source)
XLA Modules:
  0.0 30.3 jit_solution(8376284487370591495)
XLA Ops:
  0.0 0.0 copy-start
  0.0 0.0 copy-start.1
  0.0 1.1 %dynamic-slice_bitcast_fusion = (f32[272,128]{1,0:T(8,128)S(1)}, f32[272,128]{1,0:T(8,128)S(1)}) fusion(f32[64,8,128]{2,1,0:T(8,128)} %param.2, s32[]{:T(128)S(6)} %select_n.15, s32[]{:T(128)S(6)} %select_n.14), kind=kLoop, calls=%fused_computation | loop fusion | bytes 557064 | tf_op jit(solution)/shard_map/reshape | solution.py:250
  1.1 11.2 %collective-permute-start.1 = (f32[272,128]{1,0:T(8,128)S(1)}, f32[272,128]{1,0:T(8,128)S(1)}, u32[]{:S(2)}, u32[]{:S(2)}) collective-permute-start(f32[272,128]{1,0:T(8,128)S(1)} %get-tuple-element.19), channel_id=1, source_target_pairs={{4,8},{8,4},{12,16},{16,12},{20,24},{24,20},{28,32},{32,28},{36,40... | collective-permute-start | bytes 417800 | tf_op jit(solution)/shard_map/ppermute | solution.py:251
  12.3 1.9 %collective-permute-start = (f32[272,128]{1,0:T(8,128)S(1)}, f32[272,128]{1,0:T(8,128)S(1)}, u32[]{:S(2)}, u32[]{:S(2)}) collective-permute-start(f32[272,128]{1,0:T(8,128)S(1)} %get-tuple-element.20), channel_id=1, source_target_pairs={{0,4},{4,0},{8,12},{12,8},{16,20},{20,16},{24,28},{28,24},{32,36},... | collective-permute-start | bytes 417800 | tf_op jit(solution)/shard_map/ppermute | solution.py:252
  14.2 0.0 copy-done
  14.2 0.0 copy-done.1
  14.2 0.4 %own.1 = (f32[264,128]{1,0:T(8,128)S(1)}, f32[264,128]{1,0:T(8,128)S(1)}, f32[240,128]{1,0:T(8,128)S(1)}) custom-call(f32[512,128]{1,0:T(8,128)S(1)} %bitcast.7, f32[264,128]{1,0:T(8,128)S(1)} %bitcast.10), custom_call_target="tpu_custom_call" | custom-call | tf_op jit(solution)/shard_map/own/pallas_call | solution.py:259
  14.6 0.4 %collective-permute-done.1.part_ref = f32[272,128]{1,0:T(8,128)S(1)} collective-permute-done((f32[272,128]{1,0:T(8,128)S(1)}, f32[272,128]{1,0:T(8,128)S(1)}, u32[]{:S(2)}, u32[]{:S(2)}) %collective-permute-start.1) | collective-permute-done | bytes 139296 | tf_op jit(solution)/shard_map/ppermute | solution.py:251
  15.0 0.9 %far.1 = (f32[288,128]{1,0:T(8,128)S(1)}, f32[288,128]{1,0:T(8,128)S(1)}) custom-call(f32[272,128]{1,0:T(8,128)S(1)} %collective-permute-done.1.part_ref, f32[512,128]{1,0:T(8,128)S(1)} %bitcast.8, f32[240,128]{1,0:T(8,128)S(1)} %get-tuple-element.12.q_own, f32[264,128]{1,0:T(8,128)S(1)} %get-tuple-element.13.fwd, f32[264,128]{1,0:T(8,128)S(1)} %get-tuple-element.14.adj), custom_call_target="tpu_custom_call" | custom-call | tf_op jit(solution)/shard_map/far/pallas_call | solution.py:267
  15.8 0.0 collective-permute-done.part_ref
  15.8 1.1 %near.1 = (f32[8,72,128]{2,1,0:T(8,128)S(1)}, f32[4,144,128]{2,1,0:T(8,128)S(1)}) custom-call(f32[272,128]{1,0:T(8,128)S(1)} %collective-permute-done.part_ref, f32[512,128]{1,0:T(8,128)S(1)} %bitcast.9, f32[240,128]{1,0:T(8,128)S(1)} %get-tuple-element.12.q_own, f32[264,128]{1,0:T(8,128)S(1)} %get-tuple-element.13.fwd, ...), custom_call_target="tpu_custom_call" | custom-call | tf_op jit(solution)/shard_map/near/pallas_call | solution.py:275
  16.9 11.4 %all_to_all.5.got_ref = f32[4,144,128]{2,1,0:T(8,128)S(1)} all-to-all(f32[4,144,128]{2,1,0:T(8,128)S(1)} %get-tuple-element.18), channel_id=1, replica_groups=mesh['tm'=128,'row'=2,'col'=2] {'row','col'}, dimensions={0} | all-to-all | bytes 589824 | tf_op jit(solution)/shard_map/all_to_all | solution.py:287
  28.3 2.0 %tv.1 = f32[512,128]{1,0:T(8,128)} custom-call(f32[8,72,128]{2,1,0:T(8,128)S(1)} %get-tuple-element.17.v_ref, f32[4,144,128]{2,1,0:T(8,128)S(1)} %all_to_all.5.got_ref), custom_call_target="tpu_custom_call" | custom-call | tf_op jit(solution)/shard_map/tv/pallas_call | solution.py:290
Async XLA Ops:
  0.0 14.2 %copy-start = (f32[64,8,128]{2,1,0:T(8,128)S(1)}, f32[64,8,128]{2,1,0:T(8,128)}, u32[]{:S(2)}) copy-start(f32[64,8,128]{2,1,0:T(8,128)} %param.2) | copy-start | bytes 786436
  0.0 14.2 %copy-start.1 = (f32[33,8,128]{2,1,0:T(8,128)S(1)}, f32[33,8,128]{2,1,0:T(8,128)}, u32[]{:S(2)}) copy-start(f32[33,8,128]{2,1,0:T(8,128)} %param.3) | copy-start | bytes 405508
  1.1 13.9 %collective-permute-start.1 = (f32[272,128]{1,0:T(8,128)S(1)}, f32[272,128]{1,0:T(8,128)S(1)}, u32[]{:S(2)}, u32[]{:S(2)}) collective-permute-start(f32[272,128]{1,0:T(8,128)S(1)} %get-tuple-element.19), channel_id=1, source_target_pairs={{4,8},{8,4},{12,16},{16,12},{20,24},{24,20},{28,32},{32,28},{36,40... | collective-permute-start | bytes 417800 | tf_op jit(solution)/shard_map/ppermute | solution.py:251
  12.3 3.6 %collective-permute-start = (f32[272,128]{1,0:T(8,128)S(1)}, f32[272,128]{1,0:T(8,128)S(1)}, u32[]{:S(2)}, u32[]{:S(2)}) collective-permute-start(f32[272,128]{1,0:T(8,128)S(1)} %get-tuple-element.20), channel_id=1, source_target_pairs={{0,4},{4,0},{8,12},{12,8},{16,20},{20,16},{24,28},{28,24},{32,36},... | collective-permute-start | bytes 417800 | tf_op jit(solution)/shard_map/ppermute | solution.py:252

commit v6 on v5

--- a/solution.py
+++ b/solution.py
@@ -12,26 +12,59 @@
 REACH = 2
 ROWS = 8
 HALF = 36
-BLOCK, WIDE_BLOCK = 10, 12
+BLOCK, PAIRS = 10, 6
 
 
 def at(frame, count=1):
     return pl.ds(pl.multiple_of(frame * ROWS, ROWS), count * ROWS)
 
 
-def blur(weights, field, begin, block, flip=False):
+def blur(weights, field, begin, block):
     taps = weights.shape[0] // ROWS
     window = [field[at(begin + i)] for i in range(block + taps - 1)]
     acc = [None] * block
     for tap in range(taps):
         weight = weights[at(tap)]
         for i in range(block):
-            term = weight * window[i + (taps - 1 - tap if flip else tap)]
+            term = weight * window[i + tap]
             acc[i] = term if tap == 0 else acc[i] + term
     return acc
 
 
-def own_kernel(u_ref, kernel_ref, fwd, adj, q_ref):
+def blur_pairs(weights, sums, field, begin, shape, pairs, finish):
+    less, more = shape
+    taps = weights.shape[0] // ROWS
+    half = taps // 2
+    count = pairs + half
+    for t in range(count):
+        low, high = field[at(begin + 2 * t)], field[at(begin + 2 * t + 1)]
+        less[at(t)] = low - high
+        if t + 1 < count:
+            more[at(t)] = field[at(begin + 2 * t + 2)] - high
+
+    def step(number, carry):
+        base = number * PAIRS
+        first, shared, last = [None] * PAIRS, [None] * PAIRS, [None] * PAIRS
+        for k in range(half + 1):
+            even, both = weights[at(2 * k)], sums[at(k)]
+            odd = weights[at(2 * k + 1)] if k < half else None
+            for i in range(PAIRS):
+                term = even * less[at(base + i + k)]
+                first[i] = first[i] + term if k else term
+                term = both * field[at(begin + 2 * (base + i + k) + 1)]
+                shared[i] = shared[i] + term if k else term
+                if k < half:
+                    term = odd * more[at(base + i + k)]
+                    last[i] = last[i] + term if k else term
+        for i in range(PAIRS):
+            finish(2 * (base + i), first[i] + shared[i])
+            finish(2 * (base + i) + 1, last[i] + shared[i])
+        return carry
+
+    lax.fori_loop(0, pairs // PAIRS, step, 0)
+
+
+def own_kernel(u_ref, kernel_ref, fwd, adj, fwd_sums, adj_sums, q_ref):
     taps = kernel_ref.shape[0] // ROWS
     half = taps // 2
     total = kernel_ref[at(0)]
@@ -40,8 +73,12 @@
     inverse = 1.0 / total
     for tap in range(taps):
         share = kernel_ref[at(tap)] * inverse
-        adj[at(tap)] = share
+        adj[at(taps - 1 - tap)] = share
         fwd[at(tap)] = (share - 1.0 if tap == half else share) * (1.0 / 3.0)
+    for weights, sums in ((fwd, fwd_sums), (adj, adj_sums)):
+        for k in range(half):
+            sums[at(k)] = weights[at(2 * k)] + weights[at(2 * k + 1)]
+        sums[at(half)] = weights[at(taps - 1)]
 
     def forward(step, carry):
         for i, value in enumerate(blur(fwd, u_ref, 1 + step * BLOCK, BLOCK)):
@@ -51,7 +88,8 @@
     lax.fori_loop(0, q_ref.shape[0] // ROWS // BLOCK, forward, 0)
 
 
-def half_blur(side, part_ref, u_ref, q_own, fwd, adj, u, q, v, v_begin):
+def half_blur(side, part_ref, u_ref, q_own, taps_of, u, q, less, more, v, v_begin):
+    fwd, adj, fwd_sums, adj_sums = taps_of
     frames = u_ref.shape[0] // ROWS
     halo = part_ref.shape[0] // ROWS
     half = (halo - REACH) // 2
@@ -59,12 +97,10 @@
     u[at((1 - side) * halo, halo)] = u_ref[at(side * (frames - halo), halo)]
     q[at(halo + 1, q_own.shape[0] // ROWS)] = q_own[...]
 
-    def forward(step, carry):
-        for i, value in enumerate(blur(fwd, u, step * WIDE_BLOCK, WIDE_BLOCK)):
-            q[at(side * frames + step * WIDE_BLOCK + i)] = value
-        return carry
-
-    lax.fori_loop(0, HALF // WIDE_BLOCK, forward, 0)
+    def keep_q(i, value):
+        q[at(side * frames + i)] = value
+
+    blur_pairs(fwd, fwd_sums, u, 0, (less, more), HALF // 2, keep_q)
     tm = lax.axis_index("tm")
     nothing = jnp.zeros(((half + REACH) * ROWS, q.shape[1]), jnp.float32)
 
@@ -76,50 +112,51 @@
     def _():
         q[at(frames + half + REACH, half + REACH)] = nothing
 
-    def adjoint(step, carry):
-        base = step * WIDE_BLOCK
-        for i, value in enumerate(blur(adj, q, side * 2 * half + base, WIDE_BLOCK, True)):
-            v[at(v_begin + base + i)] = u[at((1 - side) * 2 * half + base + i)] - value
-        return carry
-
-    lax.fori_loop(0, HALF // WIDE_BLOCK, adjoint, 0)
-
-
-def far_kernel(part_ref, u_ref, q_own, fwd, adj, q_ref, v_ref, u, q):
+    def keep_v(i, value):
+        v[at(v_begin + i)] = u[at((1 - side) * 2 * half + i)] - value
+
+    blur_pairs(adj, adj_sums, q, side * 2 * half, (less, more), HALF // 2, keep_v)
+
+
+def far_kernel(part_ref, u_ref, q_own, fwd, adj, fwd_sums, adj_sums, q_ref, v_ref, u, q, less, more):
     side = lax.rem(lax.axis_index("tm"), 2)
     frames = u_ref.shape[0] // ROWS
-    half_blur(side, part_ref, u_ref, q_own, fwd, adj, u, q, v_ref, 0)
+    half_blur(side, part_ref, u_ref, q_own, (fwd, adj, fwd_sums, adj_sums), u, q, less, more, v_ref, 0)
     q_ref[...] = q[at(side * frames, HALF)]
 
 
-def near_kernel(part_ref, u_ref, q_own, fwd, adj, q_far, v_far, v_ref, message_ref, u, q, vflat):
+def near_kernel(
+    part_ref, u_ref, q_own, fwd, adj, fwd_sums, adj_sums, q_far, v_far, vflat, edge_ref, message_ref, u, q, less, more
+):
     row, col = lax.axis_index("row"), lax.axis_index("col")
     side = 1 - lax.rem(lax.axis_index("tm"), 2)
     frames = u_ref.shape[0] // ROWS
     halo = part_ref.shape[0] // ROWS
-    rows, deep, cols = v_ref.shape
+    deep, cols = edge_ref.shape
+    rows = vflat.shape[0] // deep
     span = frames + 2 * REACH
     q[at((1 - side) * frames, HALF)] = q_far[...]
     vflat[at((1 - side) * (span - HALF), HALF)] = v_far[...]
-    half_blur(side, part_ref, u_ref, q_own, fwd, adj, u, q, vflat, side * (span - HALF))
+    taps_of = (fwd, adj, fwd_sums, adj_sums)
+    half_blur(side, part_ref, u_ref, q_own, taps_of, u, q, less, more, vflat, side * (span - HALF))
     vflat[at(span, deep - span)] = jnp.zeros(((deep - span) * rows, cols), jnp.float32)
 
     lane = lax.broadcasted_iota(jnp.int32, (deep, cols), 1)
     edge = jnp.zeros((deep, cols), jnp.float32)
     for r in range(rows):
         plane = vflat[pl.ds(r, deep, stride=rows)]
-        v_ref[r] = plane
         first = 4 * (r + 2 * row)
         moved = pltpu.roll(plane, first + 2, axis=1)
         low = first + 2 * col
         edge = jnp.where((lane >= low) & (lane < low + 2), moved, edge)
+    edge_ref[...] = edge
     third = deep // 3
     packed = edge[:third] + pltpu.roll(edge[third : 2 * third], 40, axis=1) + pltpu.roll(edge[2 * third :], 80, axis=1)
     message_ref[2 * row + (1 - col), :third] = packed
     message_ref[2 * (1 - row) + (1 - col), :third] = packed
     begin = (rows - REACH) * (1 - row)
     for i in range(REACH):
-        message_ref[2 * (1 - row) + col, i * deep : (i + 1) * deep] = v_ref[begin + i]
+        message_ref[2 * (1 - row) + col, i * span : (i + 1) * span] = vflat[pl.ds(begin + i, span, stride=rows)]
 
 
 def unit(z_t, z_r, z_c):
@@ -133,11 +170,13 @@
     return jnp.concatenate([jnp.where(lane < 40, part, 0.0) for part in parts], axis=0)
 
 
-def tv_kernel(v_ref, got_ref, out_ref, w, p_t, p_r, p_c, e_w, e_t, e_c):
+def tv_kernel(v_ref, edge_ref, got_ref, out_ref, w, p_t, p_r, p_c, e_w, e_t, e_c):
     tm, row, col = lax.axis_index("tm"), lax.axis_index("row"), lax.axis_index("col")
-    rows, deep, cols = v_ref.shape
+    deep, cols = edge_ref.shape
+    rows = v_ref.shape[0] // deep
     frames = out_ref.shape[0] // rows
     wide = rows + REACH
+    span = frames + 2 * REACH
 
     lane = lax.broadcasted_iota(jnp.int32, (deep, cols), 1)
     time = lax.broadcasted_iota(jnp.int32, (deep, cols), 0)
@@ -153,18 +192,19 @@
     own = REACH * row
     foreign = rows * (1 - row)
     for r in range(rows):
-        w[r + own, :deep] = v_ref[r] * scale
+        w[r + own, :deep] = v_ref[pl.ds(r, deep, stride=rows)] * scale
     for i in range(REACH):
-        w[foreign + i, :deep] = got_ref[2 * (1 - row) + col, i * deep : (i + 1) * deep] * scale
+        w[foreign + i, span:deep] = jnp.zeros((deep - span, cols), jnp.float32)
+        w[foreign + i, :span] = got_ref[2 * (1 - row) + col, i * span : (i + 1) * span] * scale
     w[wide, :deep] = w[wide - 1, :deep]
 
     low = 4 * foreign
     corner = pltpu.roll(unpacked(got_ref[2 * (1 - row) + (1 - col), : deep // 3]), jnp.where(row == 0, 24, cols - 24), axis=1)
-    edge = unpacked(got_ref[2 * row + (1 - col), : deep // 3]) + jnp.where((lane >= low) & (lane < low + 8), corner, 0.0)
+    edge = edge_ref[...] + unpacked(got_ref[2 * row + (1 - col), : deep // 3]) + jnp.where((lane >= low) & (lane < low + 8), corner, 0.0)
     edge = edge * scale
-    for r in range(wide):
-        moved = pltpu.roll(w[r, :deep], 4 * r + 2, axis=1)
-        begin = 4 * r + 2 * col
+    for i in range(REACH):
+        moved = pltpu.roll(w[foreign + i, :deep], 4 * (foreign + i) + 2, axis=1)
+        begin = 4 * (foreign + i) + 2 * col
         edge = jnp.where((lane >= begin) & (lane < begin + 2), moved, edge)
 
     def edge_slopes(field):
@@ -222,7 +262,7 @@
     for r in range(wide):
         second_pass(r)
     for r in range(rows):
-        updated = v_ref[r] - theta * divergence(r + own, 3)
+        updated = v_ref[pl.ds(r, deep, stride=rows)] - theta * divergence(r + own, 3)
         p_c[r + own] = updated
         out_ref[pl.ds(r, frames, stride=rows)] = p_c[r + own, REACH : REACH + frames]
 
@@ -256,41 +296,39 @@
     def flat(count):
         return (count * rows, cols)
 
-    fwd, adj, q_own = pl.pallas_call(
+    shapes = [flat(n) for n in (taps, taps, half + 1, half + 1, frames - 2 * half - 2)]
+    *taps_of, q_own = pl.pallas_call(
         own_kernel,
-        out_shape=(on_chip_result(flat(taps)), on_chip_result(flat(taps)), on_chip_result(flat(frames - 2 * half - 2))),
+        out_shape=tuple(map(on_chip_result, shapes)),
         in_specs=[vmem] * 2,
-        out_specs=(vmem,) * 3,
+        out_specs=(vmem,) * 5,
         name="own",
     )(mine, on_chip(kernel.reshape(taps * rows, cols)))
-    fwd, adj, q_own = map(on_chip, (fwd, adj, q_own))
+    taps_of, q_own = list(map(on_chip, taps_of)), on_chip(q_own)
+    scratch = [pltpu.VMEM(flat(n), f32) for n in (2 * halo, deep + 2 * half, halo, halo)]
     q_far, v_far = pl.pallas_call(
         far_kernel,
         out_shape=(on_chip_result(flat(HALF)),) * 2,
-        in_specs=[vmem] * 5,
-        out_specs=(vmem,) * 2,
-        scratch_shapes=[pltpu.VMEM(flat(2 * halo), f32), pltpu.VMEM(flat(deep + 2 * half), f32)],
-        name="far",
-    )(far, mine, q_own, fwd, adj)
-    v, message = pl.pallas_call(
-        near_kernel,
-        out_shape=(on_chip_result((rows, deep, cols)), on_chip_result((4, REACH * deep, cols))),
         in_specs=[vmem] * 7,
         out_specs=(vmem,) * 2,
-        scratch_shapes=[
-            pltpu.VMEM(flat(2 * halo), f32),
-            pltpu.VMEM(flat(deep + 2 * half), f32),
-            pltpu.VMEM(flat(deep), f32),
-        ],
+        scratch_shapes=scratch,
+        name="far",
+    )(far, mine, q_own, *taps_of)
+    v, edge, message = pl.pallas_call(
+        near_kernel,
+        out_shape=tuple(map(on_chip_result, (flat(deep), (deep, cols), (4, REACH * (frames + 2 * REACH), cols)))),
+        in_specs=[vmem] * 9,
+        out_specs=(vmem,) * 3,
+        scratch_shapes=scratch,
         name="near",
-    )(near, mine, q_own, fwd, adj, on_chip(q_far), on_chip(v_far))
+    )(near, mine, q_own, *taps_of, on_chip(q_far), on_chip(v_far))
     got = lax.all_to_all(message, ("row", "col"), 0, 0, tiled=True)
 
     wide = rows + REACH
     out = pl.pallas_call(
         tv_kernel,
         out_shape=jax.ShapeDtypeStruct((frames * rows, cols), f32),
-        in_specs=[vmem] * 2,
+        in_specs=[vmem] * 3,
         out_specs=vmem,
         scratch_shapes=[
             pltpu.VMEM((wide + 1, deep + 8, cols), f32),
@@ -302,7 +340,7 @@
             pltpu.VMEM((4, deep, cols), f32),
         ],
         name="tv",
-    )(*map(on_chip, (v, got)))
+    )(*map(on_chip, (v, edge, got)))
     return out.reshape(frames, rows, cols)
 
 

time: 30.5 us -> 30.1 us (0.987)
  no operation moved by 1% of the time
where the time goes in v6:
time: 30.1 us; the launch traced here: 29.9 us
  starting transfers between devices  13.1 us (44%)
  blocking collectives  11.2 us (37%)
  Pallas kernels  4.03 us (13%)
  local copies, waits for them, and re-layouts  1.08 us (4%)
  waiting for transfers between devices  0.37 us (1%)
    all_to_all x1, blocking collectives, body(): got = lax.all_to_all(message, ('row', 'col'), 0, 0, tiled=True)  11.2 us
    ppermute x1, starting transfers between devices, body(): lax.ppermute(far, 'tm', [(i, i + 1 if i % 2 else i - 1) for i in range(1,...  11.2 us
    ppermute x1, starting transfers between devices, body(): near = lax.ppermute(near, 'tm', [(i, i ^ 1) for i in range(count)])  1.92 us
    pallas_call x1, Pallas kernels, body(): pl.pallas_call(tv_kernel, out_shape=jax.ShapeDtypeStruct((frames * rows,...  1.89 us
    reshape x1, local copies, waits for them, and re-layouts, body(): lax.dynamic_slice_in_dim(observed, odd * (frames - halo), halo, axis=0)  1.07 us
    pallas_call x1, Pallas kernels, body(): pl.pallas_call(near_kernel, out_shape=tuple(map(on_chip_result, (flat(dee...  0.98 us
    pallas_call x1, Pallas kernels, body(): pl.pallas_call(far_kernel, out_shape=(on_chip_result(flat(HALF)),) * 2, i...  0.75 us
  transfers between devices with their start and end apart: 2, of which 1 were waited for; matrix products, arithmetic and copies ran while one was open for 0% of the time, Pallas kernels for 4%

profile of v6, /device:TPU:56, one launch (start us, length us, event | category | flops | bytes accessed | tf_op | source)
XLA Modules:
  0.0 29.9 jit_solution(2756281485464049204)
XLA Ops:
  0.0 0.0 copy-start
  0.0 0.0 copy-start.1
  0.0 1.1 %dynamic-slice_bitcast_fusion = (f32[272,128]{1,0:T(8,128)S(1)}, f32[272,128]{1,0:T(8,128)S(1)}) fusion(f32[64,8,128]{2,1,0:T(8,128)} %param.2, s32[]{:T(128)S(6)} %select_n.15, s32[]{:T(128)S(6)} %select_n.14), kind=kLoop, calls=%fused_computation | loop fusion | bytes 557064 | tf_op jit(solution)/shard_map/reshape | solution.py:290
  1.1 11.2 %collective-permute-start.1 = (f32[272,128]{1,0:T(8,128)S(1)}, f32[272,128]{1,0:T(8,128)S(1)}, u32[]{:S(2)}, u32[]{:S(2)}) collective-permute-start(f32[272,128]{1,0:T(8,128)S(1)} %get-tuple-element.25), channel_id=1, source_target_pairs={{4,8},{8,4},{12,16},{16,12},{20,24},{24,20},{28,32},{32,28},{36,40... | collective-permute-start | bytes 417800 | tf_op jit(solution)/shard_map/ppermute | solution.py:291
  12.3 1.9 %collective-permute-start = (f32[272,128]{1,0:T(8,128)S(1)}, f32[272,128]{1,0:T(8,128)S(1)}, u32[]{:S(2)}, u32[]{:S(2)}) collective-permute-start(f32[272,128]{1,0:T(8,128)S(1)} %get-tuple-element.26), channel_id=1, source_target_pairs={{0,4},{4,0},{8,12},{12,8},{16,20},{20,16},{24,28},{28,24},{32,36},... | collective-permute-start | bytes 417800 | tf_op jit(solution)/shard_map/ppermute | solution.py:292
  14.2 0.0 copy-done
  14.2 0.0 copy-done.1
  14.2 0.4 %own.1 = (f32[264,128]{1,0:T(8,128)S(1)}, f32[264,128]{1,0:T(8,128)S(1)}, f32[136,128]{1,0:T(8,128)S(1)}, f32[136,128]{1,0:T(8,128)S(1)}, f32[240,128]{1,0:T(8,128)S(1)}) custom-call(f32[512,128]{1,0:T(8,128)S(1)} %bitcast.7, f32[264,128]{1,0:T(8,128)S(1)} %bitcast.10), custom_call_target="tpu_custom_call" | custom-call | tf_op jit(solution)/shard_map/own/pallas_call | solution.py:300
  14.6 0.4 %collective-permute-done.1.part_ref = f32[272,128]{1,0:T(8,128)S(1)} collective-permute-done((f32[272,128]{1,0:T(8,128)S(1)}, f32[272,128]{1,0:T(8,128)S(1)}, u32[]{:S(2)}, u32[]{:S(2)}) %collective-permute-start.1) | collective-permute-done | bytes 139296 | tf_op jit(solution)/shard_map/ppermute | solution.py:291
  15.0 0.8 %far.1 = (f32[288,128]{1,0:T(8,128)S(1)}, f32[288,128]{1,0:T(8,128)S(1)}) custom-call(f32[272,128]{1,0:T(8,128)S(1)} %collective-permute-done.1.part_ref, f32[512,128]{1,0:T(8,128)S(1)} %bitcast.8, f32[240,128]{1,0:T(8,128)S(1)} %get-tuple-element.15.q_own, f32[264,128]{1,0:T(8,128)S(1)} %get-tuple-element.16.fwd, f32[264,128]{1,0:T(8,128)S(1)} %get-tuple-element.17.adj, ...), custom_call_target="tpu_custom_call" | custom-call | tf_op jit(solution)/shard_map/far/pallas_call | solution.py:309
  15.7 0.0 collective-permute-done.part_ref
  15.7 1.0 %near.1 = (f32[576,128]{1,0:T(8,128)S(1)}, f32[72,128]{1,0:T(8,128)S(1)}, f32[4,136,128]{2,1,0:T(8,128)S(1)}) custom-call(f32[272,128]{1,0:T(8,128)S(1)} %collective-permute-done.part_ref, f32[512,128]{1,0:T(8,128)S(1)} %bitcast.9, f32[240,128]{1,0:T(8,128)S(1)} %get-tuple-element.15.q_own, f32[264,128]{1,0:T(8,128)S(1)} %get-tuple-element.16.fwd, ...), custom_call_target="tpu_custom_call" | custom-call | tf_op jit(solution)/shard_map/near/pallas_call | solution.py:317
  16.7 11.2 %all_to_all.5.got_ref = f32[4,136,128]{2,1,0:T(8,128)S(1)} all-to-all(f32[4,136,128]{2,1,0:T(8,128)S(1)} %get-tuple-element.24), channel_id=1, replica_groups=mesh['tm'=128,'row'=2,'col'=2] {'row','col'}, dimensions={0} | all-to-all | bytes 557056 | tf_op jit(solution)/shard_map/all_to_all | solution.py:325
  28.0 1.9 %tv.1 = f32[512,128]{1,0:T(8,128)} custom-call(f32[576,128]{1,0:T(8,128)S(1)} %get-tuple-element.22.v_ref, f32[72,128]{1,0:T(8,128)S(1)} %get-tuple-element.23.edge_ref, f32[4,136,128]{2,1,0:T(8,128)S(1)} %all_to_all.5.got_ref), custom_call_target="tpu_custom_call" | custom-call | tf_op jit(solution)/shard_map/tv/pallas_call | solution.py:328
Async XLA Ops:
  0.0 14.2 %copy-start = (f32[64,8,128]{2,1,0:T(8,128)S(1)}, f32[64,8,128]{2,1,0:T(8,128)}, u32[]{:S(2)}) copy-start(f32[64,8,128]{2,1,0:T(8,128)} %param.2) | copy-start | bytes 786436
  0.0 14.2 %copy-start.1 = (f32[33,8,128]{2,1,0:T(8,128)S(1)}, f32[33,8,128]{2,1,0:T(8,128)}, u32[]{:S(2)}) copy-start(f32[33,8,128]{2,1,0:T(8,128)} %param.3) | copy-start | bytes 405508
  1.1 13.9 %collective-permute-start.1 = (f32[272,128]{1,0:T(8,128)S(1)}, f32[272,128]{1,0:T(8,128)S(1)}, u32[]{:S(2)}, u32[]{:S(2)}) collective-permute-start(f32[272,128]{1,0:T(8,128)S(1)} %get-tuple-element.25), channel_id=1, source_target_pairs={{4,8},{8,4},{12,16},{16,12},{20,24},{24,20},{28,32},{32,28},{36,40... | collective-permute-start | bytes 417800 | tf_op jit(solution)/shard_map/ppermute | solution.py:291
  12.3 3.5 %collective-permute-start = (f32[272,128]{1,0:T(8,128)S(1)}, f32[272,128]{1,0:T(8,128)S(1)}, u32[]{:S(2)}, u32[]{:S(2)}) collective-permute-start(f32[272,128]{1,0:T(8,128)S(1)} %get-tuple-element.26), channel_id=1, source_target_pairs={{0,4},{4,0},{8,12},{12,8},{16,20},{20,16},{24,28},{28,24},{32,36},... | collective-permute-start | bytes 417800 | tf_op jit(solution)/shard_map/ppermute | solution.py:292

commit v7 on v6

--- a/solution.py
+++ b/solution.py
@@ -12,11 +12,34 @@
 REACH = 2
 ROWS = 8
 HALF = 36
+COPIES = 4
 BLOCK, PAIRS = 10, 6
 
 
 def at(frame, count=1):
     return pl.ds(pl.multiple_of(frame * ROWS, ROWS), count * ROWS)
+
+
+def far_slice_kernel(u_ref, far_ref, sems):
+    size = far_ref.shape[0]
+    begin = lax.rem(lax.axis_index("tm"), 2) * (u_ref.shape[0] - size)
+    pieces = [(size // ROWS) * i // COPIES * ROWS for i in range(COPIES + 1)]
+    copies = [
+        pltpu.make_async_copy(
+            u_ref.at[pl.ds(pl.multiple_of(begin + low, ROWS), high - low)], far_ref.at[low:high], sems.at[i]
+        )
+        for i, (low, high) in enumerate(zip(pieces, pieces[1:]))
+    ]
+    for copy in copies:
+        copy.start()
+    for copy in copies:
+        copy.wait()
+
+
+def near_slice_kernel(u_ref, near_ref):
+    size = near_ref.shape[0]
+    begin = (1 - lax.rem(lax.axis_index("tm"), 2)) * (u_ref.shape[0] - size)
+    near_ref[...] = u_ref[pl.ds(pl.multiple_of(begin, ROWS), size)]
 
 
 def blur(weights, field, begin, block):
@@ -282,16 +305,28 @@
     halo = 2 * half + REACH
     deep = -(-(frames + 2 * REACH) // 8) * 8
     count = lax.axis_size("tm")
-    odd = lax.axis_index("tm") % 2
     vmem = pl.BlockSpec(memory_space=pltpu.VMEM)
     f32 = jnp.float32
 
-    near = lax.dynamic_slice_in_dim(observed, (1 - odd) * (frames - halo), halo, axis=0).reshape(halo * rows, cols)
-    far = lax.dynamic_slice_in_dim(observed, odd * (frames - halo), halo, axis=0).reshape(halo * rows, cols)
+    mine = on_chip(observed.reshape(frames * rows, cols))
+    far = pl.pallas_call(
+        far_slice_kernel,
+        out_shape=on_chip_result((halo * rows, cols)),
+        in_specs=[pl.BlockSpec(memory_space=pl.ANY)],
+        out_specs=vmem,
+        scratch_shapes=[pltpu.SemaphoreType.DMA((COPIES,))],
+        name="far_slice",
+    )(observed.reshape(frames * rows, cols))
+    near = pl.pallas_call(
+        near_slice_kernel,
+        out_shape=on_chip_result((halo * rows, cols)),
+        in_specs=[vmem],
+        out_specs=vmem,
+        name="near_slice",
+    )(mine)
     far = lax.ppermute(far, "tm", [(i, i + 1 if i % 2 else i - 1) for i in range(1, count - 1)])
     near = lax.ppermute(near, "tm", [(i, i ^ 1) for i in range(count)])
     near, far = on_chip(near), on_chip(far)
-    mine = on_chip(observed.reshape(frames * rows, cols))
 
     def flat(count):
         return (count * rows, cols)

time: 30.1 us -> 30.1 us (level)
  local copies, waits for them, and re-layouts: 1.08 us -> 0.01 us
  Pallas kernels: 4.03 us -> 4.95 us
    reshape x1 -> x0, local copies, waits for them, and re-layouts: 1.07 us -> none  [body(): lax.dynamic_slice_in_dim(observed, odd * (frames - halo), halo, axis=0)]
    pallas_call x0 -> x2, Pallas kernels: none -> 0.92 us  [the longest x1 0.89 us: body(): pl.pallas_call(far_slice_kernel, out_shape=on_chip_result((halo * rows, c...]
where the time goes in v7:
time: 30.1 us; the launch traced here: 29.9 us
  starting transfers between devices  13.2 us (44%)
  blocking collectives  11.3 us (38%)
  Pallas kernels  4.95 us (16%)
  waiting for transfers between devices  0.33 us (1%)
    ppermute x1, starting transfers between devices, body(): lax.ppermute(far, 'tm', [(i, i + 1 if i % 2 else i - 1) for i in range(1,...  11.3 us
    all_to_all x1, blocking collectives, body(): got = lax.all_to_all(message, ('row', 'col'), 0, 0, tiled=True)  11.3 us
    ppermute x1, starting transfers between devices, body(): near = lax.ppermute(near, 'tm', [(i, i ^ 1) for i in range(count)])  1.92 us
    pallas_call x1, Pallas kernels, body(): pl.pallas_call(tv_kernel, out_shape=jax.ShapeDtypeStruct((frames * rows,...  1.89 us
    pallas_call x1, Pallas kernels, body(): pl.pallas_call(near_kernel, out_shape=tuple(map(on_chip_result, (flat(dee...  0.98 us
    pallas_call x1, Pallas kernels, body(): pl.pallas_call(far_slice_kernel, out_shape=on_chip_result((halo * rows, c...  0.89 us
    pallas_call x1, Pallas kernels, body(): pl.pallas_call(far_kernel, out_shape=(on_chip_result(flat(HALF)),) * 2, i...  0.75 us
  transfers between devices with their start and end apart: 2, of which 1 were waited for; matrix products, arithmetic and copies ran while one was open for 0% of the time, Pallas kernels for 4%

profile of v7, /device:TPU:56, one launch (start us, length us, event | category | flops | bytes accessed | tf_op | source)
XLA Modules:
  0.0 29.9 jit_solution(17749458347063834137)
XLA Ops:
  0.0 0.0 copy-start
  0.0 0.9 %far_slice.1 = f32[272,128]{1,0:T(8,128)S(1)} custom-call(f32[512,128]{1,0:T(8,128)} %bitcast.3), custom_call_target="tpu_custom_call" | custom-call | tf_op jit(solution)/shard_map/far_slice/pallas_call | solution.py:312
  0.9 0.0 copy-start.1
  0.9 11.3 %collective-permute-start.1 = (f32[272,128]{1,0:T(8,128)S(1)}, f32[272,128]{1,0:T(8,128)S(1)}, u32[]{:S(2)}, u32[]{:S(2)}) collective-permute-start(f32[272,128]{1,0:T(8,128)S(1)} %far_slice.1), channel_id=1, source_target_pairs={{4,8},{8,4},{12,16},{16,12},{20,24},{24,20},{28,32},{32,28},{36,40... | collective-permute-start | bytes 417800 | tf_op jit(solution)/shard_map/ppermute | solution.py:327
  12.2 0.0 copy-done
  12.3 1.9 %collective-permute-start = (f32[272,128]{1,0:T(8,128)S(1)}, f32[272,128]{1,0:T(8,128)S(1)}, u32[]{:S(2)}, u32[]{:S(2)}) collective-permute-start(f32[272,128]{1,0:T(8,128)S(1)} %near_slice.1), channel_id=1, source_target_pairs={{0,4},{4,0},{8,12},{12,8},{16,20},{20,16},{24,28},{28,24},{32,36},... | collective-permute-start | bytes 417800 | tf_op jit(solution)/shard_map/ppermute | solution.py:328
  14.2 0.0 copy-done.1
  14.2 0.4 %own.1 = (f32[264,128]{1,0:T(8,128)S(1)}, f32[264,128]{1,0:T(8,128)S(1)}, f32[136,128]{1,0:T(8,128)S(1)}, f32[136,128]{1,0:T(8,128)S(1)}, f32[240,128]{1,0:T(8,128)S(1)}) custom-call(f32[512,128]{1,0:T(8,128)S(1)} %bitcast.5, f32[264,128]{1,0:T(8,128)S(1)} %bitcast.8), custom_call_target="tpu_custom_call" | custom-call | tf_op jit(solution)/shard_map/own/pallas_call | solution.py:335
  14.6 0.3 %collective-permute-done.1.part_ref = f32[272,128]{1,0:T(8,128)S(1)} collective-permute-done((f32[272,128]{1,0:T(8,128)S(1)}, f32[272,128]{1,0:T(8,128)S(1)}, u32[]{:S(2)}, u32[]{:S(2)}) %collective-permute-start.1) | collective-permute-done | bytes 139296 | tf_op jit(solution)/shard_map/ppermute | solution.py:327
  15.0 0.8 %far.1 = (f32[288,128]{1,0:T(8,128)S(1)}, f32[288,128]{1,0:T(8,128)S(1)}) custom-call(f32[272,128]{1,0:T(8,128)S(1)} %collective-permute-done.1.part_ref, f32[512,128]{1,0:T(8,128)S(1)} %bitcast.6, f32[240,128]{1,0:T(8,128)S(1)} %get-tuple-element.15.q_own, f32[264,128]{1,0:T(8,128)S(1)} %get-tuple-element.16.fwd, f32[264,128]{1,0:T(8,128)S(1)} %get-tuple-element.17.adj, ...), custom_call_target="tpu_custom_call" | custom-call | tf_op jit(solution)/shard_map/far/pallas_call | solution.py:344
  15.7 0.0 collective-permute-done.part_ref
  15.7 1.0 %near.1 = (f32[576,128]{1,0:T(8,128)S(1)}, f32[72,128]{1,0:T(8,128)S(1)}, f32[4,136,128]{2,1,0:T(8,128)S(1)}) custom-call(f32[272,128]{1,0:T(8,128)S(1)} %collective-permute-done.part_ref, f32[512,128]{1,0:T(8,128)S(1)} %bitcast.7, f32[240,128]{1,0:T(8,128)S(1)} %get-tuple-element.15.q_own, f32[264,128]{1,0:T(8,128)S(1)} %get-tuple-element.16.fwd, ...), custom_call_target="tpu_custom_call" | custom-call | tf_op jit(solution)/shard_map/near/pallas_call | solution.py:352
  16.7 11.3 %all_to_all.5.got_ref = f32[4,136,128]{2,1,0:T(8,128)S(1)} all-to-all(f32[4,136,128]{2,1,0:T(8,128)S(1)} %get-tuple-element.24), channel_id=1, replica_groups=mesh['tm'=128,'row'=2,'col'=2] {'row','col'}, dimensions={0} | all-to-all | bytes 557056 | tf_op jit(solution)/shard_map/all_to_all | solution.py:360
  28.0 1.9 %tv.1 = f32[512,128]{1,0:T(8,128)} custom-call(f32[576,128]{1,0:T(8,128)S(1)} %get-tuple-element.22.v_ref, f32[72,128]{1,0:T(8,128)S(1)} %get-tuple-element.23.edge_ref, f32[4,136,128]{2,1,0:T(8,128)S(1)} %all_to_all.5.got_ref), custom_call_target="tpu_custom_call" | custom-call | tf_op jit(solution)/shard_map/tv/pallas_call | solution.py:363
  (1 shorter events, 0.0 us)
Async XLA Ops:
  0.0 12.2 %copy-start = (f32[64,8,128]{2,1,0:T(8,128)S(1)}, f32[64,8,128]{2,1,0:T(8,128)}, u32[]{:S(2)}) copy-start(f32[64,8,128]{2,1,0:T(8,128)} %param.2) | copy-start | bytes 786436
  0.9 13.3 %copy-start.1 = (f32[33,8,128]{2,1,0:T(8,128)S(1)}, f32[33,8,128]{2,1,0:T(8,128)}, u32[]{:S(2)}) copy-start(f32[33,8,128]{2,1,0:T(8,128)} %param.3) | copy-start | bytes 405508
  0.9 14.0 %collective-permute-start.1 = (f32[272,128]{1,0:T(8,128)S(1)}, f32[272,128]{1,0:T(8,128)S(1)}, u32[]{:S(2)}, u32[]{:S(2)}) collective-permute-start(f32[272,128]{1,0:T(8,128)S(1)} %far_slice.1), channel_id=1, source_target_pairs={{4,8},{8,4},{12,16},{16,12},{20,24},{24,20},{28,32},{32,28},{36,40... | collective-permute-start | bytes 417800 | tf_op jit(solution)/shard_map/ppermute | solution.py:327
  12.3 3.4 %collective-permute-start = (f32[272,128]{1,0:T(8,128)S(1)}, f32[272,128]{1,0:T(8,128)S(1)}, u32[]{:S(2)}, u32[]{:S(2)}) collective-permute-start(f32[272,128]{1,0:T(8,128)S(1)} %near_slice.1), channel_id=1, source_target_pairs={{0,4},{4,0},{8,12},{12,8},{16,20},{20,16},{24,28},{28,24},{32,36},... | collective-permute-start | bytes 417800 | tf_op jit(solution)/shard_map/ppermute | solution.py:328

commit v8 on v6

--- a/solution.py
+++ b/solution.py
@@ -61,7 +61,7 @@
             finish(2 * (base + i) + 1, last[i] + shared[i])
         return carry
 
-    lax.fori_loop(0, pairs // PAIRS, step, 0)
+    lax.fori_loop(0, pairs // PAIRS, step, 0, unroll=True)
 
 
 def own_kernel(u_ref, kernel_ref, fwd, adj, fwd_sums, adj_sums, q_ref):
@@ -85,7 +85,7 @@
             q_ref[at(step * BLOCK + i)] = value
         return carry
 
-    lax.fori_loop(0, q_ref.shape[0] // ROWS // BLOCK, forward, 0)
+    lax.fori_loop(0, q_ref.shape[0] // ROWS // BLOCK, forward, 0, unroll=True)
 
 
 def half_blur(side, part_ref, u_ref, q_own, taps_of, u, q, less, more, v, v_begin):

time: 30.1 us -> 29.6 us (0.983)
  Pallas kernels: 4.03 us -> 3.62 us
  transfers between devices with their start and end apart: 2 -> 2, of which waited for: 1 -> 1; matrix products, arithmetic and copies ran while one was open for 0% -> 0% of each run, Pallas kernels for 4% -> 3%
where the time goes in v8:
time: 29.6 us; the launch traced here: 29.5 us
  starting transfers between devices  13.1 us (44%)
  blocking collectives  11.2 us (38%)
  Pallas kernels  3.62 us (12%)
  local copies, waits for them, and re-layouts  1.08 us (4%)
  waiting for transfers between devices  0.44 us (1%)
    all_to_all x1, blocking collectives, body(): got = lax.all_to_all(message, ('row', 'col'), 0, 0, tiled=True)  11.2 us
    ppermute x1, starting transfers between devices, body(): lax.ppermute(far, 'tm', [(i, i + 1 if i % 2 else i - 1) for i in range(1,...  11.2 us
    ppermute x1, starting transfers between devices, body(): near = lax.ppermute(near, 'tm', [(i, i ^ 1) for i in range(count)])  1.92 us
    pallas_call x1, Pallas kernels, body(): pl.pallas_call(tv_kernel, out_shape=jax.ShapeDtypeStruct((frames * rows,...  1.89 us
    reshape x1, local copies, waits for them, and re-layouts, body(): lax.dynamic_slice_in_dim(observed, odd * (frames - halo), halo, axis=0)  1.07 us
    pallas_call x1, Pallas kernels, body(): pl.pallas_call(near_kernel, out_shape=tuple(map(on_chip_result, (flat(dee...  0.81 us
  transfers between devices with their start and end apart: 2, of which 1 were waited for; matrix products, arithmetic and copies ran while one was open for 0% of the time, Pallas kernels for 3%

profile of v8, /device:TPU:56, one launch (start us, length us, event | category | flops | bytes accessed | tf_op | source)
XLA Modules:
  0.0 29.5 jit_solution(14416323467888760837)
XLA Ops:
  0.0 0.0 copy-start
  0.0 0.0 copy-start.1
  0.0 1.1 %dynamic-slice_bitcast_fusion = (f32[272,128]{1,0:T(8,128)S(1)}, f32[272,128]{1,0:T(8,128)S(1)}) fusion(f32[64,8,128]{2,1,0:T(8,128)} %param.2, s32[]{:T(128)S(6)} %select_n.15, s32[]{:T(128)S(6)} %select_n.14), kind=kLoop, calls=%fused_computation | loop fusion | bytes 557064 | tf_op jit(solution)/shard_map/reshape | solution.py:290
  1.1 11.2 %collective-permute-start.1 = (f32[272,128]{1,0:T(8,128)S(1)}, f32[272,128]{1,0:T(8,128)S(1)}, u32[]{:S(2)}, u32[]{:S(2)}) collective-permute-start(f32[272,128]{1,0:T(8,128)S(1)} %get-tuple-element.25), channel_id=1, source_target_pairs={{4,8},{8,4},{12,16},{16,12},{20,24},{24,20},{28,32},{32,28},{36,40... | collective-permute-start | bytes 417800 | tf_op jit(solution)/shard_map/ppermute | solution.py:291
  12.3 1.9 %collective-permute-start = (f32[272,128]{1,0:T(8,128)S(1)}, f32[272,128]{1,0:T(8,128)S(1)}, u32[]{:S(2)}, u32[]{:S(2)}) collective-permute-start(f32[272,128]{1,0:T(8,128)S(1)} %get-tuple-element.26), channel_id=1, source_target_pairs={{0,4},{4,0},{8,12},{12,8},{16,20},{20,16},{24,28},{28,24},{32,36},... | collective-permute-start | bytes 417800 | tf_op jit(solution)/shard_map/ppermute | solution.py:292
  14.2 0.0 copy-done
  14.2 0.0 copy-done.1
  14.2 0.3 %own.1 = (f32[264,128]{1,0:T(8,128)S(1)}, f32[264,128]{1,0:T(8,128)S(1)}, f32[136,128]{1,0:T(8,128)S(1)}, f32[136,128]{1,0:T(8,128)S(1)}, f32[240,128]{1,0:T(8,128)S(1)}) custom-call(f32[512,128]{1,0:T(8,128)S(1)} %bitcast.7, f32[264,128]{1,0:T(8,128)S(1)} %bitcast.10), custom_call_target="tpu_custom_call" | custom-call | tf_op jit(solution)/shard_map/own/pallas_call | solution.py:300
  14.5 0.4 %collective-permute-done.1.part_ref = f32[272,128]{1,0:T(8,128)S(1)} collective-permute-done((f32[272,128]{1,0:T(8,128)S(1)}, f32[272,128]{1,0:T(8,128)S(1)}, u32[]{:S(2)}, u32[]{:S(2)}) %collective-permute-start.1) | collective-permute-done | bytes 139296 | tf_op jit(solution)/shard_map/ppermute | solution.py:291
  15.0 0.6 %far.1 = (f32[288,128]{1,0:T(8,128)S(1)}, f32[288,128]{1,0:T(8,128)S(1)}) custom-call(f32[272,128]{1,0:T(8,128)S(1)} %collective-permute-done.1.part_ref, f32[512,128]{1,0:T(8,128)S(1)} %bitcast.8, f32[240,128]{1,0:T(8,128)S(1)} %get-tuple-element.15.q_own, f32[264,128]{1,0:T(8,128)S(1)} %get-tuple-element.16.fwd, f32[264,128]{1,0:T(8,128)S(1)} %get-tuple-element.17.adj, ...), custom_call_target="tpu_custom_call" | custom-call | tf_op jit(solution)/shard_map/far/pallas_call | solution.py:309
  15.6 0.0 collective-permute-done.part_ref
  15.6 0.8 %near.1 = (f32[576,128]{1,0:T(8,128)S(1)}, f32[72,128]{1,0:T(8,128)S(1)}, f32[4,136,128]{2,1,0:T(8,128)S(1)}) custom-call(f32[272,128]{1,0:T(8,128)S(1)} %collective-permute-done.part_ref, f32[512,128]{1,0:T(8,128)S(1)} %bitcast.9, f32[240,128]{1,0:T(8,128)S(1)} %get-tuple-element.15.q_own, f32[264,128]{1,0:T(8,128)S(1)} %get-tuple-element.16.fwd, ...), custom_call_target="tpu_custom_call" | custom-call | tf_op jit(solution)/shard_map/near/pallas_call | solution.py:317
  16.4 11.2 %all_to_all.5.got_ref = f32[4,136,128]{2,1,0:T(8,128)S(1)} all-to-all(f32[4,136,128]{2,1,0:T(8,128)S(1)} %get-tuple-element.24), channel_id=1, replica_groups=mesh['tm'=128,'row'=2,'col'=2] {'row','col'}, dimensions={0} | all-to-all | bytes 557056 | tf_op jit(solution)/shard_map/all_to_all | solution.py:325
  27.6 1.9 %tv.1 = f32[512,128]{1,0:T(8,128)} custom-call(f32[576,128]{1,0:T(8,128)S(1)} %get-tuple-element.22.v_ref, f32[72,128]{1,0:T(8,128)S(1)} %get-tuple-element.23.edge_ref, f32[4,136,128]{2,1,0:T(8,128)S(1)} %all_to_all.5.got_ref), custom_call_target="tpu_custom_call" | custom-call | tf_op jit(solution)/shard_map/tv/pallas_call | solution.py:328
Async XLA Ops:
  0.0 14.2 %copy-start = (f32[64,8,128]{2,1,0:T(8,128)S(1)}, f32[64,8,128]{2,1,0:T(8,128)}, u32[]{:S(2)}) copy-start(f32[64,8,128]{2,1,0:T(8,128)} %param.2) | copy-start | bytes 786436
  0.0 14.2 %copy-start.1 = (f32[33,8,128]{2,1,0:T(8,128)S(1)}, f32[33,8,128]{2,1,0:T(8,128)}, u32[]{:S(2)}) copy-start(f32[33,8,128]{2,1,0:T(8,128)} %param.3) | copy-start | bytes 405508
  1.1 13.9 %collective-permute-start.1 = (f32[272,128]{1,0:T(8,128)S(1)}, f32[272,128]{1,0:T(8,128)S(1)}, u32[]{:S(2)}, u32[]{:S(2)}) collective-permute-start(f32[272,128]{1,0:T(8,128)S(1)} %get-tuple-element.25), channel_id=1, source_target_pairs={{4,8},{8,4},{12,16},{16,12},{20,24},{24,20},{28,32},{32,28},{36,40... | collective-permute-start | bytes 417800 | tf_op jit(solution)/shard_map/ppermute | solution.py:291
  12.3 3.3 %collective-permute-start = (f32[272,128]{1,0:T(8,128)S(1)}, f32[272,128]{1,0:T(8,128)S(1)}, u32[]{:S(2)}, u32[]{:S(2)}) collective-permute-start(f32[272,128]{1,0:T(8,128)S(1)} %get-tuple-element.26), channel_id=1, source_target_pairs={{0,4},{4,0},{8,12},{12,8},{16,20},{20,16},{24,28},{28,24},{32,36},... | collective-permute-start | bytes 417800 | tf_op jit(solution)/shard_map/ppermute | solution.py:292

commit v9 on v7

--- a/solution.py
+++ b/solution.py
@@ -84,7 +84,7 @@
             finish(2 * (base + i) + 1, last[i] + shared[i])
         return carry
 
-    lax.fori_loop(0, pairs // PAIRS, step, 0)
+    lax.fori_loop(0, pairs // PAIRS, step, 0, unroll=True)
 
 
 def own_kernel(u_ref, kernel_ref, fwd, adj, fwd_sums, adj_sums, q_ref):
@@ -108,7 +108,7 @@
             q_ref[at(step * BLOCK + i)] = value
         return carry
 
-    lax.fori_loop(0, q_ref.shape[0] // ROWS // BLOCK, forward, 0)
+    lax.fori_loop(0, q_ref.shape[0] // ROWS // BLOCK, forward, 0, unroll=True)
 
 
 def half_blur(side, part_ref, u_ref, q_own, taps_of, u, q, less, more, v, v_begin):

time: 30.1 us -> 29.7 us (0.987)
  Pallas kernels: 4.95 us -> 4.54 us
  transfers between devices with their start and end apart: 2 -> 2, of which waited for: 1 -> 1; matrix products, arithmetic and copies ran while one was open for 0% -> 0% of each run, Pallas kernels for 4% -> 3%
where the time goes in v9:
time: 29.7 us; the launch traced here: 29.5 us
  starting transfers between devices  13.2 us (44%)
  blocking collectives  11.2 us (38%)
  Pallas kernels  4.54 us (15%)
  waiting for transfers between devices  0.4 us (1%)
    ppermute x1, starting transfers between devices, body(): lax.ppermute(far, 'tm', [(i, i + 1 if i % 2 else i - 1) for i in range(1,...  11.3 us
    all_to_all x1, blocking collectives, body(): got = lax.all_to_all(message, ('row', 'col'), 0, 0, tiled=True)  11.2 us
    ppermute x1, starting transfers between devices, body(): near = lax.ppermute(near, 'tm', [(i, i ^ 1) for i in range(count)])  1.92 us
    pallas_call x1, Pallas kernels, body(): pl.pallas_call(tv_kernel, out_shape=jax.ShapeDtypeStruct((frames * rows,...  1.89 us
    pallas_call x1, Pallas kernels, body(): pl.pallas_call(far_slice_kernel, out_shape=on_chip_result((halo * rows, c...  0.89 us
    pallas_call x1, Pallas kernels, body(): pl.pallas_call(near_kernel, out_shape=tuple(map(on_chip_result, (flat(dee...  0.81 us
  transfers between devices with their start and end apart: 2, of which 1 were waited for; matrix products, arithmetic and copies ran while one was open for 0% of the time, Pallas kernels for 3%

profile of v9, /device:TPU:56, one launch (start us, length us, event | category | flops | bytes accessed | tf_op | source)
XLA Modules:
  0.0 29.5 jit_solution(3378322652652544107)
XLA Ops:
  0.0 0.0 copy-start
  0.0 0.9 %far_slice.1 = f32[272,128]{1,0:T(8,128)S(1)} custom-call(f32[512,128]{1,0:T(8,128)} %bitcast.3), custom_call_target="tpu_custom_call" | custom-call | tf_op jit(solution)/shard_map/far_slice/pallas_call | solution.py:312
  0.9 0.0 copy-start.1
  0.9 11.3 %collective-permute-start.1 = (f32[272,128]{1,0:T(8,128)S(1)}, f32[272,128]{1,0:T(8,128)S(1)}, u32[]{:S(2)}, u32[]{:S(2)}) collective-permute-start(f32[272,128]{1,0:T(8,128)S(1)} %far_slice.1), channel_id=1, source_target_pairs={{4,8},{8,4},{12,16},{16,12},{20,24},{24,20},{28,32},{32,28},{36,40... | collective-permute-start | bytes 417800 | tf_op jit(solution)/shard_map/ppermute | solution.py:327
  12.2 0.0 copy-done
  12.3 1.9 %collective-permute-start = (f32[272,128]{1,0:T(8,128)S(1)}, f32[272,128]{1,0:T(8,128)S(1)}, u32[]{:S(2)}, u32[]{:S(2)}) collective-permute-start(f32[272,128]{1,0:T(8,128)S(1)} %near_slice.1), channel_id=1, source_target_pairs={{0,4},{4,0},{8,12},{12,8},{16,20},{20,16},{24,28},{28,24},{32,36},... | collective-permute-start | bytes 417800 | tf_op jit(solution)/shard_map/ppermute | solution.py:328
  14.2 0.0 copy-done.1
  14.2 0.3 %own.1 = (f32[264,128]{1,0:T(8,128)S(1)}, f32[264,128]{1,0:T(8,128)S(1)}, f32[136,128]{1,0:T(8,128)S(1)}, f32[136,128]{1,0:T(8,128)S(1)}, f32[240,128]{1,0:T(8,128)S(1)}) custom-call(f32[512,128]{1,0:T(8,128)S(1)} %bitcast.5, f32[264,128]{1,0:T(8,128)S(1)} %bitcast.8), custom_call_target="tpu_custom_call" | custom-call | tf_op jit(solution)/shard_map/own/pallas_call | solution.py:335
  14.6 0.4 %collective-permute-done.1.part_ref = f32[272,128]{1,0:T(8,128)S(1)} collective-permute-done((f32[272,128]{1,0:T(8,128)S(1)}, f32[272,128]{1,0:T(8,128)S(1)}, u32[]{:S(2)}, u32[]{:S(2)}) %collective-permute-start.1) | collective-permute-done | bytes 139296 | tf_op jit(solution)/shard_map/ppermute | solution.py:327
  15.0 0.6 %far.1 = (f32[288,128]{1,0:T(8,128)S(1)}, f32[288,128]{1,0:T(8,128)S(1)}) custom-call(f32[272,128]{1,0:T(8,128)S(1)} %collective-permute-done.1.part_ref, f32[512,128]{1,0:T(8,128)S(1)} %bitcast.6, f32[240,128]{1,0:T(8,128)S(1)} %get-tuple-element.15.q_own, f32[264,128]{1,0:T(8,128)S(1)} %get-tuple-element.16.fwd, f32[264,128]{1,0:T(8,128)S(1)} %get-tuple-element.17.adj, ...), custom_call_target="tpu_custom_call" | custom-call | tf_op jit(solution)/shard_map/far/pallas_call | solution.py:344
  15.5 0.0 collective-permute-done.part_ref
  15.5 0.8 %near.1 = (f32[576,128]{1,0:T(8,128)S(1)}, f32[72,128]{1,0:T(8,128)S(1)}, f32[4,136,128]{2,1,0:T(8,128)S(1)}) custom-call(f32[272,128]{1,0:T(8,128)S(1)} %collective-permute-done.part_ref, f32[512,128]{1,0:T(8,128)S(1)} %bitcast.7, f32[240,128]{1,0:T(8,128)S(1)} %get-tuple-element.15.q_own, f32[264,128]{1,0:T(8,128)S(1)} %get-tuple-element.16.fwd, ...), custom_call_target="tpu_custom_call" | custom-call | tf_op jit(solution)/shard_map/near/pallas_call | solution.py:352
  16.4 11.2 %all_to_all.5.got_ref = f32[4,136,128]{2,1,0:T(8,128)S(1)} all-to-all(f32[4,136,128]{2,1,0:T(8,128)S(1)} %get-tuple-element.24), channel_id=1, replica_groups=mesh['tm'=128,'row'=2,'col'=2] {'row','col'}, dimensions={0} | all-to-all | bytes 557056 | tf_op jit(solution)/shard_map/all_to_all | solution.py:360
  27.6 1.9 %tv.1 = f32[512,128]{1,0:T(8,128)} custom-call(f32[576,128]{1,0:T(8,128)S(1)} %get-tuple-element.22.v_ref, f32[72,128]{1,0:T(8,128)S(1)} %get-tuple-element.23.edge_ref, f32[4,136,128]{2,1,0:T(8,128)S(1)} %all_to_all.5.got_ref), custom_call_target="tpu_custom_call" | custom-call | tf_op jit(solution)/shard_map/tv/pallas_call | solution.py:363
  (1 shorter events, 0.0 us)
Async XLA Ops:
  0.0 12.2 %copy-start = (f32[64,8,128]{2,1,0:T(8,128)S(1)}, f32[64,8,128]{2,1,0:T(8,128)}, u32[]{:S(2)}) copy-start(f32[64,8,128]{2,1,0:T(8,128)} %param.2) | copy-start | bytes 786436
  0.9 13.3 %copy-start.1 = (f32[33,8,128]{2,1,0:T(8,128)S(1)}, f32[33,8,128]{2,1,0:T(8,128)}, u32[]{:S(2)}) copy-start(f32[33,8,128]{2,1,0:T(8,128)} %param.3) | copy-start | bytes 405508
  0.9 14.0 %collective-permute-start.1 = (f32[272,128]{1,0:T(8,128)S(1)}, f32[272,128]{1,0:T(8,128)S(1)}, u32[]{:S(2)}, u32[]{:S(2)}) collective-permute-start(f32[272,128]{1,0:T(8,128)S(1)} %far_slice.1), channel_id=1, source_target_pairs={{4,8},{8,4},{12,16},{16,12},{20,24},{24,20},{28,32},{32,28},{36,40... | collective-permute-start | bytes 417800 | tf_op jit(solution)/shard_map/ppermute | solution.py:327
  12.3 3.3 %collective-permute-start = (f32[272,128]{1,0:T(8,128)S(1)}, f32[272,128]{1,0:T(8,128)S(1)}, u32[]{:S(2)}, u32[]{:S(2)}) collective-permute-start(f32[272,128]{1,0:T(8,128)S(1)} %near_slice.1), channel_id=1, source_target_pairs={{0,4},{4,0},{8,12},{12,8},{16,20},{20,16},{24,28},{28,24},{32,36},... | collective-permute-start | bytes 417800 | tf_op jit(solution)/shard_map/ppermute | solution.py:328

commit v10 on v9

--- a/solution.py
+++ b/solution.py
@@ -13,7 +13,7 @@
 ROWS = 8
 HALF = 36
 COPIES = 4
-BLOCK, PAIRS = 10, 6
+BLOCK, PAIRS = 10, 9
 
 
 def at(frame, count=1):

time: 29.7 us -> 29.7 us (level)
  no operation moved by 1% of the time
where the time goes in v10:
time: 29.7 us; the launch traced here: 29.5 us
  starting transfers between devices  13.2 us (44%)
  blocking collectives  11.2 us (38%)
  Pallas kernels  4.55 us (15%)
  waiting for transfers between devices  0.4 us (1%)
    ppermute x1, starting transfers between devices, body(): lax.ppermute(far, 'tm', [(i, i + 1 if i % 2 else i - 1) for i in range(1,...  11.3 us
    all_to_all x1, blocking collectives, body(): got = lax.all_to_all(message, ('row', 'col'), 0, 0, tiled=True)  11.2 us
    ppermute x1, starting transfers between devices, body(): near = lax.ppermute(near, 'tm', [(i, i ^ 1) for i in range(count)])  1.92 us
    pallas_call x1, Pallas kernels, body(): pl.pallas_call(tv_kernel, out_shape=jax.ShapeDtypeStruct((frames * rows,...  1.89 us
    pallas_call x1, Pallas kernels, body(): pl.pallas_call(far_slice_kernel, out_shape=on_chip_result((halo * rows, c...  0.89 us
    pallas_call x1, Pallas kernels, body(): pl.pallas_call(near_kernel, out_shape=tuple(map(on_chip_result, (flat(dee...  0.81 us
  transfers between devices with their start and end apart: 2, of which 1 were waited for; matrix products, arithmetic and copies ran while one was open for 0% of the time, Pallas kernels for 3%

profile of v10, /device:TPU:56, one launch (start us, length us, event | category | flops | bytes accessed | tf_op | source)
XLA Modules:
  0.0 29.5 jit_solution(17619222615616536852)
XLA Ops:
  0.0 0.0 copy-start
  0.0 0.9 %far_slice.1 = f32[272,128]{1,0:T(8,128)S(1)} custom-call(f32[512,128]{1,0:T(8,128)} %bitcast.3), custom_call_target="tpu_custom_call" | custom-call | tf_op jit(solution)/shard_map/far_slice/pallas_call | solution.py:312
  0.9 0.0 copy-start.1
  0.9 11.3 %collective-permute-start.1 = (f32[272,128]{1,0:T(8,128)S(1)}, f32[272,128]{1,0:T(8,128)S(1)}, u32[]{:S(2)}, u32[]{:S(2)}) collective-permute-start(f32[272,128]{1,0:T(8,128)S(1)} %far_slice.1), channel_id=1, source_target_pairs={{4,8},{8,4},{12,16},{16,12},{20,24},{24,20},{28,32},{32,28},{36,40... | collective-permute-start | bytes 417800 | tf_op jit(solution)/shard_map/ppermute | solution.py:327
  12.2 0.0 copy-done
  12.3 1.9 %collective-permute-start = (f32[272,128]{1,0:T(8,128)S(1)}, f32[272,128]{1,0:T(8,128)S(1)}, u32[]{:S(2)}, u32[]{:S(2)}) collective-permute-start(f32[272,128]{1,0:T(8,128)S(1)} %near_slice.1), channel_id=1, source_target_pairs={{0,4},{4,0},{8,12},{12,8},{16,20},{20,16},{24,28},{28,24},{32,36},... | collective-permute-start | bytes 417800 | tf_op jit(solution)/shard_map/ppermute | solution.py:328
  14.2 0.0 copy-done.1
  14.2 0.3 %own.1 = (f32[264,128]{1,0:T(8,128)S(1)}, f32[264,128]{1,0:T(8,128)S(1)}, f32[136,128]{1,0:T(8,128)S(1)}, f32[136,128]{1,0:T(8,128)S(1)}, f32[240,128]{1,0:T(8,128)S(1)}) custom-call(f32[512,128]{1,0:T(8,128)S(1)} %bitcast.5, f32[264,128]{1,0:T(8,128)S(1)} %bitcast.8), custom_call_target="tpu_custom_call" | custom-call | tf_op jit(solution)/shard_map/own/pallas_call | solution.py:335
  14.6 0.4 %collective-permute-done.1.part_ref = f32[272,128]{1,0:T(8,128)S(1)} collective-permute-done((f32[272,128]{1,0:T(8,128)S(1)}, f32[272,128]{1,0:T(8,128)S(1)}, u32[]{:S(2)}, u32[]{:S(2)}) %collective-permute-start.1) | collective-permute-done | bytes 139296 | tf_op jit(solution)/shard_map/ppermute | solution.py:327
  15.0 0.6 %far.1 = (f32[288,128]{1,0:T(8,128)S(1)}, f32[288,128]{1,0:T(8,128)S(1)}) custom-call(f32[272,128]{1,0:T(8,128)S(1)} %collective-permute-done.1.part_ref, f32[512,128]{1,0:T(8,128)S(1)} %bitcast.6, f32[240,128]{1,0:T(8,128)S(1)} %get-tuple-element.15.q_own, f32[264,128]{1,0:T(8,128)S(1)} %get-tuple-element.16.fwd, f32[264,128]{1,0:T(8,128)S(1)} %get-tuple-element.17.adj, ...), custom_call_target="tpu_custom_call" | custom-call | tf_op jit(solution)/shard_map/far/pallas_call | solution.py:344
  15.5 0.0 collective-permute-done.part_ref
  15.6 0.8 %near.1 = (f32[576,128]{1,0:T(8,128)S(1)}, f32[72,128]{1,0:T(8,128)S(1)}, f32[4,136,128]{2,1,0:T(8,128)S(1)}) custom-call(f32[272,128]{1,0:T(8,128)S(1)} %collective-permute-done.part_ref, f32[512,128]{1,0:T(8,128)S(1)} %bitcast.7, f32[240,128]{1,0:T(8,128)S(1)} %get-tuple-element.15.q_own, f32[264,128]{1,0:T(8,128)S(1)} %get-tuple-element.16.fwd, ...), custom_call_target="tpu_custom_call" | custom-call | tf_op jit(solution)/shard_map/near/pallas_call | solution.py:352
  16.4 11.2 %all_to_all.5.got_ref = f32[4,136,128]{2,1,0:T(8,128)S(1)} all-to-all(f32[4,136,128]{2,1,0:T(8,128)S(1)} %get-tuple-element.24), channel_id=1, replica_groups=mesh['tm'=128,'row'=2,'col'=2] {'row','col'}, dimensions={0} | all-to-all | bytes 557056 | tf_op jit(solution)/shard_map/all_to_all | solution.py:360
  27.6 1.9 %tv.1 = f32[512,128]{1,0:T(8,128)} custom-call(f32[576,128]{1,0:T(8,128)S(1)} %get-tuple-element.22.v_ref, f32[72,128]{1,0:T(8,128)S(1)} %get-tuple-element.23.edge_ref, f32[4,136,128]{2,1,0:T(8,128)S(1)} %all_to_all.5.got_ref), custom_call_target="tpu_custom_call" | custom-call | tf_op jit(solution)/shard_map/tv/pallas_call | solution.py:363
  (1 shorter events, 0.0 us)
Async XLA Ops:
  0.0 12.2 %copy-start = (f32[64,8,128]{2,1,0:T(8,128)S(1)}, f32[64,8,128]{2,1,0:T(8,128)}, u32[]{:S(2)}) copy-start(f32[64,8,128]{2,1,0:T(8,128)} %param.2) | copy-start | bytes 786436
  0.9 13.3 %copy-start.1 = (f32[33,8,128]{2,1,0:T(8,128)S(1)}, f32[33,8,128]{2,1,0:T(8,128)}, u32[]{:S(2)}) copy-start(f32[33,8,128]{2,1,0:T(8,128)} %param.3) | copy-start | bytes 405508
  0.9 14.0 %collective-permute-start.1 = (f32[272,128]{1,0:T(8,128)S(1)}, f32[272,128]{1,0:T(8,128)S(1)}, u32[]{:S(2)}, u32[]{:S(2)}) collective-permute-start(f32[272,128]{1,0:T(8,128)S(1)} %far_slice.1), channel_id=1, source_target_pairs={{4,8},{8,4},{12,16},{16,12},{20,24},{24,20},{28,32},{32,28},{36,40... | collective-permute-start | bytes 417800 | tf_op jit(solution)/shard_map/ppermute | solution.py:327
  12.3 3.3 %collective-permute-start = (f32[272,128]{1,0:T(8,128)S(1)}, f32[272,128]{1,0:T(8,128)S(1)}, u32[]{:S(2)}, u32[]{:S(2)}) collective-permute-start(f32[272,128]{1,0:T(8,128)S(1)} %near_slice.1), channel_id=1, source_target_pairs={{0,4},{4,0},{8,12},{12,8},{16,20},{20,16},{24,28},{28,24},{32,36},... | collective-permute-start | bytes 417800 | tf_op jit(solution)/shard_map/ppermute | solution.py:328
